TPU v7x, 32 devices: a whole 2x2x4 slice. The times are simulated.
32 devices in a mesh: pipe: 4 (over y, x), seq: 8 (over z, core).
Axes of the slice: x: 2, y: 2, z: 4, core: 2. Of those that a mesh axis runs over, the one named last changes fastest.
Arguments:
- acts: bfloat16 [4, 2048, 1024], P('pipe', 'seq'), may hold values from -6 to 6
- cotan: bfloat16 [4, 2048, 1024], P('pipe', 'seq'), may hold values from -6 to 6
- proj_in: bfloat16 [4, 1024, 2048], P('pipe'), may hold values from -0.1875 to 0.1875
- proj_out: bfloat16 [4, 1024, 1024], P('pipe'), may hold values from -0.1875 to 0.1875
- block_mix: bfloat16 [4, 2048, 256], P('pipe', 'seq'), may hold values from -0.375 to 0.375
- twiddle: float32 [4, 3, 2, 2, 1024], P('pipe'), may hold values from -2.5 to 2.5
Outputs:
- mixed: bfloat16 [4, 2048, 1024], P('pipe', 'seq')
- grad_prev: bfloat16 [4, 2048, 1024], P('pipe', 'seq')
- grad_in_proj: float32 [4, 1024, 2048], P('pipe', 'seq')
- grad_out_proj: float32 [4, 1024, 1024], P('pipe', 'seq')
- grad_block_mix: float32 [4, 2048, 256], P('pipe', 'seq')
- grad_twiddle: float32 [4, 3, 2, 2, 1024], P('pipe')
All inputs are finite; a program needn't handle non-finite values.
Results may differ from a plain program's by a relative error of at most 0.014.
Values may be sent and summed in bfloat16 or wider, within the bound.
No kernel may reach another device: no remote copies, remote signals or barrier semaphores. Data moves between devices by JAX's collectives and lax.ppermute only.
A program may use at most 128 MiB of HBM per device.

v0:
```python
import jax
import jax.numpy as jnp
from jax import lax
from jax.sharding import PartitionSpec as P


def from_behind(value, axis, steps):
    count = lax.axis_size(axis)
    first, last = (max(0, -steps), min(count, count - steps))
    return lax.ppermute(value, axis, [(source, source + steps) for source in range(first, last)])


def local_segment(blocked, segment_coef, segment_bit):
    block_count, inner_rows, feature_count = blocked.shape
    stride_len = 2**segment_bit
    shaped = blocked.reshape(
        block_count // (2 * stride_len), 2, stride_len, inner_rows, feature_count
    )
    lower_part = shaped[:, 0].astype(jnp.float32)
    upper_part = shaped[:, 1].astype(jnp.float32)
    new_lower = segment_coef[0, 0] * lower_part + segment_coef[0, 1] * upper_part
    new_upper = segment_coef[1, 0] * upper_part + segment_coef[1, 1] * lower_part
    joined = jnp.stack([new_lower, new_upper], axis=1)
    return joined.reshape(block_count, inner_rows, feature_count).astype(jnp.bfloat16)


def local_back(grad_blocked, stored, segment_coef, segment_bit):
    block_count, inner_rows, feature_count = grad_blocked.shape
    stride_len = 2**segment_bit
    dshape = grad_blocked.reshape(
        block_count // (2 * stride_len), 2, stride_len, inner_rows, feature_count
    )
    zshape = stored.reshape(
        block_count // (2 * stride_len), 2, stride_len, inner_rows, feature_count
    )
    grad_lower = dshape[:, 0].astype(jnp.float32)
    grad_upper = dshape[:, 1].astype(jnp.float32)
    val_lower = zshape[:, 0].astype(jnp.float32)
    val_upper = zshape[:, 1].astype(jnp.float32)
    prev_lower = segment_coef[0, 0] * grad_lower + segment_coef[1, 1] * grad_upper
    prev_upper = segment_coef[1, 0] * grad_upper + segment_coef[0, 1] * grad_lower
    joined = jnp.stack([prev_lower, prev_upper], axis=1)
    prev = joined.reshape(block_count, inner_rows, feature_count).astype(jnp.bfloat16)
    axes_sum = (0, 1, 2)
    partial_value = jnp.stack(
        [
            jnp.stack(
                [
                    jnp.sum(grad_lower * val_lower, axis=axes_sum),
                    jnp.sum(grad_lower * val_upper, axis=axes_sum),
                ]
            ),
            jnp.stack(
                [
                    jnp.sum(grad_upper * val_upper, axis=axes_sum),
                    jnp.sum(grad_upper * val_lower, axis=axes_sum),
                ]
            ),
        ]
    )
    return (prev, partial_value)


def on_device(acts, cotan, proj_in, proj_out, block_mix, twiddle):
    inputs = acts[0]
    grad_out = cotan[0]
    w_in = proj_in[0]
    w_out = proj_out[0]
    square_mix = block_mix[0]
    twiddle_w = twiddle[0]
    row_count, feature_count = inputs.shape
    seq_count = lax.axis_size("seq")
    segment_total = seq_count.bit_length() - 1
    projected = jnp.dot(inputs, w_in, preferred_element_type=jnp.float32)
    value = projected[:, :feature_count].astype(jnp.bfloat16)
    gate = projected[:, feature_count:].astype(jnp.bfloat16)
    first_segment = jnp.dot(square_mix, value, preferred_element_type=jnp.float32).astype(
        jnp.bfloat16
    )
    partials = [None] * segment_total
    columns = lax.all_to_all(first_segment, "seq", split_axis=0, concat_axis=0, tiled=True)
    blocked = columns.reshape(seq_count, row_count // seq_count, feature_count)
    stored = []
    for segment_bit in range(segment_total):
        stored.append(blocked)
        blocked = local_segment(blocked, twiddle_w[segment_bit], segment_bit)
    monarch = lax.all_to_all(
        blocked.reshape(row_count, feature_count), "seq", split_axis=0, concat_axis=0, tiled=True
    )
    hidden = (monarch.astype(jnp.float32) * gate.astype(jnp.float32)).astype(jnp.bfloat16)
    mixed_out = jnp.dot(hidden, w_out, preferred_element_type=jnp.float32).astype(jnp.bfloat16)
    d_hidden = lax.dot_general(
        grad_out, w_out, (((1,), (1,)), ((), ())), preferred_element_type=jnp.float32
    ).astype(jnp.bfloat16)
    wout_term = lax.dot_general(
        hidden, grad_out, (((0,), (0,)), ((), ())), preferred_element_type=jnp.float32
    )
    d_monarch = (d_hidden.astype(jnp.float32) * gate.astype(jnp.float32)).astype(jnp.bfloat16)
    d_gate = (d_hidden.astype(jnp.float32) * monarch.astype(jnp.float32)).astype(jnp.bfloat16)
    grad_columns = lax.all_to_all(d_monarch, "seq", split_axis=0, concat_axis=0, tiled=True)
    grad_blocked = grad_columns.reshape(seq_count, row_count // seq_count, feature_count)
    for segment_bit in range(segment_total - 1, -1, -1):
        grad_blocked, partials[segment_bit] = local_back(
            grad_blocked, stored[segment_bit], twiddle_w[segment_bit], segment_bit
        )
    d_first = lax.all_to_all(
        grad_blocked.reshape(row_count, feature_count),
        "seq",
        split_axis=0,
        concat_axis=0,
        tiled=True,
    )
    twiddle_grad = lax.psum(jnp.stack(partials), "seq")
    d_value = lax.dot_general(
        square_mix, d_first, (((0,), (0,)), ((), ())), preferred_element_type=jnp.float32
    ).astype(jnp.bfloat16)
    grad_square = lax.dot_general(
        d_first, value, (((1,), (1,)), ((), ())), preferred_element_type=jnp.float32
    )
    d_projected = jnp.concatenate([d_value, d_gate], axis=1)
    win_term = lax.dot_general(
        inputs, d_projected, (((0,), (0,)), ((), ())), preferred_element_type=jnp.float32
    )
    win_share, wout_share = (
        lax.psum_scatter(win_term, "seq", scatter_dimension=0, tiled=True),
        lax.psum_scatter(wout_term, "seq", scatter_dimension=0, tiled=True),
    )
    input_grad = lax.dot_general(
        d_projected, w_in, (((1,), (1,)), ((), ())), preferred_element_type=jnp.float32
    ).astype(jnp.bfloat16)
    handed = from_behind(input_grad, "pipe", -1)
    return (
        mixed_out[None],
        handed[None],
        win_share[None],
        wout_share[None],
        grad_square[None],
        twiddle_grad[None],
    )


def solution(mesh):
    in_specs = (
        P("pipe", "seq", None),
        P("pipe", "seq", None),
        P("pipe", None, None),
        P("pipe", None, None),
        P("pipe", "seq", None),
        P("pipe", None, None, None, None),
    )
    out_specs = (
        P("pipe", "seq", None),
        P("pipe", "seq", None),
        P("pipe", "seq", None),
        P("pipe", "seq", None),
        P("pipe", "seq", None),
        P("pipe", None, None, None, None),
    )
    return jax.shard_map(
        on_device, mesh=mesh, in_specs=in_specs, out_specs=out_specs, check_vma=False
    )
```

profile of v0, /device:TPU:4, one launch (start us, length us, event | category | flops | bytes accessed | tf_op | source)
XLA Modules:
  0.0 244.0 jit_solution(5401887882448910427)
XLA Ops:
  7.2 3.8 %fusion.4 = bf16[256,2048]{1,0:T(8,128)(2,1)S(1)} fusion(bf16[1,1024,2048]{2,1,0:T(8,128)(2,1)} %param.8, bf16[1,256,1024]{2,1,0:T(8,128)(2,1)} %param.6), kind=kOutput, calls=%fused_computation.5 | convolution fusion | flops 1074266112 | bytes 5767168 | tf_op jit(solution)/shard_map/dot_general | solution.py:74
  11.0 1.0 copy-done.1
  11.9 1.1 convolution_convert_fusion
  13.0 4.9 %all-to-all-start = ((bf16[8,32,1024]{2,1,0:T(8,128)(2,1)}), bf16[8,32,1024]{2,1,0:T(8,128)(2,1)S(1)}, u32[]{:S(2)}, u32[]{:S(2)}) async-start(bf16[8,32,1024]{2,1,0:T(8,128)(2,1)} %bitcast.10), calls=%async_computation | async-start | bytes 1048576 | tf_op jit(solution)/shard_map/all_to_all | solution.py:81
  18.0 15.2 %all-to-all-done = bf16[8,32,1024]{2,1,0:T(8,128)(2,1)S(1)} async-done(((bf16[8,32,1024]{2,1,0:T(8,128)(2,1)}), bf16[8,32,1024]{2,1,0:T(8,128)(2,1)S(1)}, u32[]{:S(2)}, u32[]{:S(2)}) %all-to-all-start) | async-done | bytes 524320 | tf_op jit(solution)/shard_map/all_to_all | solution.py:81
  34.0 17.9 %all_to_all.33 = bf16[8,32,1024]{2,1,0:T(8,128)(2,1)S(1)} all-to-all(bf16[8,32,1024]{2,1,0:T(8,128)(2,1)S(1)} %bitcast.133), channel_id=1, replica_groups=mesh['pipe'=4,'seq'=8] {'seq'}, dimensions={0} | all-to-all | bytes 1048576 | tf_op jit(solution)/shard_map/all_to_all | solution.py:87
  51.9 0.9 fusion.24
  52.8 17.8 %all_to_all.34 = bf16[8,32,1024]{2,1,0:T(8,128)(2,1)S(1)} all-to-all(bf16[8,32,1024]{2,1,0:T(8,128)(2,1)S(1)} %bitcast.132), channel_id=1, replica_groups=mesh['pipe'=4,'seq'=8] {'seq'}, dimensions={0} | all-to-all | bytes 1048576 | tf_op jit(solution)/shard_map/all_to_all | solution.py:100
  70.6 0.4 fusion.43
  71.0 0.4 fusion.51
  71.4 0.4 fusion.59
  71.8 17.8 %all_to_all.35 = bf16[8,32,1024]{2,1,0:T(8,128)(2,1)S(1)} all-to-all(bf16[8,32,1024]{2,1,0:T(8,128)(2,1)S(1)} %bitcast.134), channel_id=1, replica_groups=mesh['pipe'=4,'seq'=8] {'seq'}, dimensions={0} | all-to-all | bytes 1048576 | tf_op jit(solution)/shard_map/all_to_all | solution.py:106
  90.0 0.8 copy-done.6
  90.7 4.5 %convolution_bitcast_fusion = f32[1024,2048]{0,1:T(8,128)} fusion(bf16[256,1024]{1,0:T(8,128)(2,1)S(1)} %get-tuple-element.26, bf16[256,1024]{1,0:T(8,128)(2,1)S(1)} %fusion.23, bf16[1,256,1024]{2,1,0:T(8,128)(2,1)S(1)} %copy-done.8), kind=kOutput, calls=%fused_computation | convolution fusion | flops 1075838976 | bytes 9961472 | tf_op jit(solution)/shard_map/dot_general | solution.py:121
  95.3 3.8 %fusion.63 = f32[1024,1024]{1,0:T(8,128)} fusion(bf16[256,1024]{1,0:T(8,128)(2,1)S(1)} %get-tuple-element.25, bf16[1,256,1024]{2,1,0:T(8,128)(2,1)} %param.7), kind=kOutput, calls=%fused_computation.103 | convolution fusion | flops 536870912 | bytes 5242880 | tf_op jit(solution)/shard_map/dot_general | solution.py:95
  99.1 1.5 fusion.20
  100.8 4.4 %fusion.17 = bf16[256,1024]{1,0:T(8,128)(2,1)} fusion(bf16[1,1024,2048]{2,1,0:T(8,128)(2,1)} %param.8, bf16[256,1024]{1,0:T(8,128)(2,1)S(1)} %copy-done.5, bf16[256,1024]{1,0:T(8,128)(2,1)S(1)} %copy-done.7), kind=kOutput, calls=%fused_computation.17 | convolution fusion | flops 1076101120 | bytes 5767168 | tf_op jit(solution)/shard_map/dot_general | solution.py:128
  105.2 3.3 %collective-permute-start = (bf16[256,1024]{1,0:T(8,128)(2,1)}, bf16[256,1024]{1,0:T(8,128)(2,1)S(1)}, u32[]{:S(2)}, u32[]{:S(2)}) collective-permute-start(bf16[256,1024]{1,0:T(8,128)(2,1)} %fusion.17), channel_id=1, source_target_pairs={{8,0},{16,8},{24,16},{9,1},{17,9},{25,17},{10,2},{18,10},{26,18},{... | collective-permute-start | bytes 1572872 | tf_op jit(solution)/shard_map/ppermute | solution.py:10
  108.6 30.0 %psum.7 = f32[1,3,2,2,1024]{4,3,2,1,0:T(2,128)} all-reduce(f32[1,3,2,2,1024]{4,3,2,1,0:T(2,128)S(1)} %maximum_bitcast_fusion), channel_id=1, replica_groups=mesh['pipe'=4,'seq'=8] {'seq'}, use_global_device_ids=true, to_apply=%region_14.0 | all-reduce | flops 12288 | bytes 98304 | tf_op jit(solution)/shard_map/psum | solution.py:113
  138.6 2.1 convolution_bitcast_fusion.1
  140.7 44.4 %reduce-scatter.3.cloned.1.call-done = f32[128,2048]{0,1:T(8,128)} async-done(((f32[1024,2048]{0,1:T(8,128)}), f32[128,2048]{0,1:T(8,128)}) %reduce-scatter.3.cloned.1.call-update) | async-done | bytes 1048592 | tf_op jit(solution)/shard_map/reduce_scatter | solution.py:125
  185.1 2.5 %copy.13 = f32[1,128,2048]{2,1,0:T(8,128)} copy(f32[1,128,2048]{1,2,0:T(8,128)} %bitcast.135) | data formatting | bytes 2097152
  187.7 48.7 %reduce-scatter.5.cloned.1.call-done = f32[128,1024]{1,0:T(8,128)} async-done(((f32[1024,1024]{1,0:T(8,128)}), f32[128,1024]{1,0:T(8,128)}) %reduce-scatter.5.cloned.1.call-update) | async-done | bytes 524304 | tf_op jit(solution)/shard_map/reduce_scatter | solution.py:126
  236.4 0.8 copy.16
  (48 shorter events, 1.5 us)
Async XLA Ops:
  7.2 44.7 %copy-start = (bf16[1,1024,1024]{2,1,0:T(8,128)(2,1)S(1)}, bf16[1,1024,1024]{2,1,0:T(8,128)(2,1)}, u32[]{:S(2)}) copy-start(bf16[1,1024,1024]{2,1,0:T(8,128)(2,1)} %param.9) | copy-start | bytes 6291460
  7.2 4.8 %copy-start.9 = (bf16[1,256,256]{2,1,0:T(8,128)(2,1)S(1)}, bf16[1,256,256]{2,1,0:T(8,128)(2,1)}, u32[]{:S(2)}) copy-start(bf16[1,256,256]{2,1,0:T(8,128)(2,1)} %param.10) | copy-start | bytes 393220
  11.0 1.0 copy-start.1
  11.9 6.0 %copy-start.10 = (f32[1,3,2,2,1024]{4,3,2,1,0:T(2,128)S(1)}, f32[1,3,2,2,1024]{4,3,2,1,0:T(2,128)}, u32[]{:S(2)}) copy-start(f32[1,3,2,2,1024]{4,3,2,1,0:T(2,128)} %param.11) | copy-start | bytes 147460
  13.0 20.2 %all-to-all-start = ((bf16[8,32,1024]{2,1,0:T(8,128)(2,1)}), bf16[8,32,1024]{2,1,0:T(8,128)(2,1)S(1)}, u32[]{:S(2)}, u32[]{:S(2)}) async-start(bf16[8,32,1024]{2,1,0:T(8,128)(2,1)} %bitcast.10), calls=%async_computation | async-start | bytes 1048576 | tf_op jit(solution)/shard_map/all_to_all | solution.py:81
  17.9 167.2 %reduce-scatter.3.cloned.1.call-start = ((), (), s32[]{:S(2)}) async-start(), calls=%async_computation.6 | async-start | bytes 9437184 | tf_op jit(solution)/shard_map/reduce_scatter | solution.py:125
  33.7 18.2 %copy-start.2 = (bf16[256,2048]{1,0:T(8,128)(2,1)S(1)}, bf16[256,2048]{1,0:T(8,128)(2,1)}, u32[]{:S(2)}) copy-start(bf16[256,2048]{1,0:T(8,128)(2,1)} %copy-done.1) | copy-start | bytes 3145732
  33.7 18.2 %copy-start.3 = (bf16[1,256,1024]{2,1,0:T(8,128)(2,1)S(1)}, bf16[1,256,1024]{2,1,0:T(8,128)(2,1)}, u32[]{:S(2)}) copy-start(bf16[1,256,1024]{2,1,0:T(8,128)(2,1)} %param.7) | copy-start | bytes 1572868
  52.8 37.2 %copy-start.4 = (bf16[256,1024]{1,0:T(8,128)(2,1)}, bf16[256,1024]{1,0:T(8,128)(2,1)S(1)}, u32[]{:S(2)}) copy-start(bf16[256,1024]{1,0:T(8,128)(2,1)S(1)} %get-tuple-element.26) | copy-start | bytes 1572868
  71.4 19.3 %copy-start.8 = (bf16[1,256,1024]{2,1,0:T(8,128)(2,1)S(1)}, bf16[1,256,1024]{2,1,0:T(8,128)(2,1)}, u32[]{:S(2)}) copy-start(bf16[1,256,1024]{2,1,0:T(8,128)(2,1)} %param.6) | copy-start | bytes 1572868
  90.0 0.8 copy-start.6
  95.3 141.1 %reduce-scatter.5.cloned.1.call-start = ((), (), s32[]{:S(2)}) async-start(), calls=%async_computation.7 | async-start | bytes 4718592 | tf_op jit(solution)/shard_map/reduce_scatter | solution.py:126
  99.1 1.7 copy-start.5
  99.1 1.7 copy-start.7
  105.2 35.5 %collective-permute-start = (bf16[256,1024]{1,0:T(8,128)(2,1)}, bf16[256,1024]{1,0:T(8,128)(2,1)S(1)}, u32[]{:S(2)}, u32[]{:S(2)}) collective-permute-start(bf16[256,1024]{1,0:T(8,128)(2,1)} %fusion.17), channel_id=1, source_target_pairs={{8,0},{16,8},{24,16},{9,1},{17,9},{25,17},{10,2},{18,10},{26,18},{... | collective-permute-start | bytes 1572872 | tf_op jit(solution)/shard_map/ppermute | solution.py:10
Sparse Core Ops, SparseCore 0:
  95.4 89.6 reduce-scatter.2
  188.0 48.3 reduce-scatter.4
where the time goes:
time: 246 us; the launch traced here: 244 us
  waiting for transfers between devices  108 us (44%)
  blocking collectives  83.4 us (34%)
  matrix products  22.4 us (9%)
  between operations  14.4 us (6%)
  starting transfers between devices  8.29 us (3%)
  local copies, waits for them, and re-layouts  5.15 us (2%)
    reduce_scatter x1, waiting for transfers between devices, on_device(): lax.psum_scatter(wout_term, 'seq', scatter_dimension=0, tiled=True)  48.7 us
    reduce_scatter x1, waiting for transfers between devices, on_device(): lax.psum_scatter(win_term, 'seq', scatter_dimension=0, tiled=True)  44.4 us
    psum x1, blocking collectives, on_device(): twiddle_grad = lax.psum(jnp.stack(partials), 'seq')  30 us
    all_to_all x1, blocking collectives, on_device(): lax.all_to_all(blocked.reshape(row_count, feature_count), 'seq', split_ax...  17.9 us
    all_to_all x1, blocking collectives, on_device(): lax.all_to_all(d_monarch, 'seq', split_axis=0, concat_axis=0, tiled=True)  17.8 us
    all_to_all x1, blocking collectives, on_device(): lax.all_to_all(grad_blocked.reshape(row_count, feature_count), 'seq', spl...  17.8 us
    all_to_all x1, waiting for transfers between devices, on_device(): lax.all_to_all(first_segment, 'seq', split_axis=0, concat_axis=0, tiled=T...  15.2 us
    unnamed x24, local copies, waits for them, and re-layouts  5.11 us
  transfers between devices with their start and end apart: 4, of which 3 were waited for; matrix products, arithmetic and copies ran while one was open for 6% of the time, Pallas kernels for 0%

commit v1 on v0

--- a/solution.py
+++ b/solution.py
@@ -1,6 +1,8 @@
 import jax
 import jax.numpy as jnp
 from jax import lax
+from jax.experimental import pallas as pl
+from jax.experimental.pallas import tpu as pltpu
 from jax.sharding import PartitionSpec as P
 
 
@@ -61,13 +63,7 @@
     return (prev, partial_value)
 
 
-def on_device(acts, cotan, proj_in, proj_out, block_mix, twiddle):
-    inputs = acts[0]
-    grad_out = cotan[0]
-    w_in = proj_in[0]
-    w_out = proj_out[0]
-    square_mix = block_mix[0]
-    twiddle_w = twiddle[0]
+def exchange_plan(inputs, grad_out, w_in, w_out, square_mix, twiddle_w):
     row_count, feature_count = inputs.shape
     seq_count = lax.axis_size("seq")
     segment_total = seq_count.bit_length() - 1
@@ -129,14 +125,320 @@
         d_projected, w_in, (((1,), (1,)), ((), ())), preferred_element_type=jnp.float32
     ).astype(jnp.bfloat16)
     handed = from_behind(input_grad, "pipe", -1)
-    return (
-        mixed_out[None],
-        handed[None],
-        win_share[None],
-        wout_share[None],
-        grad_square[None],
-        twiddle_grad[None],
-    )
+    return mixed_out, handed, win_share, wout_share, grad_square, twiddle_grad
+
+
+def chip_hops(hops):
+    return [(2 * source + core, 2 * target + core) for source, target in hops for core in (0, 1)]
+
+
+CORE_SWAP = [(index, index ^ 1) for index in range(8)]
+INWARD = chip_hops([(0, 1), (3, 2)])
+ACROSS = chip_hops([(1, 2), (2, 1)])
+OUTWARD = chip_hops([(1, 0), (2, 3)])
+
+
+def hop(value, pairs):
+    return lax.ppermute(value, "seq", pairs)
+
+
+def dot(left, right):
+    return jnp.dot(left, right, preferred_element_type=jnp.float32)
+
+
+def dot_rows(left, right):
+    return lax.dot_general(
+        left, right, (((0,), (0,)), ((), ())), preferred_element_type=jnp.float32
+    )
+
+
+def dot_columns(left, right):
+    return lax.dot_general(
+        left, right, (((1,), (1,)), ((), ())), preferred_element_type=jnp.float32
+    )
+
+
+def narrow(value):
+    return value.astype(jnp.bfloat16)
+
+
+def wide(value):
+    return value.astype(jnp.float32)
+
+
+def coef_at(coef_ref, bit, side, term):
+    return coef_ref[pl.ds(4 * bit + 2 * side + term, 1), :]
+
+
+def forward_kernel(coef_ref, *refs):
+    seg0 = refs[0:4]
+    swapped = refs[4:8]
+    gates = refs[8:12]
+    seg1_out, seg2_out, seg3_out, hidden_out = refs[12:16]
+    first = []
+    for k in range(4):
+        own, other = wide(seg0[k][...]), wide(swapped[k][...])
+        first.append(narrow(coef_at(coef_ref, 0, 0, 0) * own + coef_at(coef_ref, 0, 0, 1) * other))
+    for k in range(2):
+        seg1_out[k] = first[k]
+    first = [wide(part) for part in first]
+    second = []
+    for k in range(4):
+        side = k & 1
+        second.append(
+            narrow(
+                coef_at(coef_ref, 1, side, 0) * first[k]
+                + coef_at(coef_ref, 1, side, 1) * first[k ^ 1]
+            )
+        )
+        seg2_out[k] = second[k]
+    second = [wide(part) for part in second]
+    for k in range(4):
+        side = k >> 1
+        third = narrow(
+            coef_at(coef_ref, 2, side, 0) * second[k]
+            + coef_at(coef_ref, 2, side, 1) * second[k ^ 2]
+        )
+        seg3_out[k] = third
+        hidden_out[k] = narrow(wide(third) * wide(gates[k][...]))
+
+
+def row_groups(value):
+    rows, columns = value.shape
+    return value.reshape(rows // 8, 8, columns).sum(axis=0)
+
+
+def backward_kernel(coef_ref, *refs):
+    d_hidden = refs[0:4]
+    gates = refs[4:8]
+    seg1_ref, seg2_ref, seg3_ref = refs[8:11]
+    d_gate_out, d_seg1_out, partial_out = refs[11:14]
+
+    @pl.when(pl.program_id(0) == 0)
+    def _():
+        partial_out[...] = jnp.zeros_like(partial_out)
+
+    third = []
+    for k in range(4):
+        grad = wide(d_hidden[k][...])
+        d_gate_out[k] = narrow(grad * wide(seg3_ref[k]))
+        third.append(wide(narrow(grad * wide(gates[k][...]))))
+    for k in range(2):
+        partial_out[4] += row_groups(third[k] * wide(seg2_ref[k]))
+        partial_out[5] += row_groups(third[k] * wide(seg2_ref[k ^ 2]))
+    second = []
+    for k in range(4):
+        side = k >> 1
+        second.append(
+            wide(
+                narrow(
+                    coef_at(coef_ref, 2, side, 0) * third[k]
+                    + coef_at(coef_ref, 2, 1 - side, 1) * third[k ^ 2]
+                )
+            )
+        )
+    for k in range(2):
+        partial_out[2 * k] += row_groups(second[k] * wide(seg1_ref[k]))
+        partial_out[2 * k + 1] += row_groups(second[k] * wide(seg1_ref[k ^ 1]))
+    for k in range(4):
+        side = k & 1
+        d_seg1_out[k] = narrow(
+            coef_at(coef_ref, 1, side, 0) * second[k]
+            + coef_at(coef_ref, 1, 1 - side, 1) * second[k ^ 1]
+        )
+
+
+def first_bit_kernel(coef_ref, *refs):
+    d_seg1_ref, d_swapped_ref = refs[0:2]
+    seg0 = refs[2:4]
+    swapped = refs[4:6]
+    d_seg0_out, partial_out = refs[6:8]
+
+    @pl.when(pl.program_id(0) == 0)
+    def _():
+        partial_out[...] = jnp.zeros_like(partial_out)
+
+    for k in range(4):
+        own, other = wide(d_seg1_ref[k]), wide(d_swapped_ref[k])
+        d_seg0_out[k] = narrow(
+            coef_at(coef_ref, 0, 0, 0) * own + coef_at(coef_ref, 0, 1, 1) * other
+        )
+        if k < 2:
+            partial_out[0] += row_groups(own * wide(seg0[k][...]))
+            partial_out[1] += row_groups(own * wide(swapped[k][...]))
+
+
+TILE = 32
+
+
+def tile(columns, column_at=0, row_at=0):
+    return pl.BlockSpec((TILE, columns), lambda i: (i + row_at, column_at))
+
+
+def stacked(count, columns, row_at=0):
+    return pl.BlockSpec((count, TILE, columns), lambda i: (0, i + row_at, 0))
+
+
+def whole(*shape):
+    return pl.BlockSpec(shape, lambda i: (0,) * len(shape))
+
+
+def shape_of(kind, *shape):
+    return jax.ShapeDtypeStruct(shape, kind)
+
+
+def relay_plan(inputs, grad_out, w_in, w_out, mix, twiddle_w):
+    rows, width = inputs.shape
+    share = width // 8
+    place = lax.axis_index("seq")
+    chip, core = place // 2, place % 2
+    inner = (chip == 1) | (chip == 2)
+    flips = (core, chip & 1, chip >> 1)
+    coefs = jnp.concatenate(
+        [
+            jnp.where(flips[bit] == 1, twiddle_w[bit][::-1], twiddle_w[bit]).reshape(4, width)
+            for bit in range(3)
+        ]
+        + [jnp.zeros((4, width), jnp.float32)]
+    )
+    half = rows // 2
+
+    def everywhere(value):
+        outer = hop(value, INWARD)
+        return [value, outer, hop(outer, ACROSS), hop(value, ACROSS)]
+
+    mixes = everywhere(mix)
+    acts = everywhere(inputs)
+    cotans = [everywhere(grad_out[h * half : (h + 1) * half]) for h in range(2)]
+
+    projected = [narrow(dot(part, w_in)) for part in acts]
+    values = [part[:, :width] for part in projected]
+    seg0 = [narrow(dot(mixes[k], values[k])) for k in range(4)]
+    swapped = [hop(part, CORE_SWAP) for part in seg0]
+
+    bf16, f32 = jnp.bfloat16, jnp.float32
+    seg1, seg2, seg3, hidden = pl.pallas_call(
+        forward_kernel,
+        grid=(rows // TILE,),
+        in_specs=[whole(16, width)] + [tile(width)] * 8 + [tile(width, 1)] * 4,
+        out_specs=[stacked(2, width)] + [stacked(4, width)] * 3,
+        out_shape=[shape_of(bf16, 2, rows, width)] + [shape_of(bf16, 4, rows, width)] * 3,
+        cost_estimate=pl.CostEstimate(
+            flops=16 * rows * width, bytes_accessed=52 * rows * width, transcendentals=0
+        ),
+        compiler_params=pltpu.CompilerParams(vmem_limit_bytes=40 * 2**20),
+        name="forward_segments",
+    )(coefs, *seg0, *swapped, *projected)
+
+    def row_shares(value, axis):
+        pieces = []
+        for core_bit in (0, 1):
+            for chip_bit in (0, 1):
+                owner = 2 * (chip ^ chip_bit) + (core ^ core_bit)
+                pieces.append(lax.dynamic_slice_in_dim(value, owner * share, share, axis))
+        return jnp.concatenate(pieces, axis=axis)
+
+    act_columns = [row_shares(part, 1) for part in acts]
+    mixed_columns = [narrow(dot(mixes[k], act_columns[k])) for k in range(4)]
+    hidden_columns = row_shares(hidden, 2)
+
+    def half_of(parts, h):
+        return jnp.concatenate([part[h * half : (h + 1) * half] for part in parts], axis=0)
+
+    win_value, win_gate, wout, twiddle_parts, first_grads = 0.0, 0.0, 0.0, 0.0, []
+    for h in range(2):
+        at = h * (half // TILE)
+        d_hidden = [narrow(dot_columns(part, w_out)) for part in cotans[h]]
+        d_gate, d_seg1, later_part = pl.pallas_call(
+            backward_kernel,
+            grid=(half // TILE,),
+            in_specs=[whole(16, width)]
+            + [tile(width)] * 4
+            + [tile(width, 1, at)] * 4
+            + [stacked(2, width, at), stacked(4, width, at), stacked(4, width, at)],
+            out_specs=[stacked(4, width), stacked(4, width), whole(6, 8, width)],
+            out_shape=[
+                shape_of(bf16, 4, half, width),
+                shape_of(bf16, 4, half, width),
+                shape_of(f32, 6, 8, width),
+            ],
+            cost_estimate=pl.CostEstimate(
+                flops=20 * half * width, bytes_accessed=52 * half * width, transcendentals=0
+            ),
+            compiler_params=pltpu.CompilerParams(vmem_limit_bytes=40 * 2**20),
+            name="backward_segments",
+        )(coefs, *d_hidden, *projected, seg1, seg2, seg3)
+        d_swapped = hop(d_seg1, CORE_SWAP)
+        d_seg0, first_part = pl.pallas_call(
+            first_bit_kernel,
+            grid=(half // TILE,),
+            in_specs=[whole(16, width)]
+            + [stacked(4, width)] * 2
+            + [tile(width, 0, at)] * 4,
+            out_specs=[stacked(4, width), whole(2, 8, width)],
+            out_shape=[shape_of(bf16, 4, half, width), shape_of(f32, 2, 8, width)],
+            cost_estimate=pl.CostEstimate(
+                flops=20 * half * width, bytes_accessed=32 * half * width, transcendentals=0
+            ),
+            compiler_params=pltpu.CompilerParams(vmem_limit_bytes=40 * 2**20),
+            name="first_segment_grad",
+        )(coefs, d_seg1, d_swapped, *seg0[:2], *swapped[:2])
+        first_grads.append(d_seg0)
+        d_gate_rows = d_gate.reshape(4 * half, width)
+        d_seg0_rows = d_seg0.reshape(4 * half, width)
+        hidden_rows = hidden_columns[:, h * half : (h + 1) * half].reshape(4 * half, width // 2)
+        win_gate += dot_rows(half_of(act_columns, h), d_gate_rows)
+        win_value += dot_rows(half_of(mixed_columns, h), d_seg0_rows)
+        wout += dot_rows(hidden_rows, jnp.concatenate(cotans[h], axis=0))
+        twiddle_parts += jnp.concatenate([first_part, later_part], axis=0).sum(axis=1)
+
+    def combine(term):
+        kept = 2 * share
+        total = term[:kept] + wide(hop(narrow(term[kept:]), CORE_SWAP))
+        arrived = wide(hop(narrow(total[share:]), OUTWARD))
+        return jnp.where(inner, total[:share], arrived)
+
+    wout_share = combine(wout)
+    gate_share = combine(win_gate)
+    value_share = combine(win_value)
+
+    def one_side(pair, flip):
+        empty = jnp.zeros_like(pair)
+        return jnp.where(flip == 1, jnp.stack([empty, pair]), jnp.stack([pair, empty]))
+
+    both = twiddle_parts[2:6].reshape(2, 2, width)
+    terms = jnp.stack(
+        [
+            one_side(twiddle_parts[0:2], flips[0]),
+            jnp.where(flips[1] == 1, both[::-1], both),
+            one_side(twiddle_parts[6:8], flips[2]),
+        ]
+    )
+    terms = terms + hop(terms, CORE_SWAP)
+    terms = terms + hop(terms, ACROSS)
+    twiddle_grad = jnp.where(inner, terms, hop(terms, OUTWARD))
+
+    monarch = jnp.where(inner, seg3[0], hop(seg3[1], OUTWARD))
+    gate = projected[0][:, width:]
+    mixed_out = narrow(dot(narrow(wide(monarch) * wide(gate)), w_out))
+    own_d_hidden = narrow(dot_columns(grad_out, w_out))
+    own_d_gate = narrow(wide(own_d_hidden) * wide(monarch))
+    own_d_first = jnp.concatenate(
+        [jnp.where(inner, part[0], hop(part[1], OUTWARD)) for part in first_grads], axis=0
+    )
+    d_value = narrow(dot_rows(mix, own_d_first))
+    grad_square = dot_columns(own_d_first, values[0])
+    input_grad = narrow(
+        dot_columns(d_value, w_in[:, :width]) + dot_columns(own_d_gate, w_in[:, width:])
+    )
+    handed = from_behind(input_grad, "pipe", -1)
+    win_share = jnp.concatenate([value_share, gate_share], axis=1)
+    return mixed_out, handed, win_share, wout_share, grad_square, twiddle_grad
+
+
+def on_device(*arguments):
+    plan = relay_plan if lax.axis_size("seq") == 8 else exchange_plan
+    return tuple(result[None] for result in plan(*(part[0] for part in arguments)))
 
 
 def solution(mesh):

time: 246 us -> 175 us (0.71)
  the two profiles are of different devices: /device:TPU:4 before, /device:TPU:10 now
where the time goes in v1:
time: 175 us; the launch traced here: 174 us
  starting transfers between devices  48.2 us (28%)
  matrix products  44 us (25%)
  waiting for transfers between devices  43.8 us (25%)
  local copies, waits for them, and re-layouts  13.6 us (8%)
  Pallas kernels  11.5 us (7%)
  other arithmetic  10.7 us (6%)
    ppermute x30, starting transfers between devices, hop(): return lax.ppermute(value, 'seq', pairs)  45.7 us
    ppermute x30, waiting for transfers between devices, hop(): return lax.ppermute(value, 'seq', pairs)  34.4 us
    dot_general x11, matrix products, dot_columns(): lax.dot_general(left, right, (((1,), (1,)), ((), ())), preferred_element_...  20.4 us
    dot_general x13, matrix products, dot(): return jnp.dot(left, right, preferred_element_type=jnp.float32)  15.6 us
    ppermute x1, waiting for transfers between devices, from_behind(): lax.ppermute(value, axis, [(source, source + steps) for source in range(f...  9.4 us
    dot_general x6, matrix products, dot_rows(): lax.dot_general(left, right, (((0,), (0,)), ((), ())), preferred_element_...  8.07 us
    pallas_call x1, Pallas kernels, relay_plan(): pl.pallas_call(forward_kernel, grid=(rows // TILE,), in_specs=[whole(16,...  5.08 us
    pallas_call x2, Pallas kernels, relay_plan(): pl.pallas_call(backward_kernel, grid=(half // TILE,), in_specs=[whole(16,...  4.68 us
  transfers between devices with their start and end apart: 31, of which 9 were waited for; matrix products, arithmetic and copies ran while one was open for 34% of the time, Pallas kernels for 3%

profile of v1, /device:TPU:10, one launch (start us, length us, event | category | flops | bytes accessed | tf_op | source)
XLA Modules:
  0.0 173.7 jit_solution(1605301537826185885)
XLA Ops:
  2.1 3.5 %collective-permute-start.5 = (bf16[256,256]{1,0:T(8,128)(2,1)}, bf16[256,256]{1,0:T(8,128)(2,1)}, u32[]{:S(2)}, u32[]{:S(2)}) collective-permute-start(bf16[256,256]{1,0:T(8,128)(2,1)} %bitcast.185), channel_id=1, source_target_pairs={{2,4},{3,5},{4,2},{5,3},{10,12},{11,13},{12,10},{13,11},{18,20},{1... | collective-permute-start | bytes 393224 | tf_op jit(solution)/shard_map/ppermute | solution.py:142
  7.4 2.3 %collective-permute-start.13 = (bf16[128,1024]{1,0:T(8,128)(2,1)}, bf16[128,1024]{1,0:T(8,128)(2,1)}, u32[]{:S(2)}, u32[]{:S(2)}) collective-permute-start(bf16[128,1024]{1,0:T(8,128)(2,1)} %get-tuple-element.56), channel_id=1, source_target_pairs={{2,4},{3,5},{4,2},{5,3},{10,12},{11,13},{12,10},{13,11},{18,20},{1... | collective-permute-start | bytes 786440 | tf_op jit(solution)/shard_map/ppermute | solution.py:142
  11.1 3.5 %collective-permute-start.18 = (bf16[128,1024]{1,0:T(8,128)(2,1)}, bf16[128,1024]{1,0:T(8,128)(2,1)}, u32[]{:S(2)}, u32[]{:S(2)}) collective-permute-start(bf16[128,1024]{1,0:T(8,128)(2,1)} %get-tuple-element.57), channel_id=1, source_target_pairs={{2,4},{3,5},{4,2},{5,3},{10,12},{11,13},{12,10},{13,11},{18,20},{1... | collective-permute-start | bytes 786440 | tf_op jit(solution)/shard_map/ppermute | solution.py:142
  20.1 3.6 %convolution_convert_fusion.3.refs_8_.refs_4_ = bf16[256,2048]{1,0:T(8,128)(2,1)S(1)} fusion(bf16[1,1024,2048]{2,1,0:T(8,128)(2,1)} %param.8, bf16[1,256,1024]{2,1,0:T(8,128)(2,1)} %param.6), kind=kOutput, calls=%fused_computation.3 | convolution fusion | flops 1074266112 | bytes 5767168 | tf_op jit(solution)/shard_map/dot_general | solution.py:146
  32.1 2.4 %collective-permute-start.4 = (bf16[256,1024]{1,0:T(8,128)(2,1)S(1)}, bf16[256,1024]{1,0:T(8,128)(2,1)S(1)}, u32[]{:S(2)}, u32[]{:S(2)}) collective-permute-start(bf16[256,1024]{1,0:T(8,128)(2,1)S(1)} %bitcast.187), channel_id=1, source_target_pairs={{2,4},{3,5},{4,2},{5,3},{10,12},{11,13},{12,10},{13,11},{18,20},{1... | collective-permute-start | bytes 1572872 | tf_op jit(solution)/shard_map/ppermute | solution.py:142
  37.2 2.7 %collective-permute-start.3 = (bf16[256,256]{1,0:T(8,128)(2,1)}, bf16[256,256]{1,0:T(8,128)(2,1)S(1)}, u32[]{:S(2)}, u32[]{:S(2)}) collective-permute-start(bf16[256,256]{1,0:T(8,128)(2,1)} %collective-permute-done.1), channel_id=1, source_target_pairs={{2,4},{3,5},{4,2},{5,3},{10,12},{11,13},{12,10},{13,11},{18,20},{1... | collective-permute-start | bytes 393224 | tf_op jit(solution)/shard_map/ppermute | solution.py:142
  40.8 5.6 %collective-permute-done = bf16[256,1024]{1,0:T(8,128)(2,1)S(1)} collective-permute-done((bf16[256,1024]{1,0:T(8,128)(2,1)S(1)}, bf16[256,1024]{1,0:T(8,128)(2,1)S(1)}, u32[]{:S(2)}, u32[]{:S(2)}) %collective-permute-start) | collective-permute-done | bytes 524320 | tf_op jit(solution)/shard_map/ppermute | solution.py:142
  46.4 2.3 %collective-permute-start.12 = (bf16[128,1024]{1,0:T(8,128)(2,1)}, bf16[128,1024]{1,0:T(8,128)(2,1)S(1)}, u32[]{:S(2)}, u32[]{:S(2)}) collective-permute-start(bf16[128,1024]{1,0:T(8,128)(2,1)} %collective-permute-done.11), channel_id=1, source_target_pairs={{2,4},{3,5},{4,2},{5,3},{10,12},{11,13},{12,10},{13,11},{18,20},{1... | collective-permute-start | bytes 786440 | tf_op jit(solution)/shard_map/ppermute | solution.py:142
  48.9 3.5 %collective-permute-start.17 = (bf16[128,1024]{1,0:T(8,128)(2,1)S(1)}, bf16[128,1024]{1,0:T(8,128)(2,1)S(1)}, u32[]{:S(2)}, u32[]{:S(2)}) collective-permute-start(bf16[128,1024]{1,0:T(8,128)(2,1)S(1)} %collective-permute-done.16), channel_id=1, source_target_pairs={{2,4},{3,5},{4,2},{5,3},{10,12},{11,13},{12,10},{13,11},{18,20},{1... | collective-permute-start | bytes 786440 | tf_op jit(solution)/shard_map/ppermute | solution.py:142
  58.3 2.5 %collective-permute-start.2 = (bf16[256,1024]{1,0:T(8,128)(2,1)S(1)}, bf16[256,1024]{1,0:T(8,128)(2,1)S(1)}, u32[]{:S(2)}, u32[]{:S(2)}) collective-permute-start(bf16[256,1024]{1,0:T(8,128)(2,1)S(1)} %collective-permute-done), channel_id=1, source_target_pairs={{2,4},{3,5},{4,2},{5,3},{10,12},{11,13},{12,10},{13,11},{18,20},{1... | collective-permute-start | bytes 1572872 | tf_op jit(solution)/shard_map/ppermute | solution.py:142
  65.8 8.7 %collective-permute-done.2 = bf16[256,1024]{1,0:T(8,128)(2,1)S(1)} collective-permute-done((bf16[256,1024]{1,0:T(8,128)(2,1)S(1)}, bf16[256,1024]{1,0:T(8,128)(2,1)S(1)}, u32[]{:S(2)}, u32[]{:S(2)}) %collective-permute-start.2) | collective-permute-done | bytes 524320 | tf_op jit(solution)/shard_map/ppermute | solution.py:142
  78.1 5.1 %forward_segments.1 = (bf16[2,256,1024]{2,1,0:T(8,128)(2,1)S(1)}, bf16[4,256,1024]{2,1,0:T(8,128)(2,1)S(1)}, bf16[4,256,1024]{2,1,0:T(8,128)(2,1)S(1)}, bf16[4,256,1024]{2,1,0:T(8,128)(2,1)}) custom-call(f32[16,1024]{1,0:T(8,128)S(1)} %maximum_maximum_fusion.coef_ref, bf16[256,1024]{1,0:T(8,128)(2,1)S(1)} %fusion.47.refs_0_.refs_2_, ...), custom_call_target="tpu_custom_call" | custom-call | flops 4194304 | bytes 13631488 | tf_op jit(solution)/shard_map/forward_segments/pallas_call | solution.py:320
  89.4 2.3 %backward_segments.3 = (bf16[4,128,1024]{2,1,0:T(8,128)(2,1)S(1)}, bf16[4,128,1024]{2,1,0:T(8,128)(2,1)S(1)}, f32[6,8,1024]{2,1,0:T(8,128)S(1)}) custom-call(f32[16,1024]{1,0:T(8,128)S(1)} %maximum_maximum_fusion.coef_ref, bf16[128,1024]{1,0:T(8,128)(2,1)S(1)} %copy-done.4, bf16[128,1024]{1,0:T(8,128)(2,1)S(1)} %fusion.66.refs_1_, ...), custom_call_target="tpu_custom_call" | custom-call | flops 2621440 | bytes 6815744 | tf_op jit(solution)/shard_map/backward_segments/pallas_call | solution.py:352
  91.7 2.4 %backward_segments.2 = (bf16[4,128,1024]{2,1,0:T(8,128)(2,1)S(1)}, bf16[4,128,1024]{2,1,0:T(8,128)(2,1)S(1)}, f32[6,8,1024]{2,1,0:T(8,128)S(1)}) custom-call(f32[16,1024]{1,0:T(8,128)S(1)} %maximum_maximum_fusion.coef_ref, bf16[128,1024]{1,0:T(8,128)(2,1)S(1)} %fusion.51.refs_0_, bf16[128,1024]{1,0:T(8,128)(2,1)S(1)} %fusion.54.refs_1_, ...), custom_call_target="tpu_custom_call" | custom-call | flops 2621440 | bytes 6815744 | tf_op jit(solution)/shard_map/backward_segments/pallas_call | solution.py:352
  101.1 8.5 %collective-permute-done.10 = bf16[256,1024]{1,0:T(8,128)(2,1)S(1)} collective-permute-done((bf16[256,1024]{1,0:T(8,128)(2,1)S(1)}, bf16[256,1024]{1,0:T(8,128)(2,1)S(1)}, u32[]{:S(2)}, u32[]{:S(2)}) %collective-permute-start.10) | collective-permute-done | bytes 524320 | tf_op jit(solution)/shard_map/ppermute | solution.py:142
  111.2 4.1 %collective-permute-done.27 = bf16[128,1024]{1,0:T(8,128)(2,1)S(1)} collective-permute-done((bf16[128,1024]{1,0:T(8,128)(2,1)S(1)}, bf16[128,1024]{1,0:T(8,128)(2,1)S(1)}, u32[]{:S(2)}, u32[]{:S(2)}) %collective-permute-start.27) | collective-permute-done | bytes 262176 | tf_op jit(solution)/shard_map/ppermute | solution.py:142
  116.1 4.3 %collective-permute-done.25 = bf16[128,1024]{1,0:T(8,128)(2,1)S(1)} collective-permute-done((bf16[128,1024]{1,0:T(8,128)(2,1)S(1)}, bf16[128,1024]{1,0:T(8,128)(2,1)S(1)}, u32[]{:S(2)}, u32[]{:S(2)}) %collective-permute-start.25) | collective-permute-done | bytes 262176 | tf_op jit(solution)/shard_map/ppermute | solution.py:142
  124.9 5.1 %collective-permute-start.20 = (bf16[128,1024]{1,0:T(8,128)(2,1)S(1)}, bf16[128,1024]{1,0:T(8,128)(2,1)}, u32[]{:S(2)}, u32[]{:S(2)}) collective-permute-start(bf16[128,1024]{1,0:T(8,128)(2,1)S(1)} %slice_bitcast_fusion.1), channel_id=1, source_target_pairs={{2,0},{3,1},{4,6},{5,7},{10,8},{11,9},{12,14},{13,15},{18,16},{19,... | collective-permute-start | bytes 786440 | tf_op jit(solution)/shard_map/ppermute | solution.py:142
  135.4 2.3 %fusion.110 = f32[512,1024]{1,0:T(8,128)S(1)} fusion(bf16[512,1024]{1,0:T(8,128)(2,1)} %bitcast.179, bf16[128,512]{1,0:T(8,128)(2,1)} %get-tuple-element.65, bf16[128,512]{1,0:T(8,128)(2,1)} %get-tuple-element.63, bf16[128,512]{1,0:T(8,128)(2,1)} %get-tuple-element.61, bf16[128,512]{1,0:T(8,128)(2,1)S(1)} %copy-done.17), kind=kOutput, calls=%fused_computation.109 | convolution fusion | flops 538968064 | bytes 3670016 | tf_op jit(solution)/shard_map/dot_general | solution.py:150
  137.7 2.4 %collective-permute-start.29 = (f32[3,2,2,1024]{3,2,1,0:T(2,128)S(1)}, f32[3,2,2,1024]{3,2,1,0:T(2,128)S(1)}, u32[]{:S(2)}, u32[]{:S(2)}) collective-permute-start(f32[3,2,2,1024]{3,2,1,0:T(2,128)S(1)} %fusion.156), channel_id=1, source_target_pairs={{2,4},{3,5},{4,2},{5,3},{10,12},{11,13},{12,10},{13,11},{18,20},{1... | collective-permute-start | bytes 147464 | tf_op jit(solution)/shard_map/ppermute | solution.py:142
  147.1 3.7 %fusion.2 = f32[256,1024]{1,0:T(8,128)} fusion(bf16[1024,2048]{1,0:T(8,128)(2,1)} %bitcast.188, bf16[128,1024]{1,0:T(8,128)(2,1)S(1)} %bitcast_select_fusion.1, bf16[128,1024]{1,0:T(8,128)(2,1)} %bitcast_select_fusion.2, bf16[1,256,256]{2,1,0:T(8,128)(2,1)} %param.10), kind=kOutput, calls=%fused_computation.6 | convolution fusion | flops 672399360 | bytes 3801088 | tf_op jit(solution)/shard_map/dot_general | solution.py:156
  150.8 4.3 %fusion.41 = bf16[256,1024]{1,0:T(8,128)(2,1)} fusion(f32[256,1024]{1,0:T(8,128)} %fusion.2, bf16[1024,2048]{1,0:T(8,128)(2,1)} %bitcast.189, bf16[1,1024,1024]{2,1,0:T(8,128)(2,1)S(1)} %copy-done, bf16[1,256,1024]{2,1,0:T(8,128)(2,1)} %param.7, bf16[256,1024]{1,0:T(8,128)(2,1)} %copy-done.20, bf16[4,256,1024]{2,1,0:T(8,128)(2,1)} %copy-done.1, pred[]{:T(512)S(6)} %or.3), kind=kOutput, calls=%fused_computation.43 | convolution fusion | flops 1075838976 | bytes 7340033 | tf_op jit(solution)/shard_map/dot_general | solution.py:156
  155.1 2.6 %collective-permute-start.21 = (bf16[256,1024]{1,0:T(8,128)(2,1)}, bf16[256,1024]{1,0:T(8,128)(2,1)S(1)}, u32[]{:S(2)}, u32[]{:S(2)}) collective-permute-start(bf16[256,1024]{1,0:T(8,128)(2,1)} %fusion.41), channel_id=1, source_target_pairs={{8,0},{16,8},{24,16},{9,1},{17,9},{25,17},{10,2},{18,10},{26,18},{... | collective-permute-start | bytes 1572872 | tf_op jit(solution)/shard_map/ppermute | solution.py:12
  162.4 9.4 %collective-permute-done.21 = bf16[256,1024]{1,0:T(8,128)(2,1)S(1)} collective-permute-done((bf16[256,1024]{1,0:T(8,128)(2,1)}, bf16[256,1024]{1,0:T(8,128)(2,1)S(1)}, u32[]{:S(2)}, u32[]{:S(2)}) %collective-permute-start.21) | collective-permute-done | bytes 524320 | tf_op jit(solution)/shard_map/ppermute | solution.py:12
  (174 shorter events, 75.0 us)
Async XLA Ops:
  0.7 35.8 %collective-permute-start.1 = (bf16[256,256]{1,0:T(8,128)(2,1)}, bf16[256,256]{1,0:T(8,128)(2,1)}, u32[]{:S(2)}, u32[]{:S(2)}) collective-permute-start(bf16[256,256]{1,0:T(8,128)(2,1)} %bitcast.184), channel_id=1, source_target_pairs={{0,2},{1,3},{6,4},{7,5},{8,10},{9,11},{14,12},{15,13},{16,18},{17,... | collective-permute-start | bytes 393224 | tf_op jit(solution)/shard_map/ppermute | solution.py:142
  2.1 53.5 %collective-permute-start.5 = (bf16[256,256]{1,0:T(8,128)(2,1)}, bf16[256,256]{1,0:T(8,128)(2,1)}, u32[]{:S(2)}, u32[]{:S(2)}) collective-permute-start(bf16[256,256]{1,0:T(8,128)(2,1)} %bitcast.185), channel_id=1, source_target_pairs={{2,4},{3,5},{4,2},{5,3},{10,12},{11,13},{12,10},{13,11},{18,20},{1... | collective-permute-start | bytes 393224 | tf_op jit(solution)/shard_map/ppermute | solution.py:142
  7.4 18.4 %collective-permute-start.13 = (bf16[128,1024]{1,0:T(8,128)(2,1)}, bf16[128,1024]{1,0:T(8,128)(2,1)}, u32[]{:S(2)}, u32[]{:S(2)}) collective-permute-start(bf16[128,1024]{1,0:T(8,128)(2,1)} %get-tuple-element.56), channel_id=1, source_target_pairs={{2,4},{3,5},{4,2},{5,3},{10,12},{11,13},{12,10},{13,11},{18,20},{1... | collective-permute-start | bytes 786440 | tf_op jit(solution)/shard_map/ppermute | solution.py:142
  9.8 19.2 %collective-permute-start.11 = (bf16[128,1024]{1,0:T(8,128)(2,1)}, bf16[128,1024]{1,0:T(8,128)(2,1)}, u32[]{:S(2)}, u32[]{:S(2)}) collective-permute-start(bf16[128,1024]{1,0:T(8,128)(2,1)} %get-tuple-element.56), channel_id=1, source_target_pairs={{0,2},{1,3},{6,4},{7,5},{8,10},{9,11},{14,12},{15,13},{16,18},{17,... | collective-permute-start | bytes 786440 | tf_op jit(solution)/shard_map/ppermute | solution.py:142
  11.1 21.0 %collective-permute-start.18 = (bf16[128,1024]{1,0:T(8,128)(2,1)}, bf16[128,1024]{1,0:T(8,128)(2,1)}, u32[]{:S(2)}, u32[]{:S(2)}) collective-permute-start(bf16[128,1024]{1,0:T(8,128)(2,1)} %get-tuple-element.57), channel_id=1, source_target_pairs={{2,4},{3,5},{4,2},{5,3},{10,12},{11,13},{12,10},{13,11},{18,20},{1... | collective-permute-start | bytes 786440 | tf_op jit(solution)/shard_map/ppermute | solution.py:142
  29.0 17.4 %collective-permute-start = (bf16[256,1024]{1,0:T(8,128)(2,1)S(1)}, bf16[256,1024]{1,0:T(8,128)(2,1)S(1)}, u32[]{:S(2)}, u32[]{:S(2)}) collective-permute-start(bf16[256,1024]{1,0:T(8,128)(2,1)S(1)} %bitcast.186), channel_id=1, source_target_pairs={{0,2},{1,3},{6,4},{7,5},{8,10},{9,11},{14,12},{15,13},{16,18},{17,... | collective-permute-start | bytes 1572872 | tf_op jit(solution)/shard_map/ppermute | solution.py:142
  32.1 16.8 %collective-permute-start.4 = (bf16[256,1024]{1,0:T(8,128)(2,1)S(1)}, bf16[256,1024]{1,0:T(8,128)(2,1)S(1)}, u32[]{:S(2)}, u32[]{:S(2)}) collective-permute-start(bf16[256,1024]{1,0:T(8,128)(2,1)S(1)} %bitcast.187), channel_id=1, source_target_pairs={{2,4},{3,5},{4,2},{5,3},{10,12},{11,13},{12,10},{13,11},{18,20},{1... | collective-permute-start | bytes 1572872 | tf_op jit(solution)/shard_map/ppermute | solution.py:142
  36.4 40.9 %collective-permute-start.6 = (bf16[256,1024]{1,0:T(8,128)(2,1)S(1)}, bf16[256,1024]{1,0:T(8,128)(2,1)S(1)}, u32[]{:S(2)}, u32[]{:S(2)}) collective-permute-start(bf16[256,1024]{1,0:T(8,128)(2,1)S(1)} %fusion.47.refs_0_.refs_2_), channel_id=1, source_target_pairs={{0,1},{1,0},{2,3},{3,2},{4,5},{5,4},{6,7},{7,6},{8,9},{9,8},{10,11... | collective-permute-start | bytes 1572872 | tf_op jit(solution)/shard_map/ppermute | solution.py:142
  37.2 38.5 %collective-permute-start.3 = (bf16[256,256]{1,0:T(8,128)(2,1)}, bf16[256,256]{1,0:T(8,128)(2,1)S(1)}, u32[]{:S(2)}, u32[]{:S(2)}) collective-permute-start(bf16[256,256]{1,0:T(8,128)(2,1)} %collective-permute-done.1), channel_id=1, source_target_pairs={{2,4},{3,5},{4,2},{5,3},{10,12},{11,13},{12,10},{13,11},{18,20},{1... | collective-permute-start | bytes 393224 | tf_op jit(solution)/shard_map/ppermute | solution.py:142
  48.9 15.9 %collective-permute-start.17 = (bf16[128,1024]{1,0:T(8,128)(2,1)S(1)}, bf16[128,1024]{1,0:T(8,128)(2,1)S(1)}, u32[]{:S(2)}, u32[]{:S(2)}) collective-permute-start(bf16[128,1024]{1,0:T(8,128)(2,1)S(1)} %collective-permute-done.16), channel_id=1, source_target_pairs={{2,4},{3,5},{4,2},{5,3},{10,12},{11,13},{12,10},{13,11},{18,20},{1... | collective-permute-start | bytes 786440 | tf_op jit(solution)/shard_map/ppermute | solution.py:142
  56.8 20.5 %collective-permute-start.9 = (bf16[256,1024]{1,0:T(8,128)(2,1)S(1)}, bf16[256,1024]{1,0:T(8,128)(2,1)S(1)}, u32[]{:S(2)}, u32[]{:S(2)}) collective-permute-start(bf16[256,1024]{1,0:T(8,128)(2,1)S(1)} %fusion.50.refs_3_), channel_id=1, source_target_pairs={{0,1},{1,0},{2,3},{3,2},{4,5},{5,4},{6,7},{7,6},{8,9},{9,8},{10,11... | collective-permute-start | bytes 1572872 | tf_op jit(solution)/shard_map/ppermute | solution.py:142
  58.3 16.2 %collective-permute-start.2 = (bf16[256,1024]{1,0:T(8,128)(2,1)S(1)}, bf16[256,1024]{1,0:T(8,128)(2,1)S(1)}, u32[]{:S(2)}, u32[]{:S(2)}) collective-permute-start(bf16[256,1024]{1,0:T(8,128)(2,1)S(1)} %collective-permute-done), channel_id=1, source_target_pairs={{2,4},{3,5},{4,2},{5,3},{10,12},{11,13},{12,10},{13,11},{18,20},{1... | collective-permute-start | bytes 1572872 | tf_op jit(solution)/shard_map/ppermute | solution.py:142
  64.8 12.5 %collective-permute-start.7 = (bf16[256,1024]{1,0:T(8,128)(2,1)S(1)}, bf16[256,1024]{1,0:T(8,128)(2,1)S(1)}, u32[]{:S(2)}, u32[]{:S(2)}) collective-permute-start(bf16[256,1024]{1,0:T(8,128)(2,1)S(1)} %fusion.48.refs_1_.refs_3_), channel_id=1, source_target_pairs={{0,1},{1,0},{2,3},{3,2},{4,5},{5,4},{6,7},{7,6},{8,9},{9,8},{10,11... | collective-permute-start | bytes 1572872 | tf_op jit(solution)/shard_map/ppermute | solution.py:142
  96.1 13.5 %collective-permute-start.10 = (bf16[256,1024]{1,0:T(8,128)(2,1)S(1)}, bf16[256,1024]{1,0:T(8,128)(2,1)S(1)}, u32[]{:S(2)}, u32[]{:S(2)}) collective-permute-start(bf16[256,1024]{1,0:T(8,128)(2,1)S(1)} %slice_bitcast_fusion), channel_id=1, source_target_pairs={{2,0},{3,1},{4,6},{5,7},{10,8},{11,9},{12,14},{13,15},{18,16},{19,... | collective-permute-start | bytes 1572872 | tf_op jit(solution)/shard_map/ppermute | solution.py:142
  97.4 23.8 %collective-permute-start.19 = (bf16[4,128,1024]{2,1,0:T(8,128)(2,1)S(1)}, bf16[4,128,1024]{2,1,0:T(8,128)(2,1)S(1)}, u32[]{:S(2)}, u32[]{:S(2)}) collective-permute-start(bf16[4,128,1024]{2,1,0:T(8,128)(2,1)S(1)} %get-tuple-element.25.refs_0_), channel_id=1, source_target_pairs={{0,1},{1,0},{2,3},{3,2},{4,5},{5,4},{6,7},{7,6},{8,9},{9,8},{10,11... | collective-permute-start | bytes 3145736 | tf_op jit(solution)/shard_map/ppermute | solution.py:142
  97.6 24.6 %collective-permute-start.14 = (bf16[4,128,1024]{2,1,0:T(8,128)(2,1)S(1)}, bf16[4,128,1024]{2,1,0:T(8,128)(2,1)S(1)}, u32[]{:S(2)}, u32[]{:S(2)}) collective-permute-start(bf16[4,128,1024]{2,1,0:T(8,128)(2,1)S(1)} %get-tuple-element.23.refs_0_), channel_id=1, source_target_pairs={{0,1},{1,0},{2,3},{3,2},{4,5},{5,4},{6,7},{7,6},{8,9},{9,8},{10,11... | collective-permute-start | bytes 3145736 | tf_op jit(solution)/shard_map/ppermute | solution.py:142
  98.2 17.0 %collective-permute-start.27 = (bf16[128,1024]{1,0:T(8,128)(2,1)S(1)}, bf16[128,1024]{1,0:T(8,128)(2,1)S(1)}, u32[]{:S(2)}, u32[]{:S(2)}) collective-permute-start(bf16[128,1024]{1,0:T(8,128)(2,1)S(1)} %slice.324), channel_id=1, source_target_pairs={{2,0},{3,1},{4,6},{5,7},{10,8},{11,9},{12,14},{13,15},{18,16},{19,... | collective-permute-start | bytes 786440 | tf_op jit(solution)/shard_map/ppermute | solution.py:142
  99.8 20.6 %collective-permute-start.25 = (bf16[128,1024]{1,0:T(8,128)(2,1)S(1)}, bf16[128,1024]{1,0:T(8,128)(2,1)S(1)}, u32[]{:S(2)}, u32[]{:S(2)}) collective-permute-start(bf16[128,1024]{1,0:T(8,128)(2,1)S(1)} %slice.325), channel_id=1, source_target_pairs={{2,0},{3,1},{4,6},{5,7},{10,8},{11,9},{12,14},{13,15},{18,16},{19,... | collective-permute-start | bytes 786440 | tf_op jit(solution)/shard_map/ppermute | solution.py:142
  124.9 20.5 %collective-permute-start.20 = (bf16[128,1024]{1,0:T(8,128)(2,1)S(1)}, bf16[128,1024]{1,0:T(8,128)(2,1)}, u32[]{:S(2)}, u32[]{:S(2)}) collective-permute-start(bf16[128,1024]{1,0:T(8,128)(2,1)S(1)} %slice_bitcast_fusion.1), channel_id=1, source_target_pairs={{2,0},{3,1},{4,6},{5,7},{10,8},{11,9},{12,14},{13,15},{18,16},{19,... | collective-permute-start | bytes 786440 | tf_op jit(solution)/shard_map/ppermute | solution.py:142
  134.0 12.3 %collective-permute-start.15 = (bf16[128,1024]{1,0:T(8,128)(2,1)S(1)}, bf16[128,1024]{1,0:T(8,128)(2,1)S(1)}, u32[]{:S(2)}, u32[]{:S(2)}) collective-permute-start(bf16[128,1024]{1,0:T(8,128)(2,1)S(1)} %slice_bitcast_fusion.3), channel_id=1, source_target_pairs={{2,0},{3,1},{4,6},{5,7},{10,8},{11,9},{12,14},{13,15},{18,16},{19,... | collective-permute-start | bytes 786440 | tf_op jit(solution)/shard_map/ppermute | solution.py:142
  141.8 15.8 %collective-permute-start.22 = (bf16[256,1024]{1,0:T(8,128)(2,1)}, bf16[256,1024]{1,0:T(8,128)(2,1)}, u32[]{:S(2)}, u32[]{:S(2)}) collective-permute-start(bf16[256,1024]{1,0:T(8,128)(2,1)} %slice.323), channel_id=1, source_target_pairs={{0,1},{1,0},{2,3},{3,2},{4,5},{5,4},{6,7},{7,6},{8,9},{9,8},{10,11... | collective-permute-start | bytes 1572872 | tf_op jit(solution)/shard_map/ppermute | solution.py:142
  143.8 16.9 %collective-permute-start.30 = (f32[3,2,2,1024]{3,2,1,0:T(2,128)S(1)}, f32[3,2,2,1024]{3,2,1,0:T(2,128)S(1)}, u32[]{:S(2)}, u32[]{:S(2)}) collective-permute-start(f32[3,2,2,1024]{3,2,1,0:T(2,128)S(1)} %fusion.187), channel_id=1, source_target_pairs={{2,0},{3,1},{4,6},{5,7},{10,8},{11,9},{12,14},{13,15},{18,16},{19,... | collective-permute-start | bytes 147464 | tf_op jit(solution)/shard_map/ppermute | solution.py:142
  155.1 16.7 %collective-permute-start.21 = (bf16[256,1024]{1,0:T(8,128)(2,1)}, bf16[256,1024]{1,0:T(8,128)(2,1)S(1)}, u32[]{:S(2)}, u32[]{:S(2)}) collective-permute-start(bf16[256,1024]{1,0:T(8,128)(2,1)} %fusion.41), channel_id=1, source_target_pairs={{8,0},{16,8},{24,16},{9,1},{17,9},{25,17},{10,2},{18,10},{26,18},{... | collective-permute-start | bytes 1572872 | tf_op jit(solution)/shard_map/ppermute | solution.py:12
  159.2 12.6 %collective-permute-start.23 = (bf16[128,1024]{1,0:T(8,128)(2,1)S(1)}, bf16[128,1024]{1,0:T(8,128)(2,1)S(1)}, u32[]{:S(2)}, u32[]{:S(2)}) collective-permute-start(bf16[128,1024]{1,0:T(8,128)(2,1)S(1)} %slice.326), channel_id=1, source_target_pairs={{2,0},{3,1},{4,6},{5,7},{10,8},{11,9},{12,14},{13,15},{18,16},{19,... | collective-permute-start | bytes 786440 | tf_op jit(solution)/shard_map/ppermute | solution.py:142
  (28 other events, 203.9 us)

commit v2 on v0

--- a/solution.py
+++ b/solution.py
@@ -1,6 +1,10 @@
+import functools
+
 import jax
 import jax.numpy as jnp
 from jax import lax
+from jax.experimental import pallas as pl
+from jax.experimental.pallas import tpu as pltpu
 from jax.sharding import PartitionSpec as P
 
 
@@ -61,13 +65,7 @@
     return (prev, partial_value)
 
 
-def on_device(acts, cotan, proj_in, proj_out, block_mix, twiddle):
-    inputs = acts[0]
-    grad_out = cotan[0]
-    w_in = proj_in[0]
-    w_out = proj_out[0]
-    square_mix = block_mix[0]
-    twiddle_w = twiddle[0]
+def exchange_plan(inputs, grad_out, w_in, w_out, square_mix, twiddle_w):
     row_count, feature_count = inputs.shape
     seq_count = lax.axis_size("seq")
     segment_total = seq_count.bit_length() - 1
@@ -129,14 +127,470 @@
         d_projected, w_in, (((1,), (1,)), ((), ())), preferred_element_type=jnp.float32
     ).astype(jnp.bfloat16)
     handed = from_behind(input_grad, "pipe", -1)
-    return (
-        mixed_out[None],
-        handed[None],
-        win_share[None],
-        wout_share[None],
-        grad_square[None],
-        twiddle_grad[None],
-    )
+    return mixed_out, handed, win_share, wout_share, grad_square, twiddle_grad
+
+
+def chip_hops(hops):
+    return [(2 * source + core, 2 * target + core) for source, target in hops for core in (0, 1)]
+
+
+CORE_SWAP = [(index, index ^ 1) for index in range(8)]
+INWARD = chip_hops([(0, 1), (3, 2)])
+ACROSS = chip_hops([(1, 2), (2, 1)])
+OUTWARD = chip_hops([(1, 0), (2, 3)])
+
+
+def relay_back(outward):
+    return [
+        (8 * (section + 1) + source, 8 * section + target)
+        for section in range(lax.axis_size("pipe") - 1)
+        for source, target in (OUTWARD if outward else [(place, place) for place in range(2, 6)])
+    ]
+
+
+def hop(value, pairs):
+    return lax.ppermute(value, "seq", pairs)
+
+
+def dot(left, right):
+    return jnp.dot(left, right, preferred_element_type=jnp.float32)
+
+
+def dot_rows(left, right):
+    return lax.dot_general(
+        left, right, (((0,), (0,)), ((), ())), preferred_element_type=jnp.float32
+    )
+
+
+def dot_columns(left, right):
+    return lax.dot_general(
+        left, right, (((1,), (1,)), ((), ())), preferred_element_type=jnp.float32
+    )
+
+
+def narrow(value):
+    return value.astype(jnp.bfloat16)
+
+
+def wide(value):
+    return value.astype(jnp.float32)
+
+
+def coef_at(coef_ref, bit, side, term):
+    return coef_ref[pl.ds(4 * bit + 2 * side + term, 1), :]
+
+
+def cross(coef_ref, bit, side, own, other):
+    return coef_at(coef_ref, bit, side, 0) * own + coef_at(coef_ref, bit, side, 1) * other
+
+
+def cross_back(coef_ref, bit, side, own, other):
+    return coef_at(coef_ref, bit, side, 0) * own + coef_at(coef_ref, bit, 1 - side, 1) * other
+
+
+def pack_kernel(acts_ref, mix_ref, pack_ref):
+    rows, width = acts_ref.shape
+    depth = mix_ref.shape[1]
+    piece = rows * depth // width
+    pack_ref[pl.ds(0, rows), :] = acts_ref[...]
+    for i in range(rows // piece):
+        pack_ref[pl.ds(rows, piece), pl.ds(i * depth, depth)] = mix_ref[pl.ds(i * piece, piece), :]
+
+
+def unpack_mix(pack_ref, rows):
+    piece = pack_ref.shape[0] - rows
+    return jnp.concatenate(
+        [pack_ref[pl.ds(rows, piece), pl.ds(i * rows, rows)] for i in range(rows // piece)], axis=0
+    )
+
+
+def block_kernel(starts_ref, pack_ref, weight_ref, columns_ref, mixed_ref, seg0_ref, gate_ref, *value):
+    rows, width = gate_ref.shape
+    half, share = width // 2, width // 8
+    acts = pack_ref[pl.ds(0, rows), :]
+    mix = unpack_mix(pack_ref, rows)
+    for i in range(4):
+        product = narrow(dot(acts, weight_ref[:, pl.ds(i * half, half)]))
+        if i < 2:
+            seg0_ref[:, pl.ds(i * half, half)] = narrow(dot(mix, product))
+            if value:
+                value[0][:, pl.ds(i * half, half)] = product
+        else:
+            gate_ref[:, pl.ds((i - 2) * half, half)] = product
+    for j in range(4):
+        start = pl.multiple_of(starts_ref[j], share)
+        columns_ref[:, pl.ds(j * share, share)] = pack_ref[pl.ds(0, rows), pl.ds(start, share)]
+    mixed_ref[...] = narrow(dot(mix, columns_ref[...]))
+
+
+def d_hidden_kernel(weight_ref, *refs):
+    for cotan_ref, out_ref in zip(refs[: len(refs) // 2], refs[len(refs) // 2 :]):
+        out_ref[...] = narrow(dot_columns(cotan_ref[...], weight_ref[...]))
+
+
+def early_grads_kernel(*refs):
+    columns, d_gate_ref, hidden_ref, cotans = refs[0:4], refs[4], refs[5], refs[6:10]
+    given_ref, kept_ref = refs[10:12]
+    half = columns[0].shape[1] // 2
+    for part in range(2):
+        gate_total, out_total = 0.0, 0.0
+        cut = pl.ds(part * half, half)
+        for k in range(4):
+            gate_total += dot_rows(columns[k][:, cut], d_gate_ref[k])
+            out_total += dot_rows(hidden_ref[k, :, cut], cotans[k][...])
+        if part == 0:
+            given_ref[pl.ds(0, half), :] = narrow(gate_total)
+            given_ref[pl.ds(half, half), :] = narrow(out_total)
+        else:
+            kept_ref[pl.ds(0, half), :] = gate_total
+            kept_ref[pl.ds(half, half), :] = out_total
+
+
+def late_grads_kernel(*refs):
+    mixed, d_seg0_ref, given_ref, kept_ref = refs[0:4], refs[4], refs[5], refs[6]
+    half = given_ref.shape[0]
+    for part in range(2):
+        total = 0.0
+        for k in range(4):
+            total += dot_rows(mixed[k][:, pl.ds(part * half, half)], d_seg0_ref[k])
+        if part == 0:
+            given_ref[...] = narrow(total)
+        else:
+            kept_ref[...] = total
+
+
+def sums_kernel(kept_ref, got_ref, out_ref):
+    share = out_ref.shape[0] // (kept_ref.shape[0] // 256)
+    for i in range(kept_ref.shape[0] // (2 * share)):
+        there = pl.ds((2 * i + 1) * share, share)
+        out_ref[pl.ds(i * share, share), :] = narrow(kept_ref[there, :] + wide(got_ref[there, :]))
+
+
+def own_kernel(d_seg0_ref, d_gate_ref, weight_ref, *refs):
+    packs, values, d_acts, squares = refs[0:2], refs[2:4], refs[4:6], refs[6:8]
+    rows, width = values[0].shape
+    for k in range(2):
+        d_seg0 = d_seg0_ref[k]
+        d_value = narrow(dot_rows(unpack_mix(packs[k], rows), d_seg0))
+        d_acts[k][...] = narrow(
+            dot_columns(d_value, weight_ref[:, pl.ds(0, width)])
+            + dot_columns(d_gate_ref[k], weight_ref[:, pl.ds(width, width)])
+        )
+        squares[k][...] = dot_columns(d_seg0, values[k][...])
+
+
+def mixed_kernel(hidden_ref, weight_ref, *outs):
+    for k in range(2):
+        outs[k][...] = narrow(dot(hidden_ref[k], weight_ref[...]))
+
+
+def forward_kernel(starts_ref, coef_ref, *refs):
+    seg0 = refs[0:4]
+    swapped = refs[4:8]
+    gates = refs[8:12]
+    seg1_out, seg2_out, hidden_out, columns_out, held = refs[12:17]
+    share = coef_ref.shape[1] // 8
+    first = [cross(coef_ref, 0, 0, seg0[k][...], swapped[k][...]) for k in range(4)]
+    for k in range(2):
+        seg1_out[k] = first[k]
+    second = [cross(coef_ref, 1, k & 1, first[k], first[k ^ 1]) for k in range(4)]
+    for k in range(4):
+        seg2_out[k] = second[k]
+    for k in range(4):
+        hidden = cross(coef_ref, 2, k >> 1, second[k], second[k ^ 2]) * gates[k][...]
+        held[k] = hidden
+        if k < 2:
+            hidden_out[k] = hidden
+    for k in range(4):
+        for j in range(4):
+            start = pl.multiple_of(starts_ref[j], share)
+            columns_out[k, :, pl.ds(j * share, share)] = held[k, :, pl.ds(start, share)]
+
+
+def row_sums(value):
+    return dot(jnp.ones((8, value.shape[0]), value.dtype), value)
+
+
+def backward_kernel(coef_ref, *refs):
+    d_hidden = refs[0:4]
+    gates = refs[4:8]
+    seg1_ref, seg2_ref = refs[8:10]
+    d_gate_out, d_seg1_out, partial_out = refs[10:13]
+
+    @pl.when(pl.program_id(0) == 0)
+    def _():
+        partial_out[...] = jnp.zeros_like(partial_out)
+
+    third = []
+    for k in range(4):
+        grad = d_hidden[k][...]
+        d_gate_out[k] = grad * cross(coef_ref, 2, k >> 1, seg2_ref[k], seg2_ref[k ^ 2])
+        third.append(grad * gates[k][...])
+    for k in range(2):
+        partial_out[4] += row_sums(third[k] * seg2_ref[k])
+        partial_out[5] += row_sums(third[k] * seg2_ref[k ^ 2])
+    second = [cross_back(coef_ref, 2, k >> 1, third[k], third[k ^ 2]) for k in range(4)]
+    for k in range(2):
+        partial_out[2 * k] += row_sums(second[k] * seg1_ref[k])
+        partial_out[2 * k + 1] += row_sums(second[k] * seg1_ref[k ^ 1])
+    for k in range(4):
+        d_seg1_out[k] = cross_back(coef_ref, 1, k & 1, second[k], second[k ^ 1])
+
+
+def first_bit_kernel(coef_ref, *refs):
+    d_seg1_ref, d_swapped_ref = refs[0:2]
+    seg0 = refs[2:4]
+    swapped = refs[4:6]
+    d_seg0_out, partial_out = refs[6:8]
+
+    @pl.when(pl.program_id(0) == 0)
+    def _():
+        partial_out[...] = jnp.zeros_like(partial_out)
+
+    for k in range(4):
+        own, other = d_seg1_ref[k], d_swapped_ref[k]
+        d_seg0 = cross_back(coef_ref, 0, 0, own, other)
+        d_seg0_out[k] = d_seg0
+        if k < 2:
+            partial_out[0] += row_sums(own * seg0[k][...])
+            partial_out[1] += row_sums(own * swapped[k][...])
+
+
+TILE = 64
+
+
+def tile(columns, column_at=0, row_at=0):
+    return pl.BlockSpec((TILE, columns), lambda i: (i + row_at, column_at))
+
+
+def stacked(count, columns, row_at=0):
+    return pl.BlockSpec((count, TILE, columns), lambda i: (0, i + row_at, 0))
+
+
+def whole(*shape):
+    return pl.BlockSpec(shape, lambda i: (0,) * len(shape))
+
+
+def shape_of(kind, *shape):
+    return jax.ShapeDtypeStruct(shape, kind)
+
+
+def kernel_call(kernel, name, work=1, **settings):
+    return pl.pallas_call(
+        kernel,
+        cost_estimate=pl.CostEstimate(flops=work, bytes_accessed=1, transcendentals=0),
+        compiler_params=pltpu.CompilerParams(vmem_limit_bytes=16 * 2**20),
+        name=name,
+        **settings,
+    )
+
+
+def in_place(kernel, name, operands, *outs, work=1, scalars=0):
+    local = pl.BlockSpec(memory_space=pltpu.VMEM)
+    return kernel_call(
+        kernel,
+        name,
+        work,
+        in_specs=[pl.BlockSpec(memory_space=pltpu.SMEM)] * scalars
+        + [local] * (len(operands) - scalars),
+        out_specs=[local] * len(outs),
+        out_shape=list(outs),
+    )(*operands)
+
+
+def after(value, *earlier):
+    return lax.optimization_barrier((value, *earlier))[0]
+
+
+def relay_plan(inputs, grad_out, w_in, w_out, mix, twiddle_w):
+    rows, width = inputs.shape
+    share = width // 8
+    bf16, f32 = jnp.bfloat16, jnp.float32
+    place = lax.axis_index("seq")
+    chip, core = place // 2, place % 2
+    inner = (chip == 1) | (chip == 2)
+    flips = (core, chip & 1, chip >> 1)
+    scalar = pl.BlockSpec(memory_space=pltpu.SMEM)
+
+    starts = jnp.stack(
+        [
+            (2 * (chip ^ chip_bit) + (core ^ core_bit)) * share
+            for core_bit in (1, 0)
+            for chip_bit in (0, 1)
+        ]
+    ).astype(jnp.int32)
+
+    full, narrow_full = shape_of(bf16, rows, width), shape_of(bf16, rows, width // 2)
+    packed_rows = rows + mix.size // width
+    pack = kernel_call(pack_kernel, "pack", out_shape=shape_of(bf16, packed_rows, width))(
+        inputs, mix
+    )
+
+    def block(k, packed, work=1):
+        return in_place(
+            block_kernel,
+            f"block_{k}",
+            [starts, packed, w_in],
+            *([narrow_full] * 2 + [full] * (2 + (k < 2))),
+            work=work,
+            scalars=1,
+        )
+
+    outer_pack, across_pack = hop(pack, INWARD), hop(pack, ACROSS)
+    own = block(0, pack, 4 * rows * width * width)
+    (d_hidden_own,) = in_place(
+        d_hidden_kernel, "d_hidden", [w_out, grad_out], full, work=2 * rows * width * width
+    )
+    far_pack = hop(after(outer_pack, own[0], d_hidden_own), ACROSS)
+    outer_cotan = hop(after(grad_out, outer_pack), INWARD)
+    across_cotan = hop(after(grad_out, outer_pack), ACROSS)
+    far_cotan = hop(outer_cotan, ACROSS)
+    outer = block(1, outer_pack)
+    across = block(3, after(across_pack, outer[0]))
+    far = block(2, after(far_pack, outer_cotan, across[0]))
+
+    coefs = jnp.concatenate(
+        [
+            jnp.where(flips[bit] == 1, twiddle_w[bit][::-1], twiddle_w[bit]).reshape(4, width)
+            for bit in range(3)
+        ]
+        + [jnp.zeros((4, width), jnp.float32)]
+    ).astype(bf16)
+    blocks = [own, outer, far, across]
+    seg0 = [part[2] for part in blocks]
+    gates = [part[3] for part in blocks]
+    swapped = [hop(part, CORE_SWAP) for part in seg0]
+    seg1, seg2, hidden, hidden_columns = kernel_call(
+        forward_kernel,
+        "forward_segments",
+        grid=(rows // TILE,),
+        in_specs=[scalar, whole(16, width)] + [tile(width)] * 12,
+        out_specs=[
+            stacked(2, width),
+            stacked(4, width),
+            stacked(2, width),
+            stacked(4, width // 2),
+        ],
+        out_shape=[
+            shape_of(bf16, 2, rows, width),
+            shape_of(bf16, 4, rows, width),
+            shape_of(bf16, 2, rows, width),
+            shape_of(bf16, 4, rows, width // 2),
+        ],
+        scratch_shapes=[pltpu.VMEM((4, TILE, width), bf16)],
+    )(starts, coefs, *seg0, *swapped, *gates)
+    d_hidden_outer, d_hidden_across = in_place(
+        d_hidden_kernel,
+        "d_hidden",
+        [w_out, outer_cotan, after(across_cotan, hidden)],
+        full,
+        full,
+    )
+    own_mixed, outer_mixed = in_place(mixed_kernel, "mixed", [hidden, w_out], full, full)
+    sent_mixed = hop(outer_mixed, OUTWARD)
+
+    far_cotan = after(far_cotan, outer_mixed, d_hidden_outer)
+    (d_hidden_far,) = in_place(d_hidden_kernel, "d_hidden", [w_out, far_cotan], full)
+    d_hidden = [d_hidden_own, d_hidden_outer, d_hidden_far, d_hidden_across]
+    d_gate, d_seg1, later_part = kernel_call(
+        backward_kernel,
+        "backward_segments",
+        grid=(rows // TILE,),
+        in_specs=[whole(16, width)]
+        + [tile(width)] * 8
+        + [stacked(2, width), stacked(4, width)],
+        out_specs=[stacked(4, width), stacked(4, width), whole(6, 8, width)],
+        out_shape=[shape_of(bf16, 4, rows, width)] * 2 + [shape_of(f32, 6, 8, width)],
+    )(coefs, *d_hidden, *gates, seg1, seg2)
+    d_swapped = hop(d_seg1, CORE_SWAP)
+
+    early_given, early_kept = in_place(
+        early_grads_kernel,
+        "early_grads",
+        [part[0] for part in blocks]
+        + [d_gate, hidden_columns, grad_out, outer_cotan, far_cotan, across_cotan],
+        shape_of(bf16, 4 * share, width),
+        shape_of(f32, 4 * share, width),
+    )
+    early_got = hop(early_given, CORE_SWAP)
+    (early_sums,) = in_place(
+        sums_kernel, "early_sums", [early_kept, early_got], shape_of(bf16, 2 * share, width)
+    )
+    sent_early = hop(early_sums, OUTWARD)
+    d_seg0, first_part = kernel_call(
+        first_bit_kernel,
+        "first_segment_grad",
+        grid=(rows // TILE,),
+        in_specs=[whole(16, width)] + [stacked(4, width)] * 2 + [tile(width)] * 4,
+        out_specs=[stacked(4, width), whole(2, 8, width)],
+        out_shape=[shape_of(bf16, 4, rows, width), shape_of(f32, 2, 8, width)],
+    )(coefs, d_seg1, after(d_swapped, early_sums), *seg0[:2], *swapped[:2])
+    late_given, late_kept = in_place(
+        late_grads_kernel,
+        "late_grads",
+        [part[1] for part in blocks] + [d_seg0],
+        shape_of(bf16, 2 * share, width),
+        shape_of(f32, 2 * share, width),
+    )
+    late_got = hop(late_given, CORE_SWAP)
+    own_d_acts, outer_d_acts, own_square, outer_square = in_place(
+        own_kernel,
+        "own_grads",
+        [after(d_seg0, late_given), d_gate, w_in, pack, outer_pack, own[4], outer[4]],
+        full,
+        full,
+        shape_of(f32, rows, rows),
+        shape_of(f32, rows, rows),
+    )
+    (late_sums,) = in_place(
+        sums_kernel, "late_sums", [late_kept, late_got], shape_of(bf16, share, width)
+    )
+    sent_late = hop(late_sums, OUTWARD)
+    sent_square = hop(narrow(outer_square), OUTWARD)
+    own_handed = lax.ppermute(own_d_acts, ("pipe", "seq"), relay_back(False))
+    outer_handed = lax.ppermute(outer_d_acts, ("pipe", "seq"), relay_back(True))
+
+    def one_side(pair_terms, flip):
+        empty = jnp.zeros_like(pair_terms)
+        return jnp.where(
+            flip == 1, jnp.stack([empty, pair_terms]), jnp.stack([pair_terms, empty])
+        )
+
+    first_terms, later_terms = after(first_part[:, 0], late_sums), after(later_part[:, 0], late_sums)
+    both = later_terms[:4].reshape(2, 2, width)
+    terms = jnp.stack(
+        [
+            one_side(first_terms, flips[0]),
+            jnp.where(flips[1] == 1, both[::-1], both),
+            one_side(later_terms[4:], flips[2]),
+        ]
+    )
+    terms = terms + hop(terms, CORE_SWAP)
+    terms = terms + hop(terms, ACROSS)
+    twiddle_grad = jnp.where(inner, terms, hop(terms, OUTWARD))
+
+    mixed_out = jnp.where(inner, own_mixed, after(sent_mixed, late_sums))
+    handed = jnp.where(inner, own_handed, outer_handed)
+    grad_square = jnp.where(inner, own_square, wide(sent_square))
+    sent_early = wide(after(sent_early, twiddle_grad))
+    sent_late = wide(after(sent_late, twiddle_grad))
+
+    def share_of(kept, got, sent, at):
+        here = slice(2 * at * share, (2 * at + 1) * share)
+        mine = kept[here] + wide(got[here])
+        return jnp.where(inner, mine, sent[at * share : (at + 1) * share])
+
+    win_share = jnp.concatenate(
+        [share_of(late_kept, late_got, sent_late, 0), share_of(early_kept, early_got, sent_early, 0)],
+        axis=1,
+    )
+    wout_share = share_of(early_kept, early_got, sent_early, 1)
+    return mixed_out, handed, win_share, wout_share, grad_square, twiddle_grad
+
+
+def on_device(*arguments):
+    plan = relay_plan if lax.axis_size("seq") == 8 else exchange_plan
+    return tuple(result[None] for result in plan(*(part[0] for part in arguments)))
 
 
 def solution(mesh):

time: 246 us -> 142 us (0.58)
  blocking collectives: 83.4 us -> 0 us
  waiting for transfers between devices: 108 us -> 31.9 us
  Pallas kernels: 0 us -> 40.1 us
  local copies, waits for them, and re-layouts: 5.15 us -> 30.3 us
  matrix products: 22.4 us -> 0 us
  starting transfers between devices: 8.29 us -> 28 us
  between operations: 14.4 us -> 1.33 us
  other arithmetic: 2.01 us -> 8.77 us
    reduce_scatter x2 -> x0, waiting for transfers between devices: 93.1 us -> none  [the longest x1 48.7 us: on_device(): lax.psum_scatter(wout_term, 'seq', scatter_dimension=0, tiled=True)]
    all_to_all x3 -> x0, blocking collectives: 53.4 us -> none  [the longest x1 17.9 us: on_device(): lax.all_to_all(blocked.reshape(row_count, feature_count), 'seq', split_ax...]
    pallas_call x0 -> x17, Pallas kernels: none -> 40.1 us  [the longest x13 29.4 us: in_place(): kernel_call(kernel, name, work, in_specs=[pl.BlockSpec(memory_space=pltpu...]
    ppermute x1 -> x22, waiting for transfers between devices: 0.01 us -> 31.9 us  [the longest x20 26.1 us: hop(): return lax.ppermute(value, 'seq', pairs)]
    psum x1 -> x0, blocking collectives: 30 us -> none  [on_device(): twiddle_grad = lax.psum(jnp.stack(partials), 'seq')]
    ppermute x1 -> x22, starting transfers between devices: 3.34 us -> 28 us  [the longest x20 26 us: hop(): return lax.ppermute(value, 'seq', pairs)]
    unnamed x24 -> x113, local copies, waits for them, and re-layouts: 5.11 us -> 29.1 us
    dot_general x9 -> x0, matrix products: 22.4 us -> none  [the longest x1 4.51 us: on_device(): lax.dot_general(inputs, d_projected, (((0,), (0,)), ((), ())), preferred_...]
  transfers between devices with their start and end apart: 4 -> 22, of which waited for: 3 -> 6; matrix products, arithmetic and copies ran while one was open for 6% -> 6% of each run, Pallas kernels for 0% -> 22%
where the time goes in v2:
time: 142 us; the launch traced here: 140 us
  Pallas kernels  40.1 us (28%)
  waiting for transfers between devices  31.9 us (22%)
  local copies, waits for them, and re-layouts  30.3 us (21%)
  starting transfers between devices  28 us (20%)
  other arithmetic  8.77 us (6%)
    pallas_call x13, Pallas kernels, in_place(): kernel_call(kernel, name, work, in_specs=[pl.BlockSpec(memory_space=pltpu...  29.4 us
    unnamed x113, local copies, waits for them, and re-layouts  29.1 us
    ppermute x20, waiting for transfers between devices, hop(): return lax.ppermute(value, 'seq', pairs)  26.1 us
    ppermute x20, starting transfers between devices, hop(): return lax.ppermute(value, 'seq', pairs)  26 us
    ppermute x1, waiting for transfers between devices, relay_plan(): outer_handed = lax.ppermute(outer_d_acts, ('pipe', 'seq'), relay_back(True))  5.87 us
    broadcast_in_dim x5, other arithmetic, on_device(): result[None]  5.59 us
    pallas_call x1, Pallas kernels, relay_plan(): kernel_call(forward_kernel, 'forward_segments', grid=(rows // TILE,), in_...  4.39 us
    pallas_call x1, Pallas kernels, relay_plan(): kernel_call(first_bit_kernel, 'first_segment_grad', grid=(rows // TILE,),...  3.34 us
  transfers between devices with their start and end apart: 22, of which 6 were waited for; matrix products, arithmetic and copies ran while one was open for 6% of the time, Pallas kernels for 22%

profile of v2, /device:TPU:4, one launch (start us, length us, event | category | flops | bytes accessed | tf_op | source)
XLA Modules:
  0.0 140.4 jit_solution(4276982532275544953)
XLA Ops:
  2.6 3.5 %collective-permute-start = (bf16[320,1024]{1,0:T(8,128)(2,1)S(1)}, bf16[320,1024]{1,0:T(8,128)(2,1)S(1)}, u32[]{:S(2)}, u32[]{:S(2)}) collective-permute-start(bf16[320,1024]{1,0:T(8,128)(2,1)S(1)} %pack.1.pack_ref.refs_0_), channel_id=1, source_target_pairs={{0,2},{1,3},{6,4},{7,5},{8,10},{9,11},{14,12},{15,13},{16,18},{17,... | collective-permute-start | bytes 1966088 | tf_op jit(solution)/shard_map/ppermute | solution.py:152
  7.8 2.2 %copy-done = bf16[1,1024,2048]{2,1,0:T(8,128)(2,1)S(1)} copy-done((bf16[1,1024,2048]{2,1,0:T(8,128)(2,1)S(1)}, bf16[1,1024,2048]{2,1,0:T(8,128)(2,1)}, u32[]{:S(2)}) %copy-start) | copy-done | bytes 4194328
  10.0 2.5 %block_0.1 = (bf16[256,512]{1,0:T(8,128)(2,1)S(1)}, bf16[256,512]{1,0:T(8,128)(2,1)S(1)}, bf16[256,1024]{1,0:T(8,128)(2,1)}, bf16[256,1024]{1,0:T(8,128)(2,1)S(1)}, bf16[256,1024]{1,0:T(8,128)(2,1)S(1)}) custom-call(s32[4]{0:T(128)S(1)} %pad_add_fusion.starts_ref, bf16[320,1024]{1,0:T(8,128)(2,1)S(1)} %pack.1.pack_ref.refs_0_, bf16[1024,2048]{1,0:T(8,128)(2,1)S(1)} %bitcast.40), custom_call_target="tpu_custom_call" | custom-call | flops 1073741824 | bytes 1 | tf_op jit(solution)/shard_map/block_0/pallas_call | solution.py:390
  12.4 2.2 %d_hidden.3.refs_0_ = bf16[256,1024]{1,0:T(8,128)(2,1)S(1)} custom-call(bf16[1024,1024]{1,0:T(8,128)(2,1)S(1)} %bitcast.45, bf16[256,1024]{1,0:T(8,128)(2,1)} %bitcast.11.refs_0_.refs_6_), custom_call_target="tpu_custom_call" | custom-call | flops 536870912 | bytes 1 | tf_op jit(solution)/shard_map/d_hidden/pallas_call | solution.py:390
  15.5 4.6 %collective-permute-done.pack_ref.refs_1_ = bf16[320,1024]{1,0:T(8,128)(2,1)S(1)} collective-permute-done((bf16[320,1024]{1,0:T(8,128)(2,1)S(1)}, bf16[320,1024]{1,0:T(8,128)(2,1)S(1)}, u32[]{:S(2)}, u32[]{:S(2)}) %collective-permute-start) | collective-permute-done | bytes 655392 | tf_op jit(solution)/shard_map/ppermute | solution.py:152
  21.6 7.2 %collective-permute-start.2 = (bf16[256,1024]{1,0:T(8,128)(2,1)}, bf16[256,1024]{1,0:T(8,128)(2,1)}, u32[]{:S(2)}, u32[]{:S(2)}) collective-permute-start(bf16[256,1024]{1,0:T(8,128)(2,1)} %bitcast.11.refs_0_.refs_6_), channel_id=1, source_target_pairs={{0,2},{1,3},{6,4},{7,5},{8,10},{9,11},{14,12},{15,13},{16,18},{17,... | collective-permute-start | bytes 1572872 | tf_op jit(solution)/shard_map/ppermute | solution.py:152
  30.3 2.2 %copy-done.1 = bf16[1,1024,2048]{2,1,0:T(8,128)(2,1)S(1)} copy-done((bf16[1,1024,2048]{2,1,0:T(8,128)(2,1)S(1)}, bf16[1,1024,2048]{2,1,0:T(8,128)(2,1)}, u32[]{:S(2)}) %copy-start.1) | copy-done | bytes 4194328
  32.5 2.4 %block_1.1 = (bf16[256,512]{1,0:T(8,128)(2,1)S(1)}, bf16[256,512]{1,0:T(8,128)(2,1)S(1)}, bf16[256,1024]{1,0:T(8,128)(2,1)}, bf16[256,1024]{1,0:T(8,128)(2,1)S(1)}, bf16[256,1024]{1,0:T(8,128)(2,1)S(1)}) custom-call(s32[4]{0:T(128)S(1)} %pad_add_fusion.starts_ref, bf16[320,1024]{1,0:T(8,128)(2,1)S(1)} %collective-permute-done.pack_ref.refs_1_, ...), custom_call_target="tpu_custom_call" | custom-call | flops 1 | bytes 1 | tf_op jit(solution)/shard_map/block_1/pallas_call | solution.py:390
  38.5 3.0 %block_3.1 = (bf16[256,512]{1,0:T(8,128)(2,1)S(1)}, bf16[256,512]{1,0:T(8,128)(2,1)S(1)}, bf16[256,1024]{1,0:T(8,128)(2,1)}, bf16[256,1024]{1,0:T(8,128)(2,1)S(1)}) custom-call(s32[4]{0:T(128)S(1)} %pad_add_fusion.starts_ref, bf16[320,1024]{1,0:T(8,128)(2,1)} %collective-permute-done.3.pack_ref, bf16[1024,2048]{1,0:T(8,128)(2,1)S(1)} %bitcast.42), custom_call_target="tpu_custom_call" | custom-call | flops 1 | bytes 1 | tf_op jit(solution)/shard_map/block_3/pallas_call | solution.py:390
  45.3 3.0 %block_2.1 = (bf16[256,512]{1,0:T(8,128)(2,1)S(1)}, bf16[256,512]{1,0:T(8,128)(2,1)S(1)}, bf16[256,1024]{1,0:T(8,128)(2,1)}, bf16[256,1024]{1,0:T(8,128)(2,1)S(1)}) custom-call(s32[4]{0:T(128)S(1)} %pad_add_fusion.starts_ref, bf16[320,1024]{1,0:T(8,128)(2,1)} %collective-permute-done.1.pack_ref, bf16[1024,2048]{1,0:T(8,128)(2,1)S(1)} %bitcast.43), custom_call_target="tpu_custom_call" | custom-call | flops 1 | bytes 1 | tf_op jit(solution)/shard_map/block_2/pallas_call | solution.py:390
  51.3 1.6 %collective-permute-done.6.refs_6_ = bf16[256,1024]{1,0:T(8,128)(2,1)} collective-permute-done((bf16[256,1024]{1,0:T(8,128)(2,1)}, bf16[256,1024]{1,0:T(8,128)(2,1)}, u32[]{:S(2)}, u32[]{:S(2)}) %collective-permute-start.6) | collective-permute-done | bytes 524320 | tf_op jit(solution)/shard_map/ppermute | solution.py:152
  57.0 4.4 %forward_segments.1 = (bf16[2,256,1024]{2,1,0:T(8,128)(2,1)S(1)}, bf16[4,256,1024]{2,1,0:T(8,128)(2,1)S(1)}, bf16[2,256,1024]{2,1,0:T(8,128)(2,1)S(1)}, bf16[4,256,512]{2,1,0:T(8,128)(2,1)S(1)}) custom-call(s32[4]{0:T(128)S(1)} %pad_add_fusion.starts_ref, bf16[16,1024]{1,0:T(8,128)(2,1)S(1)} %maximum_maximum_fusion.coef_ref, ...), custom_call_target="tpu_custom_call" | custom-call | flops 1 | bytes 1 | tf_op jit(solution)/shard_map/forward_segments/pallas_call | solution.py:463
  62.7 2.8 %d_hidden.4 = (bf16[256,1024]{1,0:T(8,128)(2,1)S(1)}, bf16[256,1024]{1,0:T(8,128)(2,1)S(1)}) custom-call(bf16[1024,1024]{1,0:T(8,128)(2,1)S(1)} %bitcast.47, bf16[256,1024]{1,0:T(8,128)(2,1)} %collective-permute-done.2.refs_0_.refs_7_, bf16[256,1024]{1,0:T(8,128)(2,1)} %collective-permute-done.9.refs_1_.refs_9_), custom_call_target="tpu_custom_call" | custom-call | flops 1 | bytes 1 | tf_op jit(solution)/shard_map/d_hidden/pallas_call | solution.py:390
  65.6 1.9 %d_hidden.5.refs_2_ = bf16[256,1024]{1,0:T(8,128)(2,1)S(1)} custom-call(bf16[1024,1024]{1,0:T(8,128)(2,1)S(1)} %bitcast.48, bf16[256,1024]{1,0:T(8,128)(2,1)} %collective-permute-done.10.refs_0_.refs_8_), custom_call_target="tpu_custom_call" | custom-call | flops 1 | bytes 1 | tf_op jit(solution)/shard_map/d_hidden/pallas_call | solution.py:390
  67.7 2.8 %backward_segments.1 = (bf16[4,256,1024]{2,1,0:T(8,128)(2,1)S(1)}, bf16[4,256,1024]{2,1,0:T(8,128)(2,1)S(1)}, f32[6,8,1024]{2,1,0:T(8,128)S(1)}) custom-call(bf16[16,1024]{1,0:T(8,128)(2,1)S(1)} %maximum_maximum_fusion.coef_ref, bf16[256,1024]{1,0:T(8,128)(2,1)S(1)} %copy-done.26, bf16[256,1024]{1,0:T(8,128)(2,1)S(1)} %get-tuple-element.81.refs_1_, ...), custom_call_target="tpu_custom_call" | custom-call | flops 1 | bytes 1 | tf_op jit(solution)/shard_map/backward_segments/pallas_call | solution.py:495
  71.0 3.9 %early_grads.1 = (bf16[512,1024]{1,0:T(8,128)(2,1)S(1)}, f32[512,1024]{1,0:T(8,128)S(1)}) custom-call(bf16[256,512]{1,0:T(8,128)(2,1)S(1)} %copy-done.38, bf16[256,512]{1,0:T(8,128)(2,1)S(1)} %copy-done.44, bf16[256,512]{1,0:T(8,128)(2,1)S(1)} %copy-done.50, bf16[256,512]{1,0:T(8,128)(2,1)S(1)} %copy-done.48, ...), custom_call_target="tpu_custom_call" | custom-call | flops 1 | bytes 1 | tf_op jit(solution)/shard_map/early_grads/pallas_call | solution.py:390
  75.1 2.5 %collective-permute-done.12.got_ref = bf16[512,1024]{1,0:T(8,128)(2,1)S(1)} collective-permute-done((bf16[512,1024]{1,0:T(8,128)(2,1)S(1)}, bf16[512,1024]{1,0:T(8,128)(2,1)S(1)}, u32[]{:S(2)}, u32[]{:S(2)}) %collective-permute-start.12) | collective-permute-done | bytes 1048608 | tf_op jit(solution)/shard_map/ppermute | solution.py:152
  79.5 3.3 %first_segment_grad.1 = (bf16[4,256,1024]{2,1,0:T(8,128)(2,1)S(1)}, f32[2,8,1024]{2,1,0:T(8,128)S(1)}) custom-call(bf16[16,1024]{1,0:T(8,128)(2,1)S(1)} %maximum_maximum_fusion.coef_ref, bf16[4,256,1024]{2,1,0:T(8,128)(2,1)S(1)} %get-tuple-element.86.refs_0_, bf16[4,256,1024]{2,1,0:T(8,128)(2,1)S(1)} %collective-permute-done.11.refs_1_, ...), custom_call_target="tpu_custom_call" | custom-call | flops 1 | bytes 1 | tf_op jit(solution)/shard_map/first_segment_grad/pallas_call | solution.py:520
  90.5 2.2 %copy-done.2 = bf16[1,1024,2048]{2,1,0:T(8,128)(2,1)S(1)} copy-done((bf16[1,1024,2048]{2,1,0:T(8,128)(2,1)S(1)}, bf16[1,1024,2048]{2,1,0:T(8,128)(2,1)}, u32[]{:S(2)}) %copy-start.2) | copy-done | bytes 4194328
  96.4 3.7 %own_grads.1 = (bf16[256,1024]{1,0:T(8,128)(2,1)}, bf16[256,1024]{1,0:T(8,128)(2,1)}, f32[256,256]{1,0:T(8,128)S(1)}, f32[256,256]{1,0:T(8,128)S(1)}) custom-call(bf16[4,256,1024]{2,1,0:T(8,128)(2,1)S(1)} %copy-done.5, bf16[4,256,1024]{2,1,0:T(8,128)(2,1)S(1)} %get-tuple-element.88.refs_4_.d_gate_ref, bf16[1024,2048]{1,0:T(8,128)(2,1)S(1)} %bitcast.44, ...), custom_call_target="tpu_custom_call" | custom-call | flops 1 | bytes 1 | tf_op jit(solution)/shard_map/own_grads/pallas_call | solution.py:390
  104.8 12.9 %collective-permute-done.21 = bf16[256,256]{1,0:T(8,128)(2,1)S(1)} collective-permute-done((bf16[256,256]{1,0:T(8,128)(2,1)S(1)}, bf16[256,256]{1,0:T(8,128)(2,1)S(1)}, u32[]{:S(2)}, u32[]{:S(2)}) %collective-permute-start.21) | collective-permute-done | bytes 131104 | tf_op jit(solution)/shard_map/ppermute | solution.py:152
  120.5 1.9 %select_bitcast_fusion.1 = bf16[1,256,1024]{2,1,0:T(8,128)(2,1)} fusion(bf16[256,1024]{1,0:T(8,128)(2,1)S(1)} %copy-done.30, bf16[256,1024]{1,0:T(8,128)(2,1)} %collective-permute-done.8, pred[]{:T(512)S(6)} %or.3), kind=kLoop, calls=%fused_computation.6 | loop fusion | flops 262144 | bytes 1572865 | tf_op jit(solution)/shard_map/broadcast_in_dim | solution.py:593
  124.1 5.9 %collective-permute-done.15 = bf16[256,1024]{1,0:T(8,128)(2,1)S(1)} collective-permute-done((bf16[256,1024]{1,0:T(8,128)(2,1)}, bf16[256,1024]{1,0:T(8,128)(2,1)S(1)}, u32[]{:S(2)}, u32[]{:S(2)}) %collective-permute-start.15) | collective-permute-done | bytes 524320 | tf_op jit(solution)/shard_map/ppermute | solution.py:551
  130.8 4.3 %collective-permute-done.19 = f32[3,2,2,1024]{3,2,1,0:T(2,128)S(1)} collective-permute-done((f32[3,2,2,1024]{3,2,1,0:T(2,128)S(1)}, f32[3,2,2,1024]{3,2,1,0:T(2,128)S(1)}, u32[]{:S(2)}, u32[]{:S(2)}) %collective-permute-start.19) | collective-permute-done | bytes 49184 | tf_op jit(solution)/shard_map/ppermute | solution.py:152
  (181 shorter events, 51.9 us)
Async XLA Ops:
  2.6 17.5 %collective-permute-start = (bf16[320,1024]{1,0:T(8,128)(2,1)S(1)}, bf16[320,1024]{1,0:T(8,128)(2,1)S(1)}, u32[]{:S(2)}, u32[]{:S(2)}) collective-permute-start(bf16[320,1024]{1,0:T(8,128)(2,1)S(1)} %pack.1.pack_ref.refs_0_), channel_id=1, source_target_pairs={{0,2},{1,3},{6,4},{7,5},{8,10},{9,11},{14,12},{15,13},{16,18},{17,... | collective-permute-start | bytes 1966088 | tf_op jit(solution)/shard_map/ppermute | solution.py:152
  6.2 31.8 %collective-permute-start.3 = (bf16[320,1024]{1,0:T(8,128)(2,1)S(1)}, bf16[320,1024]{1,0:T(8,128)(2,1)}, u32[]{:S(2)}, u32[]{:S(2)}) collective-permute-start(bf16[320,1024]{1,0:T(8,128)(2,1)S(1)} %pack.1.pack_ref.refs_0_), channel_id=1, source_target_pairs={{2,4},{3,5},{4,2},{5,3},{10,12},{11,13},{12,10},{13,11},{18,20},{1... | collective-permute-start | bytes 1966088 | tf_op jit(solution)/shard_map/ppermute | solution.py:152
  12.4 16.4 %copy-start.55 = (f32[1,3,2,2,1024]{4,3,2,1,0:T(2,128)S(1)}, f32[1,3,2,2,1024]{4,3,2,1,0:T(2,128)}, u32[]{:S(2)}) copy-start(f32[1,3,2,2,1024]{4,3,2,1,0:T(2,128)} %param.11) | copy-start | bytes 147460
  20.1 23.7 %collective-permute-start.1 = (bf16[320,1024]{1,0:T(8,128)(2,1)S(1)}, bf16[320,1024]{1,0:T(8,128)(2,1)}, u32[]{:S(2)}, u32[]{:S(2)}) collective-permute-start(bf16[320,1024]{1,0:T(8,128)(2,1)S(1)} %collective-permute-done.pack_ref.refs_1_), channel_id=1, source_target_pairs={{2,4},{3,5},{4,2},{5,3},{10,12},{11,13},{12,10},{13,11},{18,20},{1... | collective-permute-start | bytes 1966088 | tf_op jit(solution)/shard_map/ppermute | solution.py:152
  21.6 22.2 %collective-permute-start.2 = (bf16[256,1024]{1,0:T(8,128)(2,1)}, bf16[256,1024]{1,0:T(8,128)(2,1)}, u32[]{:S(2)}, u32[]{:S(2)}) collective-permute-start(bf16[256,1024]{1,0:T(8,128)(2,1)} %bitcast.11.refs_0_.refs_6_), channel_id=1, source_target_pairs={{0,2},{1,3},{6,4},{7,5},{8,10},{9,11},{14,12},{15,13},{16,18},{17,... | collective-permute-start | bytes 1572872 | tf_op jit(solution)/shard_map/ppermute | solution.py:152
  28.8 21.7 %collective-permute-start.4 = (bf16[256,1024]{1,0:T(8,128)(2,1)}, bf16[256,1024]{1,0:T(8,128)(2,1)}, u32[]{:S(2)}, u32[]{:S(2)}) collective-permute-start(bf16[256,1024]{1,0:T(8,128)(2,1)} %get-tuple-element.58.refs_0_.refs_2_), channel_id=1, source_target_pairs={{0,1},{1,0},{2,3},{3,2},{4,5},{5,4},{6,7},{7,6},{8,9},{9,8},{10,11... | collective-permute-start | bytes 1572872 | tf_op jit(solution)/shard_map/ppermute | solution.py:152
  28.8 33.9 %collective-permute-start.9 = (bf16[256,1024]{1,0:T(8,128)(2,1)}, bf16[256,1024]{1,0:T(8,128)(2,1)}, u32[]{:S(2)}, u32[]{:S(2)}) collective-permute-start(bf16[256,1024]{1,0:T(8,128)(2,1)} %bitcast.11.refs_0_.refs_6_), channel_id=1, source_target_pairs={{2,4},{3,5},{4,2},{5,3},{10,12},{11,13},{12,10},{13,11},{18,20},{1... | collective-permute-start | bytes 1572872 | tf_op jit(solution)/shard_map/ppermute | solution.py:152
  38.0 13.3 %collective-permute-start.5 = (bf16[256,1024]{1,0:T(8,128)(2,1)}, bf16[256,1024]{1,0:T(8,128)(2,1)}, u32[]{:S(2)}, u32[]{:S(2)}) collective-permute-start(bf16[256,1024]{1,0:T(8,128)(2,1)} %get-tuple-element.59.refs_1_.refs_3_), channel_id=1, source_target_pairs={{0,1},{1,0},{2,3},{3,2},{4,5},{5,4},{6,7},{7,6},{8,9},{9,8},{10,11... | collective-permute-start | bytes 1572872 | tf_op jit(solution)/shard_map/ppermute | solution.py:152
  43.8 7.5 %collective-permute-start.7 = (bf16[256,1024]{1,0:T(8,128)(2,1)}, bf16[256,1024]{1,0:T(8,128)(2,1)}, u32[]{:S(2)}, u32[]{:S(2)}) collective-permute-start(bf16[256,1024]{1,0:T(8,128)(2,1)} %get-tuple-element.68.refs_3_), channel_id=1, source_target_pairs={{0,1},{1,0},{2,3},{3,2},{4,5},{5,4},{6,7},{7,6},{8,9},{9,8},{10,11... | collective-permute-start | bytes 1572872 | tf_op jit(solution)/shard_map/ppermute | solution.py:152
  43.8 21.8 %collective-permute-start.10 = (bf16[256,1024]{1,0:T(8,128)(2,1)}, bf16[256,1024]{1,0:T(8,128)(2,1)}, u32[]{:S(2)}, u32[]{:S(2)}) collective-permute-start(bf16[256,1024]{1,0:T(8,128)(2,1)} %collective-permute-done.2.refs_0_.refs_7_), channel_id=1, source_target_pairs={{2,4},{3,5},{4,2},{5,3},{10,12},{11,13},{12,10},{13,11},{18,20},{1... | collective-permute-start | bytes 1572872 | tf_op jit(solution)/shard_map/ppermute | solution.py:152
  50.5 2.4 %collective-permute-start.6 = (bf16[256,1024]{1,0:T(8,128)(2,1)}, bf16[256,1024]{1,0:T(8,128)(2,1)}, u32[]{:S(2)}, u32[]{:S(2)}) collective-permute-start(bf16[256,1024]{1,0:T(8,128)(2,1)} %get-tuple-element.67.refs_2_), channel_id=1, source_target_pairs={{0,1},{1,0},{2,3},{3,2},{4,5},{5,4},{6,7},{7,6},{8,9},{9,8},{10,11... | collective-permute-start | bytes 1572872 | tf_op jit(solution)/shard_map/ppermute | solution.py:152
  70.6 8.9 %collective-permute-start.11 = (bf16[4,256,1024]{2,1,0:T(8,128)(2,1)S(1)}, bf16[4,256,1024]{2,1,0:T(8,128)(2,1)S(1)}, u32[]{:S(2)}, u32[]{:S(2)}) collective-permute-start(bf16[4,256,1024]{2,1,0:T(8,128)(2,1)S(1)} %get-tuple-element.86.refs_0_), channel_id=1, source_target_pairs={{0,1},{1,0},{2,3},{3,2},{4,5},{5,4},{6,7},{7,6},{8,9},{9,8},{10,11... | collective-permute-start | bytes 6291464 | tf_op jit(solution)/shard_map/ppermute | solution.py:152
  74.9 2.7 %collective-permute-start.12 = (bf16[512,1024]{1,0:T(8,128)(2,1)S(1)}, bf16[512,1024]{1,0:T(8,128)(2,1)S(1)}, u32[]{:S(2)}, u32[]{:S(2)}) collective-permute-start(bf16[512,1024]{1,0:T(8,128)(2,1)S(1)} %get-tuple-element.91), channel_id=1, source_target_pairs={{0,1},{1,0},{2,3},{3,2},{4,5},{5,4},{6,7},{7,6},{8,9},{9,8},{10,11... | collective-permute-start | bytes 3145736 | tf_op jit(solution)/shard_map/ppermute | solution.py:152
  86.7 15.5 %collective-permute-start.13 = (bf16[256,1024]{1,0:T(8,128)(2,1)}, bf16[256,1024]{1,0:T(8,128)(2,1)}, u32[]{:S(2)}, u32[]{:S(2)}) collective-permute-start(bf16[256,1024]{1,0:T(8,128)(2,1)} %get-tuple-element.95), channel_id=1, source_target_pairs={{0,1},{1,0},{2,3},{3,2},{4,5},{5,4},{6,7},{7,6},{8,9},{9,8},{10,11... | collective-permute-start | bytes 1572872 | tf_op jit(solution)/shard_map/ppermute | solution.py:152
  86.9 31.6 %collective-permute-start.8 = (bf16[256,1024]{1,0:T(8,128)(2,1)}, bf16[256,1024]{1,0:T(8,128)(2,1)}, u32[]{:S(2)}, u32[]{:S(2)}) collective-permute-start(bf16[256,1024]{1,0:T(8,128)(2,1)} %copy-done.54), channel_id=1, source_target_pairs={{2,0},{3,1},{4,6},{5,7},{10,8},{11,9},{12,14},{13,15},{18,16},{19,... | collective-permute-start | bytes 1572872 | tf_op jit(solution)/shard_map/ppermute | solution.py:152
  89.2 46.5 %collective-permute-start.20 = (bf16[256,1024]{1,0:T(8,128)(2,1)}, bf16[256,1024]{1,0:T(8,128)(2,1)}, u32[]{:S(2)}, u32[]{:S(2)}) collective-permute-start(bf16[256,1024]{1,0:T(8,128)(2,1)} %copy-done.27), channel_id=1, source_target_pairs={{2,0},{3,1},{4,6},{5,7},{10,8},{11,9},{12,14},{13,15},{18,16},{19,... | collective-permute-start | bytes 1572872 | tf_op jit(solution)/shard_map/ppermute | solution.py:152
  100.1 20.4 %copy-start.30 = (bf16[256,1024]{1,0:T(8,128)(2,1)S(1)}, bf16[256,1024]{1,0:T(8,128)(2,1)}, u32[]{:S(2)}) copy-start(bf16[256,1024]{1,0:T(8,128)(2,1)} %copy-done.29) | copy-start | bytes 1572868
  100.1 17.6 %collective-permute-start.21 = (bf16[256,256]{1,0:T(8,128)(2,1)S(1)}, bf16[256,256]{1,0:T(8,128)(2,1)S(1)}, u32[]{:S(2)}, u32[]{:S(2)}) collective-permute-start(bf16[256,256]{1,0:T(8,128)(2,1)S(1)} %convert_element_type.27), channel_id=1, source_target_pairs={{2,0},{3,1},{4,6},{5,7},{10,8},{11,9},{12,14},{13,15},{18,16},{19,... | collective-permute-start | bytes 393224 | tf_op jit(solution)/shard_map/ppermute | solution.py:152
  101.6 22.5 %collective-permute-start.14 = (bf16[256,1024]{1,0:T(8,128)(2,1)}, bf16[256,1024]{1,0:T(8,128)(2,1)S(1)}, u32[]{:S(2)}, u32[]{:S(2)}) collective-permute-start(bf16[256,1024]{1,0:T(8,128)(2,1)} %get-tuple-element.100), channel_id=1, source_target_pairs={{10,2},{11,3},{12,4},{13,5},{18,10},{19,11},{20,12},{21,13},{26,18... | collective-permute-start | bytes 1572872 | tf_op jit(solution)/shard_map/ppermute | solution.py:550
  102.3 27.6 %collective-permute-start.15 = (bf16[256,1024]{1,0:T(8,128)(2,1)}, bf16[256,1024]{1,0:T(8,128)(2,1)S(1)}, u32[]{:S(2)}, u32[]{:S(2)}) collective-permute-start(bf16[256,1024]{1,0:T(8,128)(2,1)} %get-tuple-element.101), channel_id=1, source_target_pairs={{10,0},{11,1},{12,6},{13,7},{18,8},{19,9},{20,14},{21,15},{26,16},... | collective-permute-start | bytes 1572872 | tf_op jit(solution)/shard_map/ppermute | solution.py:551
  117.8 2.0 %collective-permute-start.17 = (f32[3,2,2,1024]{3,2,1,0:T(2,128)S(1)}, f32[3,2,2,1024]{3,2,1,0:T(2,128)S(1)}, u32[]{:S(2)}, u32[]{:S(2)}) collective-permute-start(f32[3,2,2,1024]{3,2,1,0:T(2,128)S(1)} %pad_maximum_fusion), channel_id=1, source_target_pairs={{0,1},{1,0},{2,3},{3,2},{4,5},{5,4},{6,7},{7,6},{8,9},{9,8},{10,11... | collective-permute-start | bytes 147464 | tf_op jit(solution)/shard_map/ppermute | solution.py:152
  118.5 19.5 %collective-permute-start.16 = (bf16[128,1024]{1,0:T(8,128)(2,1)S(1)}, bf16[128,1024]{1,0:T(8,128)(2,1)S(1)}, u32[]{:S(2)}, u32[]{:S(2)}) collective-permute-start(bf16[128,1024]{1,0:T(8,128)(2,1)S(1)} %late_sums.1), channel_id=1, source_target_pairs={{2,0},{3,1},{4,6},{5,7},{10,8},{11,9},{12,14},{13,15},{18,16},{19,... | collective-permute-start | bytes 786440 | tf_op jit(solution)/shard_map/ppermute | solution.py:152
  119.9 2.6 %collective-permute-start.18 = (f32[3,2,2,1024]{3,2,1,0:T(2,128)S(1)}, f32[3,2,2,1024]{3,2,1,0:T(2,128)S(1)}, u32[]{:S(2)}, u32[]{:S(2)}) collective-permute-start(f32[3,2,2,1024]{3,2,1,0:T(2,128)S(1)} %fusion.5), channel_id=1, source_target_pairs={{2,4},{3,5},{4,2},{5,3},{10,12},{11,13},{12,10},{13,11},{18,20},{1... | collective-permute-start | bytes 147464 | tf_op jit(solution)/shard_map/ppermute | solution.py:152
  122.5 12.6 %collective-permute-start.19 = (f32[3,2,2,1024]{3,2,1,0:T(2,128)S(1)}, f32[3,2,2,1024]{3,2,1,0:T(2,128)S(1)}, u32[]{:S(2)}, u32[]{:S(2)}) collective-permute-start(f32[3,2,2,1024]{3,2,1,0:T(2,128)S(1)} %fusion.6), channel_id=1, source_target_pairs={{2,0},{3,1},{4,6},{5,7},{10,8},{11,9},{12,14},{13,15},{18,16},{19,... | collective-permute-start | bytes 147464 | tf_op jit(solution)/shard_map/ppermute | solution.py:152
  (54 other events, 168.3 us)

commit v3 on v2

--- a/solution.py
+++ b/solution.py
@@ -204,15 +204,20 @@
     )
 
 
-def block_kernel(starts_ref, pack_ref, weight_ref, columns_ref, mixed_ref, seg0_ref, gate_ref, *value):
+def block_kernel(starts_ref, pack_ref, weight_ref, columns_ref, mixed_ref, gate_ref, *refs):
     rows, width = gate_ref.shape
+    seg0, value = (refs[:2], ()) if refs[0].shape[1] < width else (refs[:1], refs[1:])
     half, share = width // 2, width // 8
     acts = pack_ref[pl.ds(0, rows), :]
     mix = unpack_mix(pack_ref, rows)
     for i in range(4):
         product = narrow(dot(acts, weight_ref[:, pl.ds(i * half, half)]))
         if i < 2:
-            seg0_ref[:, pl.ds(i * half, half)] = narrow(dot(mix, product))
+            segment = narrow(dot(mix, product))
+            if len(seg0) == 2:
+                seg0[i][...] = segment
+            else:
+                seg0[0][:, pl.ds(i * half, half)] = segment
             if value:
                 value[0][:, pl.ds(i * half, half)] = product
         else:
@@ -230,53 +235,61 @@
 
 def early_grads_kernel(*refs):
     columns, d_gate_ref, hidden_ref, cotans = refs[0:4], refs[4], refs[5], refs[6:10]
-    given_ref, kept_ref = refs[10:12]
-    half = columns[0].shape[1] // 2
-    for part in range(2):
-        gate_total, out_total = 0.0, 0.0
-        cut = pl.ds(part * half, half)
-        for k in range(4):
-            gate_total += dot_rows(columns[k][:, cut], d_gate_ref[k])
-            out_total += dot_rows(hidden_ref[k, :, cut], cotans[k][...])
-        if part == 0:
-            given_ref[pl.ds(0, half), :] = narrow(gate_total)
-            given_ref[pl.ds(half, half), :] = narrow(out_total)
-        else:
-            kept_ref[pl.ds(0, half), :] = gate_total
-            kept_ref[pl.ds(half, half), :] = out_total
-
-
-def late_grads_kernel(*refs):
-    mixed, d_seg0_ref, given_ref, kept_ref = refs[0:4], refs[4], refs[5], refs[6]
-    half = given_ref.shape[0]
+    given_refs, kept_ref = refs[10:14], refs[14]
+    half = kept_ref.shape[0] // 2
+    d_gates = [d_gate_ref.at[k] for k in range(4)]
+    split_grad(columns, d_gates, given_refs[0:2], kept_ref.at[pl.ds(0, half), :])
+    hiddens = [hidden_ref.at[k] for k in range(4)]
+    split_grad(hiddens, cotans, given_refs[2:4], kept_ref.at[pl.ds(half, half), :])
+
+
+def split_grad(lefts, rights, given_refs, kept_ref):
+    half = kept_ref.shape[0]
     for part in range(2):
         total = 0.0
-        for k in range(4):
-            total += dot_rows(mixed[k][:, pl.ds(part * half, half)], d_seg0_ref[k])
+        for left, right in zip(lefts, rights):
+            total += dot_rows(left[:, pl.ds(part * half, half)], right[...])
         if part == 0:
-            given_ref[...] = narrow(total)
+            for i, ref in enumerate(given_refs):
+                size = ref.shape[0]
+                ref[...] = narrow(total[i * size : (i + 1) * size])
         else:
             kept_ref[...] = total
 
 
-def sums_kernel(kept_ref, got_ref, out_ref):
-    share = out_ref.shape[0] // (kept_ref.shape[0] // 256)
-    for i in range(kept_ref.shape[0] // (2 * share)):
-        there = pl.ds((2 * i + 1) * share, share)
-        out_ref[pl.ds(i * share, share), :] = narrow(kept_ref[there, :] + wide(got_ref[there, :]))
+def value_grads_kernel(d_seg0_ref, *refs):
+    values, given_refs, kept_ref = refs[4:6], refs[6:8], refs[8]
+    split_grad(refs[0:4], [d_seg0_ref.at[k] for k in range(4)], given_refs, kept_ref)
+    for k in range(2):
+        refs[9 + k][...] = dot_columns(d_seg0_ref[k], values[k][...])
+
+
+def sums_kernel(kept_ref, *refs):
+    out_ref = refs[-1]
+    share = kept_ref.shape[1] // 8
+    terms = kept_ref.shape[0] // (2 * share)
+    got, extra = refs[: 2 * terms], refs[2 * terms : -1]
+    for i in range(terms):
+        there = kept_ref[pl.ds((2 * i + 1) * share, share), :]
+        out_ref[pl.ds(i * share, share), :] = narrow(there + wide(got[2 * i + 1][...]))
+    for ref in extra:
+        depth = ref.shape[1]
+        piece = out_ref.shape[0] - terms * share
+        for i in range(ref.shape[0] // piece):
+            out_ref[pl.ds(terms * share, piece), pl.ds(i * depth, depth)] = narrow(
+                ref[pl.ds(i * piece, piece), :]
+            )
 
 
 def own_kernel(d_seg0_ref, d_gate_ref, weight_ref, *refs):
-    packs, values, d_acts, squares = refs[0:2], refs[2:4], refs[4:6], refs[6:8]
-    rows, width = values[0].shape
+    packs, d_acts = refs[0:2], refs[2:4]
+    rows, width = d_acts[0].shape
     for k in range(2):
-        d_seg0 = d_seg0_ref[k]
-        d_value = narrow(dot_rows(unpack_mix(packs[k], rows), d_seg0))
+        d_value = narrow(dot_rows(unpack_mix(packs[k], rows), d_seg0_ref[k]))
         d_acts[k][...] = narrow(
             dot_columns(d_value, weight_ref[:, pl.ds(0, width)])
             + dot_columns(d_gate_ref[k], weight_ref[:, pl.ds(width, width)])
         )
-        squares[k][...] = dot_columns(d_seg0, values[k][...])
 
 
 def mixed_kernel(hidden_ref, weight_ref, *outs):
@@ -284,13 +297,17 @@
         outs[k][...] = narrow(dot(hidden_ref[k], weight_ref[...]))
 
 
+def joined_far(refs):
+    far = jnp.concatenate([refs[3][...], refs[4][...]], axis=1)
+    return [refs[0][...], refs[1][...], far, refs[2][...]]
+
+
 def forward_kernel(starts_ref, coef_ref, *refs):
-    seg0 = refs[0:4]
-    swapped = refs[4:8]
-    gates = refs[8:12]
-    seg1_out, seg2_out, hidden_out, columns_out, held = refs[12:17]
+    seg0, swapped = joined_far(refs[0:5]), joined_far(refs[5:10])
+    gates = refs[10:14]
+    seg1_out, seg2_out, hidden_out, columns_out, held = refs[14:19]
     share = coef_ref.shape[1] // 8
-    first = [cross(coef_ref, 0, 0, seg0[k][...], swapped[k][...]) for k in range(4)]
+    first = [cross(coef_ref, 0, 0, seg0[k], swapped[k]) for k in range(4)]
     for k in range(2):
         seg1_out[k] = first[k]
     second = [cross(coef_ref, 1, k & 1, first[k], first[k ^ 1]) for k in range(4)]
@@ -307,15 +324,17 @@
             columns_out[k, :, pl.ds(j * share, share)] = held[k, :, pl.ds(start, share)]
 
 
-def row_sums(value):
-    return dot(jnp.ones((8, value.shape[0]), value.dtype), value)
+def row_sums(value, row):
+    shape = (8, value.shape[0])
+    chosen = lax.broadcasted_iota(jnp.int32, shape, 0) == row
+    return dot(jnp.where(chosen, 1.0, 0.0).astype(value.dtype), value)
 
 
 def backward_kernel(coef_ref, *refs):
     d_hidden = refs[0:4]
     gates = refs[4:8]
     seg1_ref, seg2_ref = refs[8:10]
-    d_gate_out, d_seg1_out, partial_out = refs[10:13]
+    d_gate_out, d_seg1_out, partial_out = refs[10], refs[11:15], refs[15]
 
     @pl.when(pl.program_id(0) == 0)
     def _():
@@ -327,33 +346,33 @@
         d_gate_out[k] = grad * cross(coef_ref, 2, k >> 1, seg2_ref[k], seg2_ref[k ^ 2])
         third.append(grad * gates[k][...])
     for k in range(2):
-        partial_out[4] += row_sums(third[k] * seg2_ref[k])
-        partial_out[5] += row_sums(third[k] * seg2_ref[k ^ 2])
+        partial_out[...] += row_sums(third[k] * seg2_ref[k], 4)
+        partial_out[...] += row_sums(third[k] * seg2_ref[k ^ 2], 5)
     second = [cross_back(coef_ref, 2, k >> 1, third[k], third[k ^ 2]) for k in range(4)]
     for k in range(2):
-        partial_out[2 * k] += row_sums(second[k] * seg1_ref[k])
-        partial_out[2 * k + 1] += row_sums(second[k] * seg1_ref[k ^ 1])
+        partial_out[...] += row_sums(second[k] * seg1_ref[k], 2 * k)
+        partial_out[...] += row_sums(second[k] * seg1_ref[k ^ 1], 2 * k + 1)
     for k in range(4):
-        d_seg1_out[k] = cross_back(coef_ref, 1, k & 1, second[k], second[k ^ 1])
+        d_seg1_out[k][...] = cross_back(coef_ref, 1, k & 1, second[k], second[k ^ 1])
 
 
 def first_bit_kernel(coef_ref, *refs):
-    d_seg1_ref, d_swapped_ref = refs[0:2]
-    seg0 = refs[2:4]
-    swapped = refs[4:6]
-    d_seg0_out, partial_out = refs[6:8]
+    d_seg1, d_swapped = refs[0:4], refs[4:8]
+    seg0 = refs[8:10]
+    swapped = refs[10:12]
+    d_seg0_out, partial_out = refs[12:14]
 
     @pl.when(pl.program_id(0) == 0)
     def _():
         partial_out[...] = jnp.zeros_like(partial_out)
 
     for k in range(4):
-        own, other = d_seg1_ref[k], d_swapped_ref[k]
+        own, other = d_seg1[k][...], d_swapped[k][...]
         d_seg0 = cross_back(coef_ref, 0, 0, own, other)
         d_seg0_out[k] = d_seg0
         if k < 2:
-            partial_out[0] += row_sums(own * seg0[k][...])
-            partial_out[1] += row_sums(own * swapped[k][...])
+            partial_out[...] += row_sums(own * seg0[k][...], 0)
+            partial_out[...] += row_sums(own * swapped[k][...], 1)
 
 
 TILE = 64
@@ -375,22 +394,27 @@
     return jax.ShapeDtypeStruct(shape, kind)
 
 
-def kernel_call(kernel, name, work=1, **settings):
+def in_hbm(kind, *shape):
+    return pltpu.HBM(shape, kind)
+
+
+def kernel_call(kernel, name, work=1, room=16, **settings):
     return pl.pallas_call(
         kernel,
         cost_estimate=pl.CostEstimate(flops=work, bytes_accessed=1, transcendentals=0),
-        compiler_params=pltpu.CompilerParams(vmem_limit_bytes=16 * 2**20),
+        compiler_params=pltpu.CompilerParams(vmem_limit_bytes=room * 2**20),
         name=name,
         **settings,
     )
 
 
-def in_place(kernel, name, operands, *outs, work=1, scalars=0):
+def in_place(kernel, name, operands, *outs, work=1, scalars=0, room=16):
     local = pl.BlockSpec(memory_space=pltpu.VMEM)
     return kernel_call(
         kernel,
         name,
         work,
+        room,
         in_specs=[pl.BlockSpec(memory_space=pltpu.SMEM)] * scalars
         + [local] * (len(operands) - scalars),
         out_specs=[local] * len(outs),
@@ -420,10 +444,11 @@
         ]
     ).astype(jnp.int32)
 
-    full, narrow_full = shape_of(bf16, rows, width), shape_of(bf16, rows, width // 2)
+    full, full_hbm = shape_of(bf16, rows, width), in_hbm(bf16, rows, width)
+    narrow_hbm = in_hbm(bf16, rows, width // 2)
     packed_rows = rows + mix.size // width
-    pack = kernel_call(pack_kernel, "pack", out_shape=shape_of(bf16, packed_rows, width))(
-        inputs, mix
+    (pack,) = in_place(
+        pack_kernel, "pack", [inputs, mix], in_hbm(bf16, packed_rows, width), room=60
     )
 
     def block(k, packed, work=1):
@@ -431,7 +456,8 @@
             block_kernel,
             f"block_{k}",
             [starts, packed, w_in],
-            *([narrow_full] * 2 + [full] * (2 + (k < 2))),
+            *([narrow_hbm] * 2 + [full_hbm]),
+            *([narrow_hbm] * 2 if k == 2 else [full_hbm] * (1 + (k < 2))),
             work=work,
             scalars=1,
         )
@@ -457,14 +483,17 @@
         + [jnp.zeros((4, width), jnp.float32)]
     ).astype(bf16)
     blocks = [own, outer, far, across]
-    seg0 = [part[2] for part in blocks]
-    gates = [part[3] for part in blocks]
+    gates = [part[2] for part in blocks]
+    seg0 = [own[3], outer[3], across[3], far[3], far[4]]
     swapped = [hop(part, CORE_SWAP) for part in seg0]
     seg1, seg2, hidden, hidden_columns = kernel_call(
         forward_kernel,
         "forward_segments",
+        room=60,
         grid=(rows // TILE,),
-        in_specs=[scalar, whole(16, width)] + [tile(width)] * 12,
+        in_specs=[scalar, whole(16, width)]
+        + ([tile(width)] * 3 + [tile(width // 2)] * 2) * 2
+        + [tile(width)] * 4,
         out_specs=[
             stacked(2, width),
             stacked(4, width),
@@ -478,77 +507,81 @@
             shape_of(bf16, 4, rows, width // 2),
         ],
         scratch_shapes=[pltpu.VMEM((4, TILE, width), bf16)],
-    )(starts, coefs, *seg0, *swapped, *gates)
+    )(starts, coefs, *seg0, after(swapped[0], across_cotan), *swapped[1:], *gates)
+    own_mixed, outer_mixed = in_place(
+        mixed_kernel, "mixed", [hidden, w_out], full, full
+    )
+    sent_mixed = hop(outer_mixed, OUTWARD)
+
     d_hidden_outer, d_hidden_across = in_place(
         d_hidden_kernel,
         "d_hidden",
-        [w_out, outer_cotan, after(across_cotan, hidden)],
-        full,
-        full,
-    )
-    own_mixed, outer_mixed = in_place(mixed_kernel, "mixed", [hidden, w_out], full, full)
-    sent_mixed = hop(outer_mixed, OUTWARD)
-
-    far_cotan = after(far_cotan, outer_mixed, d_hidden_outer)
-    (d_hidden_far,) = in_place(d_hidden_kernel, "d_hidden", [w_out, far_cotan], full)
+        [w_out, after(outer_cotan, outer_mixed), across_cotan],
+        *[full] * 2,
+    )
+    (d_hidden_far,) = in_place(
+        d_hidden_kernel, "d_hidden", [w_out, after(far_cotan, d_hidden_outer)], full
+    )
     d_hidden = [d_hidden_own, d_hidden_outer, d_hidden_far, d_hidden_across]
-    d_gate, d_seg1, later_part = kernel_call(
+    d_gate, *d_seg1, later_part = kernel_call(
         backward_kernel,
         "backward_segments",
         grid=(rows // TILE,),
         in_specs=[whole(16, width)]
         + [tile(width)] * 8
         + [stacked(2, width), stacked(4, width)],
-        out_specs=[stacked(4, width), stacked(4, width), whole(6, 8, width)],
-        out_shape=[shape_of(bf16, 4, rows, width)] * 2 + [shape_of(f32, 6, 8, width)],
+        out_specs=[stacked(4, width)] + [tile(width)] * 4 + [whole(8, width)],
+        out_shape=[shape_of(bf16, 4, rows, width)] + [full] * 4 + [shape_of(f32, 8, width)],
     )(coefs, *d_hidden, *gates, seg1, seg2)
-    d_swapped = hop(d_seg1, CORE_SWAP)
-
-    early_given, early_kept = in_place(
+    d_swapped = [hop(part, CORE_SWAP) for part in d_seg1]
+
+    *early_given, early_kept = in_place(
         early_grads_kernel,
         "early_grads",
         [part[0] for part in blocks]
         + [d_gate, hidden_columns, grad_out, outer_cotan, far_cotan, across_cotan],
-        shape_of(bf16, 4 * share, width),
+        *[shape_of(bf16, share, width)] * 4,
         shape_of(f32, 4 * share, width),
     )
-    early_got = hop(early_given, CORE_SWAP)
+    early_got = [hop(part, CORE_SWAP) for part in early_given]
     (early_sums,) = in_place(
-        sums_kernel, "early_sums", [early_kept, early_got], shape_of(bf16, 2 * share, width)
+        sums_kernel, "early_sums", [after(early_kept, sent_mixed, *d_swapped), *early_got], shape_of(bf16, 2 * share, width)
     )
     sent_early = hop(early_sums, OUTWARD)
     d_seg0, first_part = kernel_call(
         first_bit_kernel,
         "first_segment_grad",
         grid=(rows // TILE,),
-        in_specs=[whole(16, width)] + [stacked(4, width)] * 2 + [tile(width)] * 4,
-        out_specs=[stacked(4, width), whole(2, 8, width)],
-        out_shape=[shape_of(bf16, 4, rows, width), shape_of(f32, 2, 8, width)],
-    )(coefs, d_seg1, after(d_swapped, early_sums), *seg0[:2], *swapped[:2])
-    late_given, late_kept = in_place(
-        late_grads_kernel,
-        "late_grads",
-        [part[1] for part in blocks] + [d_seg0],
-        shape_of(bf16, 2 * share, width),
-        shape_of(f32, 2 * share, width),
-    )
-    late_got = hop(late_given, CORE_SWAP)
-    own_d_acts, outer_d_acts, own_square, outer_square = in_place(
+        in_specs=[whole(16, width)] + [tile(width)] * 12,
+        out_specs=[stacked(4, width), whole(8, width)],
+        out_shape=[shape_of(bf16, 4, rows, width), shape_of(f32, 8, width)],
+    )(coefs, *d_seg1, after(d_swapped[0], early_sums), *d_swapped[1:], *seg0[:2], *swapped[:2])
+    *late_given, late_kept, own_square, outer_square = in_place(
+        value_grads_kernel,
+        "value_grads",
+        [d_seg0] + [part[1] for part in blocks] + [own[4], outer[4]],
+        *[shape_of(bf16, share, width)] * 2,
+        in_hbm(f32, 2 * share, width),
+        in_hbm(f32, rows, rows),
+        in_hbm(f32, rows, rows),
+    )
+    late_got = [hop(part, CORE_SWAP) for part in late_given]
+    (late_sums,) = in_place(
+        sums_kernel,
+        "late_sums",
+        [late_kept, *late_got, outer_square],
+        shape_of(bf16, share + rows * rows // width, width),
+    )
+    sent_late = hop(late_sums, OUTWARD)
+    own_d_acts, outer_d_acts = in_place(
         own_kernel,
         "own_grads",
-        [after(d_seg0, late_given), d_gate, w_in, pack, outer_pack, own[4], outer[4]],
+        [after(d_seg0, late_sums, sent_early), d_gate, w_in, pack, outer_pack],
         full,
         full,
-        shape_of(f32, rows, rows),
-        shape_of(f32, rows, rows),
-    )
-    (late_sums,) = in_place(
-        sums_kernel, "late_sums", [late_kept, late_got], shape_of(bf16, share, width)
-    )
-    sent_late = hop(late_sums, OUTWARD)
-    sent_square = hop(narrow(outer_square), OUTWARD)
+    )
+    outer_handed = lax.ppermute(outer_d_acts, ("pipe", "seq"), relay_back(True))
     own_handed = lax.ppermute(own_d_acts, ("pipe", "seq"), relay_back(False))
-    outer_handed = lax.ppermute(outer_d_acts, ("pipe", "seq"), relay_back(True))
 
     def one_side(pair_terms, flip):
         empty = jnp.zeros_like(pair_terms)
@@ -556,35 +589,38 @@
             flip == 1, jnp.stack([empty, pair_terms]), jnp.stack([pair_terms, empty])
         )
 
-    first_terms, later_terms = after(first_part[:, 0], late_sums), after(later_part[:, 0], late_sums)
+    first_terms, later_terms = lax.optimization_barrier(
+        (first_part[:2], later_part, outer_d_acts, late_sums)
+    )[:2]
     both = later_terms[:4].reshape(2, 2, width)
     terms = jnp.stack(
         [
             one_side(first_terms, flips[0]),
             jnp.where(flips[1] == 1, both[::-1], both),
-            one_side(later_terms[4:], flips[2]),
+            one_side(later_terms[4:6], flips[2]),
         ]
     )
     terms = terms + hop(terms, CORE_SWAP)
     terms = terms + hop(terms, ACROSS)
-    twiddle_grad = jnp.where(inner, terms, hop(terms, OUTWARD))
-
-    mixed_out = jnp.where(inner, own_mixed, after(sent_mixed, late_sums))
-    handed = jnp.where(inner, own_handed, outer_handed)
-    grad_square = jnp.where(inner, own_square, wide(sent_square))
-    sent_early = wide(after(sent_early, twiddle_grad))
-    sent_late = wide(after(sent_late, twiddle_grad))
+    twiddle_grad = jnp.where(inner, terms, hop(after(terms, sent_late), OUTWARD))
+
+    mixed_out = jnp.where(inner, own_mixed, after(sent_mixed, outer_d_acts))
+    sent_early = after(sent_early, outer_d_acts)
 
     def share_of(kept, got, sent, at):
-        here = slice(2 * at * share, (2 * at + 1) * share)
-        mine = kept[here] + wide(got[here])
-        return jnp.where(inner, mine, sent[at * share : (at + 1) * share])
+        mine = kept[2 * at * share : (2 * at + 1) * share] + wide(got[2 * at])
+        return jnp.where(inner, mine, wide(sent[at * share : (at + 1) * share]))
 
     win_share = jnp.concatenate(
         [share_of(late_kept, late_got, sent_late, 0), share_of(early_kept, early_got, sent_early, 0)],
         axis=1,
     )
     wout_share = share_of(early_kept, early_got, sent_early, 1)
+    sent_square = jnp.concatenate(
+        [sent_late[share:, i * rows : (i + 1) * rows] for i in range(width // rows)]
+    )
+    grad_square = jnp.where(inner, own_square, wide(sent_square))
+    handed = jnp.where(inner, own_handed, outer_handed)
     return mixed_out, handed, win_share, wout_share, grad_square, twiddle_grad
 
 

time: 142 us -> 130 us (0.915)
  the two profiles are of different devices: /device:TPU:4 before, /device:TPU:18 now
where the time goes in v3:
time: 130 us; the launch traced here: 128 us
  Pallas kernels  48.7 us (37%)
  starting transfers between devices  31.2 us (24%)
  waiting for transfers between devices  22.4 us (17%)
  local copies, waits for them, and re-layouts  15.9 us (12%)
  other arithmetic  8.8 us (7%)
  between operations  1.4 us (1%)
    pallas_call x14, Pallas kernels, in_place(): kernel_call(kernel, name, work, room, in_specs=[pl.BlockSpec(memory_space...  36.4 us
    ppermute x27, starting transfers between devices, hop(): return lax.ppermute(value, 'seq', pairs)  27.8 us
    ppermute x27, waiting for transfers between devices, hop(): return lax.ppermute(value, 'seq', pairs)  19.3 us
    unnamed x88, local copies, waits for them, and re-layouts  15 us
    broadcast_in_dim x6, other arithmetic, on_device(): result[None]  6.75 us
    pallas_call x1, Pallas kernels, relay_plan(): kernel_call(forward_kernel, 'forward_segments', room=60, grid=(rows // TI...  6.58 us
    ppermute x1, waiting for transfers between devices, relay_plan(): own_handed = lax.ppermute(own_d_acts, ('pipe', 'seq'), relay_back(False))  3.18 us
    pallas_call x1, Pallas kernels, relay_plan(): kernel_call(first_bit_kernel, 'first_segment_grad', grid=(rows // TILE,),...  2.96 us
  transfers between devices with their start and end apart: 29, of which 13 were waited for; matrix products, arithmetic and copies ran while one was open for 7% of the time, Pallas kernels for 36%

profile of v3, /device:TPU:18, one launch (start us, length us, event | category | flops | bytes accessed | tf_op | source)
XLA Modules:
  0.0 128.5 jit_solution(10592391798126139103)
XLA Ops:
  3.9 2.4 %collective-permute-start.1 = (bf16[320,1024]{1,0:T(8,128)(2,1)}, bf16[320,1024]{1,0:T(8,128)(2,1)}, u32[]{:S(2)}, u32[]{:S(2)}) collective-permute-start(bf16[320,1024]{1,0:T(8,128)(2,1)} %pack.1.pack_ref.refs_0_), channel_id=1, source_target_pairs={{2,4},{3,5},{4,2},{5,3},{10,12},{11,13},{12,10},{13,11},{18,20},{1... | collective-permute-start | bytes 1966088 | tf_op jit(solution)/shard_map/ppermute | solution.py:152
  6.4 2.2 %copy-done = bf16[1,1024,2048]{2,1,0:T(8,128)(2,1)S(1)} copy-done((bf16[1,1024,2048]{2,1,0:T(8,128)(2,1)S(1)}, bf16[1,1024,2048]{2,1,0:T(8,128)(2,1)}, u32[]{:S(2)}) %copy-start) | copy-done | bytes 4194328
  9.6 3.3 %block_0.1 = (bf16[256,512]{1,0:T(8,128)(2,1)}, bf16[256,512]{1,0:T(8,128)(2,1)}, bf16[256,1024]{1,0:T(8,128)(2,1)}, bf16[256,1024]{1,0:T(8,128)(2,1)}, bf16[256,1024]{1,0:T(8,128)(2,1)}) custom-call(s32[4]{0:T(128)S(1)} %pad_add_fusion.starts_ref, bf16[320,1024]{1,0:T(8,128)(2,1)S(1)} %copy-done.7, bf16[1024,2048]{1,0:T(8,128)(2,1)S(1)} %bitcast.36), custom_call_target="tpu_custom_call" | custom-call | flops 1073741824 | bytes 1 | tf_op jit(solution)/shard_map/block_0/pallas_call | solution.py:413
  14.8 6.4 %collective-permute-done.pack_ref.refs_1_ = bf16[320,1024]{1,0:T(8,128)(2,1)S(1)} collective-permute-done((bf16[320,1024]{1,0:T(8,128)(2,1)}, bf16[320,1024]{1,0:T(8,128)(2,1)S(1)}, u32[]{:S(2)}, u32[]{:S(2)}) %collective-permute-start) | collective-permute-done | bytes 655392 | tf_op jit(solution)/shard_map/ppermute | solution.py:152
  21.2 2.3 %collective-permute-start.2 = (bf16[320,1024]{1,0:T(8,128)(2,1)S(1)}, bf16[320,1024]{1,0:T(8,128)(2,1)}, u32[]{:S(2)}, u32[]{:S(2)}) collective-permute-start(bf16[320,1024]{1,0:T(8,128)(2,1)S(1)} %collective-permute-done.pack_ref.refs_1_), channel_id=1, source_target_pairs={{2,4},{3,5},{4,2},{5,3},{10,12},{11,13},{12,10},{13,11},{18,20},{1... | collective-permute-start | bytes 1966088 | tf_op jit(solution)/shard_map/ppermute | solution.py:152
  24.9 3.5 %collective-permute-start.5 = (bf16[256,1024]{1,0:T(8,128)(2,1)}, bf16[256,1024]{1,0:T(8,128)(2,1)}, u32[]{:S(2)}, u32[]{:S(2)}) collective-permute-start(bf16[256,1024]{1,0:T(8,128)(2,1)} %bitcast.11.refs_0_.refs_6_), channel_id=1, source_target_pairs={{2,4},{3,5},{4,2},{5,3},{10,12},{11,13},{12,10},{13,11},{18,20},{1... | collective-permute-start | bytes 1572872 | tf_op jit(solution)/shard_map/ppermute | solution.py:152
  30.6 3.4 %block_1.1 = (bf16[256,512]{1,0:T(8,128)(2,1)}, bf16[256,512]{1,0:T(8,128)(2,1)}, bf16[256,1024]{1,0:T(8,128)(2,1)}, bf16[256,1024]{1,0:T(8,128)(2,1)}, bf16[256,1024]{1,0:T(8,128)(2,1)}) custom-call(s32[4]{0:T(128)S(1)} %pad_add_fusion.starts_ref, bf16[320,1024]{1,0:T(8,128)(2,1)S(1)} %collective-permute-done.pack_ref.refs_1_, bf16[1024,2048]{1,0:T(8,128)(2,1)S(1)} %bitcast.37), custom_call_target="tpu_custom_call" | custom-call | flops 1 | bytes 1 | tf_op jit(solution)/shard_map/block_1/pallas_call | solution.py:413
  34.2 3.7 %block_3.1 = (bf16[256,512]{1,0:T(8,128)(2,1)}, bf16[256,512]{1,0:T(8,128)(2,1)}, bf16[256,1024]{1,0:T(8,128)(2,1)}, bf16[256,1024]{1,0:T(8,128)(2,1)}) custom-call(s32[4]{0:T(128)S(1)} %pad_add_fusion.starts_ref, bf16[320,1024]{1,0:T(8,128)(2,1)} %collective-permute-done.1.pack_ref, bf16[1024,2048]{1,0:T(8,128)(2,1)S(1)} %bitcast.38), custom_call_target="tpu_custom_call" | custom-call | flops 1 | bytes 1 | tf_op jit(solution)/shard_map/block_3/pallas_call | solution.py:413
  38.3 2.5 %collective-permute-done.2.pack_ref = bf16[320,1024]{1,0:T(8,128)(2,1)} collective-permute-done((bf16[320,1024]{1,0:T(8,128)(2,1)S(1)}, bf16[320,1024]{1,0:T(8,128)(2,1)}, u32[]{:S(2)}, u32[]{:S(2)}) %collective-permute-start.2) | collective-permute-done | bytes 655392 | tf_op jit(solution)/shard_map/ppermute | solution.py:152
  40.8 2.3 %collective-permute-start.11 = (bf16[256,1024]{1,0:T(8,128)(2,1)}, bf16[256,1024]{1,0:T(8,128)(2,1)}, u32[]{:S(2)}, u32[]{:S(2)}) collective-permute-start(bf16[256,1024]{1,0:T(8,128)(2,1)} %collective-permute-done.3.refs_0_.refs_7_), channel_id=1, source_target_pairs={{2,4},{3,5},{4,2},{5,3},{10,12},{11,13},{12,10},{13,11},{18,20},{1... | collective-permute-start | bytes 1572872 | tf_op jit(solution)/shard_map/ppermute | solution.py:152
  45.4 3.8 %block_2.1 = (bf16[256,512]{1,0:T(8,128)(2,1)}, bf16[256,512]{1,0:T(8,128)(2,1)}, bf16[256,1024]{1,0:T(8,128)(2,1)}, bf16[256,512]{1,0:T(8,128)(2,1)}, bf16[256,512]{1,0:T(8,128)(2,1)}) custom-call(s32[4]{0:T(128)S(1)} %pad_add_fusion.starts_ref, bf16[320,1024]{1,0:T(8,128)(2,1)} %collective-permute-done.2.pack_ref, bf16[1024,2048]{1,0:T(8,128)(2,1)S(1)} %bitcast.39), custom_call_target="tpu_custom_call" | custom-call | flops 1 | bytes 1 | tf_op jit(solution)/shard_map/block_2/pallas_call | solution.py:413
  49.2 2.9 %collective-permute-done.5.refs_1_.refs_9_ = bf16[256,1024]{1,0:T(8,128)(2,1)} collective-permute-done((bf16[256,1024]{1,0:T(8,128)(2,1)}, bf16[256,1024]{1,0:T(8,128)(2,1)}, u32[]{:S(2)}, u32[]{:S(2)}) %collective-permute-start.5) | collective-permute-done | bytes 524320 | tf_op jit(solution)/shard_map/ppermute | solution.py:152
  53.9 6.6 %forward_segments.1 = (bf16[2,256,1024]{2,1,0:T(8,128)(2,1)}, bf16[4,256,1024]{2,1,0:T(8,128)(2,1)}, bf16[2,256,1024]{2,1,0:T(8,128)(2,1)}, bf16[4,256,512]{2,1,0:T(8,128)(2,1)}) custom-call(s32[4]{0:T(128)} %copy-done.37, bf16[16,1024]{1,0:T(8,128)(2,1)} %maximum_maximum_fusion.coef_ref, bf16[256,1024]{1,0:T(8,128)(2,1)} %get-tuple-element.68.refs_0_.refs_8_, ...), custom_call_target="tpu_custom_call" | custom-call | flops 1 | bytes 1 | tf_op jit(solution)/shard_map/forward_segments/pallas_call | solution.py:489
  65.3 2.6 %d_hidden.4 = (bf16[256,1024]{1,0:T(8,128)(2,1)S(1)}, bf16[256,1024]{1,0:T(8,128)(2,1)S(1)}) custom-call(bf16[1024,1024]{1,0:T(8,128)(2,1)S(1)} %bitcast.43, bf16[256,1024]{1,0:T(8,128)(2,1)} %collective-permute-done.3.refs_0_.refs_7_, bf16[256,1024]{1,0:T(8,128)(2,1)} %collective-permute-done.5.refs_1_.refs_9_), custom_call_target="tpu_custom_call" | custom-call | flops 1 | bytes 1 | tf_op jit(solution)/shard_map/d_hidden/pallas_call | solution.py:413
  70.1 2.7 %backward_segments.1 = (bf16[4,256,1024]{2,1,0:T(8,128)(2,1)S(1)}, bf16[256,1024]{1,0:T(8,128)(2,1)S(1)}, bf16[256,1024]{1,0:T(8,128)(2,1)S(1)}, bf16[256,1024]{...) custom-call(bf16[16,1024]{1,0:T(8,128)(2,1)S(1)} %copy-done.23, ...), custom_call_target="tpu_custom_call" | custom-call | flops 1 | bytes 1 | tf_op jit(solution)/shard_map/backward_segments/pallas_call | solution.py:526
  73.9 3.9 %early_grads.1 = (bf16[128,1024]{1,0:T(8,128)(2,1)S(1)}, bf16[128,1024]{1,0:T(8,128)(2,1)S(1)}, bf16[128,1024]{1,0:T(8,128)(2,1)S(1)}, bf16[128,1024]{1,0:T(8,128)(2,1)S(1)}, f32[512,1024]{1,0:T(8,128)S(1)}) custom-call(bf16[256,512]{1,0:T(8,128)(2,1)S(1)} %copy-done.32, bf16[256,512]{1,0:T(8,128)(2,1)S(1)} %copy-done.33, bf16[256,512]{1,0:T(8,128)(2,1)S(1)} %copy-done.35, ...), custom_call_target="tpu_custom_call" | custom-call | flops 1 | bytes 1 | tf_op jit(solution)/shard_map/early_grads/pallas_call | solution.py:413
  81.5 4.4 %collective-permute-start.22 = (bf16[256,1024]{1,0:T(8,128)(2,1)}, bf16[256,1024]{1,0:T(8,128)(2,1)}, u32[]{:S(2)}, u32[]{:S(2)}) collective-permute-start(bf16[256,1024]{1,0:T(8,128)(2,1)} %early_sums.1), channel_id=1, source_target_pairs={{2,0},{3,1},{4,6},{5,7},{10,8},{11,9},{12,14},{13,15},{18,16},{19,... | collective-permute-start | bytes 1572872 | tf_op jit(solution)/shard_map/ppermute | solution.py:152
  85.8 3.0 %first_segment_grad.1 = (bf16[4,256,1024]{2,1,0:T(8,128)(2,1)S(1)}, f32[8,1024]{1,0:T(8,128)S(1)}) custom-call(bf16[16,1024]{1,0:T(8,128)(2,1)S(1)} %copy-done.23, bf16[256,1024]{1,0:T(8,128)(2,1)S(1)} %get-tuple-element.94.refs_0_, bf16[256,1024]{1,0:T(8,128)(2,1)S(1)} %get-tuple-element.95.refs_1_, bf16[256,1024]{1,0:T(8,128)(2,1)S(1)} %get-tuple-element.96.refs_2_, ...), custom_call_target="tpu_custom_call" | custom-call | flops 1 | bytes 1 | tf_op jit(solution)/shard_map/first_segment_grad/pallas_call | solution.py:551
  88.9 2.7 %value_grads.1 = (bf16[128,1024]{1,0:T(8,128)(2,1)}, bf16[128,1024]{1,0:T(8,128)(2,1)}, f32[256,1024]{1,0:T(8,128)}, f32[256,256]{1,0:T(8,128)}, f32[256,256]{1,0:T(8,128)}) custom-call(bf16[4,256,1024]{2,1,0:T(8,128)(2,1)S(1)} %get-tuple-element.119.d_seg0_ref, bf16[256,512]{1,0:T(8,128)(2,1)S(1)} %copy-done.28, bf16[256,512]{1,0:T(8,128)(2,1)S(1)} %copy-done.29, ...), custom_call_target="tpu_custom_call" | custom-call | flops 1 | bytes 1 | tf_op jit(solution)/shard_map/value_grads/pallas_call | solution.py:413
  102.1 3.4 %own_grads.1 = (bf16[256,1024]{1,0:T(8,128)(2,1)S(1)}, bf16[256,1024]{1,0:T(8,128)(2,1)}) custom-call(bf16[4,256,1024]{2,1,0:T(8,128)(2,1)S(1)} %copy-done.6, bf16[4,256,1024]{2,1,0:T(8,128)(2,1)S(1)} %get-tuple-element.99.refs_4_.d_gate_ref, bf16[1024,2048]{1,0:T(8,128)(2,1)S(1)} %bitcast.40, bf16[320,1024]{1,0:T(8,128)(2,1)S(1)} %copy-done.8, ...), custom_call_target="tpu_custom_call" | custom-call | flops 1 | bytes 1 | tf_op jit(solution)/shard_map/own_grads/pallas_call | solution.py:413
  108.1 2.6 %select_bitcast_fusion = (f32[1,128,1024]{2,1,0:T(8,128)}, f32[128,1024]{1,0:T(8,128)S(1)}) fusion(bf16[128,1024]{1,0:T(8,128)(2,1)} %copy-done.21, f32[512,1024]{1,0:T(8,128)} %copy-done.9, bf16[256,1024]{1,0:T(8,128)(2,1)} %collective-permute-done.22, pred[]{:T(512)S(6)} %or.3, bf16[128,1024]{1,0:T(8,128)(2,1)} %copy-done.20), kind=kLoop, calls=%fused_computation.1 | loop fusion | flops 1048576 | bytes 3145729 | tf_op jit(solution)/shard_map/broadcast_in_dim | solution.py:629
  112.7 2.4 %collective-permute-start.27 = (f32[3,2,2,1024]{3,2,1,0:T(2,128)S(1)}, f32[3,2,2,1024]{3,2,1,0:T(2,128)S(1)}, u32[]{:S(2)}, u32[]{:S(2)}) collective-permute-start(f32[3,2,2,1024]{3,2,1,0:T(2,128)S(1)} %fusion.4), channel_id=1, source_target_pairs={{2,4},{3,5},{4,2},{5,3},{10,12},{11,13},{12,10},{13,11},{18,20},{1... | collective-permute-start | bytes 147464 | tf_op jit(solution)/shard_map/ppermute | solution.py:152
  115.9 2.7 %collective-permute-done.27 = f32[3,2,2,1024]{3,2,1,0:T(2,128)S(1)} collective-permute-done((f32[3,2,2,1024]{3,2,1,0:T(2,128)S(1)}, f32[3,2,2,1024]{3,2,1,0:T(2,128)S(1)}, u32[]{:S(2)}, u32[]{:S(2)}) %collective-permute-start.27) | collective-permute-done | bytes 49184 | tf_op jit(solution)/shard_map/ppermute | solution.py:152
  124.4 3.2 %collective-permute-done.23 = bf16[256,1024]{1,0:T(8,128)(2,1)S(1)} collective-permute-done((bf16[256,1024]{1,0:T(8,128)(2,1)S(1)}, bf16[256,1024]{1,0:T(8,128)(2,1)S(1)}, u32[]{:S(2)}, u32[]{:S(2)}) %collective-permute-start.23) | collective-permute-done | bytes 524320 | tf_op jit(solution)/shard_map/ppermute | solution.py:584
  (167 shorter events, 48.3 us)
Async XLA Ops:
  2.6 18.6 %collective-permute-start = (bf16[320,1024]{1,0:T(8,128)(2,1)}, bf16[320,1024]{1,0:T(8,128)(2,1)S(1)}, u32[]{:S(2)}, u32[]{:S(2)}) collective-permute-start(bf16[320,1024]{1,0:T(8,128)(2,1)} %pack.1.pack_ref.refs_0_), channel_id=1, source_target_pairs={{0,2},{1,3},{6,4},{7,5},{8,10},{9,11},{14,12},{15,13},{16,18},{17,... | collective-permute-start | bytes 1966088 | tf_op jit(solution)/shard_map/ppermute | solution.py:152
  3.9 30.1 %collective-permute-start.1 = (bf16[320,1024]{1,0:T(8,128)(2,1)}, bf16[320,1024]{1,0:T(8,128)(2,1)}, u32[]{:S(2)}, u32[]{:S(2)}) collective-permute-start(bf16[320,1024]{1,0:T(8,128)(2,1)} %pack.1.pack_ref.refs_0_), channel_id=1, source_target_pairs={{2,4},{3,5},{4,2},{5,3},{10,12},{11,13},{12,10},{13,11},{18,20},{1... | collective-permute-start | bytes 1966088 | tf_op jit(solution)/shard_map/ppermute | solution.py:152
  21.2 19.7 %collective-permute-start.2 = (bf16[320,1024]{1,0:T(8,128)(2,1)S(1)}, bf16[320,1024]{1,0:T(8,128)(2,1)}, u32[]{:S(2)}, u32[]{:S(2)}) collective-permute-start(bf16[320,1024]{1,0:T(8,128)(2,1)S(1)} %collective-permute-done.pack_ref.refs_1_), channel_id=1, source_target_pairs={{2,4},{3,5},{4,2},{5,3},{10,12},{11,13},{12,10},{13,11},{18,20},{1... | collective-permute-start | bytes 1966088 | tf_op jit(solution)/shard_map/ppermute | solution.py:152
  23.5 14.8 %collective-permute-start.3 = (bf16[256,1024]{1,0:T(8,128)(2,1)}, bf16[256,1024]{1,0:T(8,128)(2,1)}, u32[]{:S(2)}, u32[]{:S(2)}) collective-permute-start(bf16[256,1024]{1,0:T(8,128)(2,1)} %bitcast.11.refs_0_.refs_6_), channel_id=1, source_target_pairs={{0,2},{1,3},{6,4},{7,5},{8,10},{9,11},{14,12},{15,13},{16,18},{17,... | collective-permute-start | bytes 1572872 | tf_op jit(solution)/shard_map/ppermute | solution.py:152
  24.8 24.4 %collective-permute-start.4 = (bf16[256,1024]{1,0:T(8,128)(2,1)}, bf16[256,1024]{1,0:T(8,128)(2,1)}, u32[]{:S(2)}, u32[]{:S(2)}) collective-permute-start(bf16[256,1024]{1,0:T(8,128)(2,1)} %get-tuple-element.68.refs_0_.refs_8_), channel_id=1, source_target_pairs={{0,1},{1,0},{2,3},{3,2},{4,5},{5,4},{6,7},{7,6},{8,9},{9,8},{10,11... | collective-permute-start | bytes 1572872 | tf_op jit(solution)/shard_map/ppermute | solution.py:152
  24.9 27.2 %collective-permute-start.5 = (bf16[256,1024]{1,0:T(8,128)(2,1)}, bf16[256,1024]{1,0:T(8,128)(2,1)}, u32[]{:S(2)}, u32[]{:S(2)}) collective-permute-start(bf16[256,1024]{1,0:T(8,128)(2,1)} %bitcast.11.refs_0_.refs_6_), channel_id=1, source_target_pairs={{2,4},{3,5},{4,2},{5,3},{10,12},{11,13},{12,10},{13,11},{18,20},{1... | collective-permute-start | bytes 1572872 | tf_op jit(solution)/shard_map/ppermute | solution.py:152
  34.0 18.9 %collective-permute-start.6 = (bf16[256,1024]{1,0:T(8,128)(2,1)}, bf16[256,1024]{1,0:T(8,128)(2,1)}, u32[]{:S(2)}, u32[]{:S(2)}) collective-permute-start(bf16[256,1024]{1,0:T(8,128)(2,1)} %get-tuple-element.69.refs_1_.refs_9_), channel_id=1, source_target_pairs={{0,1},{1,0},{2,3},{3,2},{4,5},{5,4},{6,7},{7,6},{8,9},{9,8},{10,11... | collective-permute-start | bytes 1572872 | tf_op jit(solution)/shard_map/ppermute | solution.py:152
  38.3 14.6 %collective-permute-start.7 = (bf16[256,1024]{1,0:T(8,128)(2,1)}, bf16[256,1024]{1,0:T(8,128)(2,1)}, u32[]{:S(2)}, u32[]{:S(2)}) collective-permute-start(bf16[256,1024]{1,0:T(8,128)(2,1)} %get-tuple-element.72.refs_2_), channel_id=1, source_target_pairs={{0,1},{1,0},{2,3},{3,2},{4,5},{5,4},{6,7},{7,6},{8,9},{9,8},{10,11... | collective-permute-start | bytes 1572872 | tf_op jit(solution)/shard_map/ppermute | solution.py:152
  40.8 27.2 %collective-permute-start.11 = (bf16[256,1024]{1,0:T(8,128)(2,1)}, bf16[256,1024]{1,0:T(8,128)(2,1)}, u32[]{:S(2)}, u32[]{:S(2)}) collective-permute-start(bf16[256,1024]{1,0:T(8,128)(2,1)} %collective-permute-done.3.refs_0_.refs_7_), channel_id=1, source_target_pairs={{2,4},{3,5},{4,2},{5,3},{10,12},{11,13},{12,10},{13,11},{18,20},{1... | collective-permute-start | bytes 1572872 | tf_op jit(solution)/shard_map/ppermute | solution.py:152
  49.2 3.7 %collective-permute-start.8 = (bf16[256,512]{1,0:T(8,128)(2,1)}, bf16[256,512]{1,0:T(8,128)(2,1)}, u32[]{:S(2)}, u32[]{:S(2)}) collective-permute-start(bf16[256,512]{1,0:T(8,128)(2,1)} %get-tuple-element.78.refs_3_), channel_id=1, source_target_pairs={{0,1},{1,0},{2,3},{3,2},{4,5},{5,4},{6,7},{7,6},{8,9},{9,8},{10,11... | collective-permute-start | bytes 786440 | tf_op jit(solution)/shard_map/ppermute | solution.py:152
  63.8 14.0 %collective-permute-start.10 = (bf16[256,1024]{1,0:T(8,128)(2,1)S(1)}, bf16[256,1024]{1,0:T(8,128)(2,1)S(1)}, u32[]{:S(2)}, u32[]{:S(2)}) collective-permute-start(bf16[256,1024]{1,0:T(8,128)(2,1)S(1)} %get-tuple-element.87), channel_id=1, source_target_pairs={{2,0},{3,1},{4,6},{5,7},{10,8},{11,9},{12,14},{13,15},{18,16},{19,... | collective-permute-start | bytes 1572872 | tf_op jit(solution)/shard_map/ppermute | solution.py:152
  72.8 5.2 %collective-permute-start.12 = (bf16[256,1024]{1,0:T(8,128)(2,1)S(1)}, bf16[256,1024]{1,0:T(8,128)(2,1)S(1)}, u32[]{:S(2)}, u32[]{:S(2)}) collective-permute-start(bf16[256,1024]{1,0:T(8,128)(2,1)S(1)} %get-tuple-element.94.refs_0_), channel_id=1, source_target_pairs={{0,1},{1,0},{2,3},{3,2},{4,5},{5,4},{6,7},{7,6},{8,9},{9,8},{10,11... | collective-permute-start | bytes 1572872 | tf_op jit(solution)/shard_map/ppermute | solution.py:152
  73.0 5.4 %collective-permute-start.13 = (bf16[256,1024]{1,0:T(8,128)(2,1)S(1)}, bf16[256,1024]{1,0:T(8,128)(2,1)S(1)}, u32[]{:S(2)}, u32[]{:S(2)}) collective-permute-start(bf16[256,1024]{1,0:T(8,128)(2,1)S(1)} %get-tuple-element.95.refs_1_), channel_id=1, source_target_pairs={{0,1},{1,0},{2,3},{3,2},{4,5},{5,4},{6,7},{7,6},{8,9},{9,8},{10,11... | collective-permute-start | bytes 1572872 | tf_op jit(solution)/shard_map/ppermute | solution.py:152
  73.4 5.2 %collective-permute-start.14 = (bf16[256,1024]{1,0:T(8,128)(2,1)S(1)}, bf16[256,1024]{1,0:T(8,128)(2,1)S(1)}, u32[]{:S(2)}, u32[]{:S(2)}) collective-permute-start(bf16[256,1024]{1,0:T(8,128)(2,1)S(1)} %get-tuple-element.96.refs_2_), channel_id=1, source_target_pairs={{0,1},{1,0},{2,3},{3,2},{4,5},{5,4},{6,7},{7,6},{8,9},{9,8},{10,11... | collective-permute-start | bytes 1572872 | tf_op jit(solution)/shard_map/ppermute | solution.py:152
  73.5 5.4 %collective-permute-start.15 = (bf16[256,1024]{1,0:T(8,128)(2,1)S(1)}, bf16[256,1024]{1,0:T(8,128)(2,1)S(1)}, u32[]{:S(2)}, u32[]{:S(2)}) collective-permute-start(bf16[256,1024]{1,0:T(8,128)(2,1)S(1)} %get-tuple-element.97.refs_3_), channel_id=1, source_target_pairs={{0,1},{1,0},{2,3},{3,2},{4,5},{5,4},{6,7},{7,6},{8,9},{9,8},{10,11... | collective-permute-start | bytes 1572872 | tf_op jit(solution)/shard_map/ppermute | solution.py:152
  78.5 2.0 %collective-permute-start.19 = (bf16[128,1024]{1,0:T(8,128)(2,1)S(1)}, bf16[128,1024]{1,0:T(8,128)(2,1)S(1)}, u32[]{:S(2)}, u32[]{:S(2)}) collective-permute-start(bf16[128,1024]{1,0:T(8,128)(2,1)S(1)} %get-tuple-element.106), channel_id=1, source_target_pairs={{0,1},{1,0},{2,3},{3,2},{4,5},{5,4},{6,7},{7,6},{8,9},{9,8},{10,11... | collective-permute-start | bytes 786440 | tf_op jit(solution)/shard_map/ppermute | solution.py:152
  81.5 18.4 %collective-permute-start.22 = (bf16[256,1024]{1,0:T(8,128)(2,1)}, bf16[256,1024]{1,0:T(8,128)(2,1)}, u32[]{:S(2)}, u32[]{:S(2)}) collective-permute-start(bf16[256,1024]{1,0:T(8,128)(2,1)} %early_sums.1), channel_id=1, source_target_pairs={{2,0},{3,1},{4,6},{5,7},{10,8},{11,9},{12,14},{13,15},{18,16},{19,... | collective-permute-start | bytes 1572872 | tf_op jit(solution)/shard_map/ppermute | solution.py:152
  91.6 2.2 %collective-permute-start.21 = (bf16[128,1024]{1,0:T(8,128)(2,1)}, bf16[128,1024]{1,0:T(8,128)(2,1)}, u32[]{:S(2)}, u32[]{:S(2)}) collective-permute-start(bf16[128,1024]{1,0:T(8,128)(2,1)} %get-tuple-element.117), channel_id=1, source_target_pairs={{0,1},{1,0},{2,3},{3,2},{4,5},{5,4},{6,7},{7,6},{8,9},{9,8},{10,11... | collective-permute-start | bytes 786440 | tf_op jit(solution)/shard_map/ppermute | solution.py:152
  97.8 20.9 %collective-permute-start.25 = (bf16[192,1024]{1,0:T(8,128)(2,1)}, bf16[192,1024]{1,0:T(8,128)(2,1)}, u32[]{:S(2)}, u32[]{:S(2)}) collective-permute-start(bf16[192,1024]{1,0:T(8,128)(2,1)} %late_sums.1), channel_id=1, source_target_pairs={{2,0},{3,1},{4,6},{5,7},{10,8},{11,9},{12,14},{13,15},{18,16},{19,... | collective-permute-start | bytes 1179656 | tf_op jit(solution)/shard_map/ppermute | solution.py:152
  106.3 21.3 %collective-permute-start.24 = (bf16[256,1024]{1,0:T(8,128)(2,1)}, bf16[256,1024]{1,0:T(8,128)(2,1)S(1)}, u32[]{:S(2)}, u32[]{:S(2)}) collective-permute-start(bf16[256,1024]{1,0:T(8,128)(2,1)} %get-tuple-element.120), channel_id=1, source_target_pairs={{10,0},{11,1},{12,6},{13,7},{18,8},{19,9},{20,14},{21,15},{26,16},... | collective-permute-start | bytes 1572872 | tf_op jit(solution)/shard_map/ppermute | solution.py:583
  107.9 4.8 %collective-permute-start.26 = (f32[3,2,2,1024]{3,2,1,0:T(2,128)S(1)}, f32[3,2,2,1024]{3,2,1,0:T(2,128)S(1)}, u32[]{:S(2)}, u32[]{:S(2)}) collective-permute-start(f32[3,2,2,1024]{3,2,1,0:T(2,128)S(1)} %pad_maximum_fusion), channel_id=1, source_target_pairs={{0,1},{1,0},{2,3},{3,2},{4,5},{5,4},{6,7},{7,6},{8,9},{9,8},{10,11... | collective-permute-start | bytes 147464 | tf_op jit(solution)/shard_map/ppermute | solution.py:152
  110.7 16.9 %collective-permute-start.23 = (bf16[256,1024]{1,0:T(8,128)(2,1)S(1)}, bf16[256,1024]{1,0:T(8,128)(2,1)S(1)}, u32[]{:S(2)}, u32[]{:S(2)}) collective-permute-start(bf16[256,1024]{1,0:T(8,128)(2,1)S(1)} %copy-done.39), channel_id=1, source_target_pairs={{10,2},{11,3},{12,4},{13,5},{18,10},{19,11},{20,12},{21,13},{26,18... | collective-permute-start | bytes 1572872 | tf_op jit(solution)/shard_map/ppermute | solution.py:584
  112.7 6.0 %collective-permute-start.27 = (f32[3,2,2,1024]{3,2,1,0:T(2,128)S(1)}, f32[3,2,2,1024]{3,2,1,0:T(2,128)S(1)}, u32[]{:S(2)}, u32[]{:S(2)}) collective-permute-start(f32[3,2,2,1024]{3,2,1,0:T(2,128)S(1)} %fusion.4), channel_id=1, source_target_pairs={{2,4},{3,5},{4,2},{5,3},{10,12},{11,13},{12,10},{13,11},{18,20},{1... | collective-permute-start | bytes 147464 | tf_op jit(solution)/shard_map/ppermute | solution.py:152
  118.7 5.0 %collective-permute-start.28 = (f32[3,2,2,1024]{3,2,1,0:T(2,128)S(1)}, f32[3,2,2,1024]{3,2,1,0:T(2,128)S(1)}, u32[]{:S(2)}, u32[]{:S(2)}) collective-permute-start(f32[3,2,2,1024]{3,2,1,0:T(2,128)S(1)} %fusion.6), channel_id=1, source_target_pairs={{2,0},{3,1},{4,6},{5,7},{10,8},{11,9},{12,14},{13,15},{18,16},{19,... | collective-permute-start | bytes 147464 | tf_op jit(solution)/shard_map/ppermute | solution.py:152
  (49 other events, 258.7 us)

commit v4 on v3

--- a/solution.py
+++ b/solution.py
@@ -238,13 +238,13 @@
     given_refs, kept_ref = refs[10:14], refs[14]
     half = kept_ref.shape[0] // 2
     d_gates = [d_gate_ref.at[k] for k in range(4)]
-    split_grad(columns, d_gates, given_refs[0:2], kept_ref.at[pl.ds(0, half), :])
+    split_grad(columns, d_gates, given_refs[0:2], [kept_ref.at[pl.ds(0, half), :]])
     hiddens = [hidden_ref.at[k] for k in range(4)]
-    split_grad(hiddens, cotans, given_refs[2:4], kept_ref.at[pl.ds(half, half), :])
-
-
-def split_grad(lefts, rights, given_refs, kept_ref):
-    half = kept_ref.shape[0]
+    split_grad(hiddens, cotans, given_refs[2:4], [kept_ref.at[pl.ds(half, half), :]])
+
+
+def split_grad(lefts, rights, given_refs, kept_refs):
+    half = sum(ref.shape[0] for ref in kept_refs)
     for part in range(2):
         total = 0.0
         for left, right in zip(lefts, rights):
@@ -254,31 +254,35 @@
                 size = ref.shape[0]
                 ref[...] = narrow(total[i * size : (i + 1) * size])
         else:
-            kept_ref[...] = total
+            for i, ref in enumerate(kept_refs):
+                size = ref.shape[0]
+                ref[...] = total[i * size : (i + 1) * size]
 
 
 def value_grads_kernel(d_seg0_ref, *refs):
-    values, given_refs, kept_ref = refs[4:6], refs[6:8], refs[8]
-    split_grad(refs[0:4], [d_seg0_ref.at[k] for k in range(4)], given_refs, kept_ref)
+    values, given_refs, kept_refs = refs[4:6], refs[6:8], refs[8:10]
+    split_grad(refs[0:4], [d_seg0_ref.at[k] for k in range(4)], given_refs, kept_refs)
     for k in range(2):
-        refs[9 + k][...] = dot_columns(d_seg0_ref[k], values[k][...])
-
-
-def sums_kernel(kept_ref, *refs):
-    out_ref = refs[-1]
-    share = kept_ref.shape[1] // 8
-    terms = kept_ref.shape[0] // (2 * share)
-    got, extra = refs[: 2 * terms], refs[2 * terms : -1]
-    for i in range(terms):
+        refs[10 + k][...] = dot_columns(d_seg0_ref[k], values[k][...])
+
+
+def early_sums_kernel(kept_ref, *refs):
+    got, out_ref = refs[:4], refs[4]
+    share = out_ref.shape[0] // 2
+    for i in range(2):
         there = kept_ref[pl.ds((2 * i + 1) * share, share), :]
         out_ref[pl.ds(i * share, share), :] = narrow(there + wide(got[2 * i + 1][...]))
-    for ref in extra:
-        depth = ref.shape[1]
-        piece = out_ref.shape[0] - terms * share
-        for i in range(ref.shape[0] // piece):
-            out_ref[pl.ds(terms * share, piece), pl.ds(i * depth, depth)] = narrow(
-                ref[pl.ds(i * piece, piece), :]
-            )
+
+
+def late_sums_kernel(there_ref, got_ref, square_ref, out_ref):
+    share = there_ref.shape[0]
+    out_ref[pl.ds(0, share), :] = narrow(there_ref[...] + wide(got_ref[...]))
+    depth = square_ref.shape[1]
+    piece = out_ref.shape[0] - share
+    for i in range(square_ref.shape[0] // piece):
+        out_ref[pl.ds(share, piece), pl.ds(i * depth, depth)] = narrow(
+            square_ref[pl.ds(i * piece, piece), :]
+        )
 
 
 def own_kernel(d_seg0_ref, d_gate_ref, weight_ref, *refs):
@@ -375,7 +379,7 @@
             partial_out[...] += row_sums(own * swapped[k][...], 1)
 
 
-TILE = 64
+TILE = 128
 
 
 def tile(columns, column_at=0, row_at=0):
@@ -444,6 +448,13 @@
         ]
     ).astype(jnp.int32)
 
+    coefs = jnp.concatenate(
+        [
+            jnp.where(flips[bit] == 1, twiddle_w[bit][::-1], twiddle_w[bit]).reshape(4, width)
+            for bit in range(3)
+        ]
+        + [jnp.zeros((4, width), jnp.float32)]
+    ).astype(bf16)
     full, full_hbm = shape_of(bf16, rows, width), in_hbm(bf16, rows, width)
     narrow_hbm = in_hbm(bf16, rows, width // 2)
     packed_rows = rows + mix.size // width
@@ -471,17 +482,10 @@
     outer_cotan = hop(after(grad_out, outer_pack), INWARD)
     across_cotan = hop(after(grad_out, outer_pack), ACROSS)
     far_cotan = hop(outer_cotan, ACROSS)
-    outer = block(1, outer_pack)
+    outer = block(1, after(outer_pack, coefs))
     across = block(3, after(across_pack, outer[0]))
     far = block(2, after(far_pack, outer_cotan, across[0]))
 
-    coefs = jnp.concatenate(
-        [
-            jnp.where(flips[bit] == 1, twiddle_w[bit][::-1], twiddle_w[bit]).reshape(4, width)
-            for bit in range(3)
-        ]
-        + [jnp.zeros((4, width), jnp.float32)]
-    ).astype(bf16)
     blocks = [own, outer, far, across]
     gates = [part[2] for part in blocks]
     seg0 = [own[3], outer[3], across[3], far[3], far[4]]
@@ -545,7 +549,7 @@
     )
     early_got = [hop(part, CORE_SWAP) for part in early_given]
     (early_sums,) = in_place(
-        sums_kernel, "early_sums", [after(early_kept, sent_mixed, *d_swapped), *early_got], shape_of(bf16, 2 * share, width)
+        early_sums_kernel, "early_sums", [after(early_kept, sent_mixed, *d_swapped), *early_got], shape_of(bf16, 2 * share, width)
     )
     sent_early = hop(early_sums, OUTWARD)
     d_seg0, first_part = kernel_call(
@@ -556,33 +560,33 @@
         out_specs=[stacked(4, width), whole(8, width)],
         out_shape=[shape_of(bf16, 4, rows, width), shape_of(f32, 8, width)],
     )(coefs, *d_seg1, after(d_swapped[0], early_sums), *d_swapped[1:], *seg0[:2], *swapped[:2])
-    *late_given, late_kept, own_square, outer_square = in_place(
-        value_grads_kernel,
-        "value_grads",
-        [d_seg0] + [part[1] for part in blocks] + [own[4], outer[4]],
-        *[shape_of(bf16, share, width)] * 2,
-        in_hbm(f32, 2 * share, width),
-        in_hbm(f32, rows, rows),
-        in_hbm(f32, rows, rows),
-    )
-    late_got = [hop(part, CORE_SWAP) for part in late_given]
-    (late_sums,) = in_place(
-        sums_kernel,
-        "late_sums",
-        [late_kept, *late_got, outer_square],
-        shape_of(bf16, share + rows * rows // width, width),
-    )
-    sent_late = hop(late_sums, OUTWARD)
     own_d_acts, outer_d_acts = in_place(
         own_kernel,
         "own_grads",
-        [after(d_seg0, late_sums, sent_early), d_gate, w_in, pack, outer_pack],
+        [d_seg0, d_gate, w_in, pack, outer_pack],
         full,
         full,
     )
     outer_handed = lax.ppermute(outer_d_acts, ("pipe", "seq"), relay_back(True))
     own_handed = lax.ppermute(own_d_acts, ("pipe", "seq"), relay_back(False))
-
+    *late_given, late_here, late_there, own_square, outer_square = in_place(
+        value_grads_kernel,
+        "value_grads",
+        [d_seg0, after(own[1], outer_d_acts)] + [part[1] for part in blocks[1:]] + [own[4], outer[4]],
+        *[shape_of(bf16, share, width)] * 2,
+        in_hbm(f32, share, width),
+        shape_of(f32, share, width),
+        in_hbm(f32, rows, rows),
+        shape_of(f32, rows, rows),
+    )
+    late_got = [hop(part, CORE_SWAP) for part in late_given]
+    (late_sums,) = in_place(
+        late_sums_kernel,
+        "late_sums",
+        [after(late_there, sent_early), late_got[1], outer_square],
+        shape_of(bf16, share + rows * rows // width, width),
+    )
+    sent_late = hop(late_sums, OUTWARD)
     def one_side(pair_terms, flip):
         empty = jnp.zeros_like(pair_terms)
         return jnp.where(
@@ -604,7 +608,7 @@
     terms = terms + hop(terms, ACROSS)
     twiddle_grad = jnp.where(inner, terms, hop(after(terms, sent_late), OUTWARD))
 
-    mixed_out = jnp.where(inner, own_mixed, after(sent_mixed, outer_d_acts))
+    mixed_out = jnp.where(inner, own_mixed, after(sent_mixed, sent_late))
     sent_early = after(sent_early, outer_d_acts)
 
     def share_of(kept, got, sent, at):
@@ -612,7 +616,7 @@
         return jnp.where(inner, mine, wide(sent[at * share : (at + 1) * share]))
 
     win_share = jnp.concatenate(
-        [share_of(late_kept, late_got, sent_late, 0), share_of(early_kept, early_got, sent_early, 0)],
+        [share_of(late_here, late_got, sent_late, 0), share_of(early_kept, early_got, sent_early, 0)],
         axis=1,
     )
     wout_share = share_of(early_kept, early_got, sent_early, 1)

time: 130 us -> 126 us (0.969)
  the two profiles are of different devices: /device:TPU:18 before, /device:TPU:4 now
where the time goes in v4:
time: 126 us; the launch traced here: 125 us
  Pallas kernels  45.1 us (36%)
  waiting for transfers between devices  32.9 us (26%)
  starting transfers between devices  27.3 us (22%)
  other arithmetic  9.23 us (7%)
  local copies, waits for them, and re-layouts  8.71 us (7%)
  between operations  1.39 us (1%)
    pallas_call x14, Pallas kernels, in_place(): kernel_call(kernel, name, work, room, in_specs=[pl.BlockSpec(memory_space...  35.2 us
    ppermute x27, waiting for transfers between devices, hop(): return lax.ppermute(value, 'seq', pairs)  26.8 us
    ppermute x27, starting transfers between devices, hop(): return lax.ppermute(value, 'seq', pairs)  24.6 us
    unnamed x88, local copies, waits for them, and re-layouts  7.77 us
    broadcast_in_dim x6, other arithmetic, on_device(): result[None]  7.27 us
    ppermute x1, waiting for transfers between devices, relay_plan(): outer_handed = lax.ppermute(outer_d_acts, ('pipe', 'seq'), relay_back(True))  6.03 us
    pallas_call x1, Pallas kernels, relay_plan(): kernel_call(forward_kernel, 'forward_segments', room=60, grid=(rows // TI...  5.67 us
  transfers between devices with their start and end apart: 29, of which 12 were waited for; matrix products, arithmetic and copies ran while one was open for 8% of the time, Pallas kernels for 34%

profile of v4, /device:TPU:4, one launch (start us, length us, event | category | flops | bytes accessed | tf_op | source)
XLA Modules:
  0.0 124.6 jit_solution(11394176131161890962)
XLA Ops:
  0.6 2.0 %pack.1.pack_ref.refs_0_ = bf16[320,1024]{1,0:T(8,128)(2,1)} custom-call(bf16[256,1024]{1,0:T(8,128)(2,1)} %bitcast.45, bf16[256,256]{1,0:T(8,128)(2,1)} %bitcast.46), custom_call_target="tpu_custom_call" | custom-call | flops 1 | bytes 1 | tf_op jit(solution)/shard_map/pack/pallas_call | solution.py:417
  2.6 3.5 %collective-permute-start = (bf16[320,1024]{1,0:T(8,128)(2,1)}, bf16[320,1024]{1,0:T(8,128)(2,1)S(1)}, u32[]{:S(2)}, u32[]{:S(2)}) collective-permute-start(bf16[320,1024]{1,0:T(8,128)(2,1)} %pack.1.pack_ref.refs_0_), channel_id=1, source_target_pairs={{0,2},{1,3},{6,4},{7,5},{8,10},{9,11},{14,12},{15,13},{16,18},{17,... | collective-permute-start | bytes 1966088 | tf_op jit(solution)/shard_map/ppermute | solution.py:152
  7.7 2.2 %copy-done = bf16[1,1024,2048]{2,1,0:T(8,128)(2,1)S(1)} copy-done((bf16[1,1024,2048]{2,1,0:T(8,128)(2,1)S(1)}, bf16[1,1024,2048]{2,1,0:T(8,128)(2,1)}, u32[]{:S(2)}) %copy-start) | copy-done | bytes 4194328
  11.0 3.3 %block_0.1 = (bf16[256,512]{1,0:T(8,128)(2,1)}, bf16[256,512]{1,0:T(8,128)(2,1)}, bf16[256,1024]{1,0:T(8,128)(2,1)}, bf16[256,1024]{1,0:T(8,128)(2,1)}, bf16[256,1024]{1,0:T(8,128)(2,1)}) custom-call(s32[4]{0:T(128)S(1)} %pad_add_fusion.starts_ref, bf16[320,1024]{1,0:T(8,128)(2,1)S(1)} %copy-done.4, bf16[1024,2048]{1,0:T(8,128)(2,1)S(1)} %bitcast.36), custom_call_target="tpu_custom_call" | custom-call | flops 1073741824 | bytes 1 | tf_op jit(solution)/shard_map/block_0/pallas_call | solution.py:417
  16.2 4.2 %collective-permute-done.pack_ref.refs_1_ = bf16[320,1024]{1,0:T(8,128)(2,1)S(1)} collective-permute-done((bf16[320,1024]{1,0:T(8,128)(2,1)}, bf16[320,1024]{1,0:T(8,128)(2,1)S(1)}, u32[]{:S(2)}, u32[]{:S(2)}) %collective-permute-start) | collective-permute-done | bytes 655392 | tf_op jit(solution)/shard_map/ppermute | solution.py:152
  20.4 5.1 %collective-permute-start.3 = (bf16[256,1024]{1,0:T(8,128)(2,1)}, bf16[256,1024]{1,0:T(8,128)(2,1)}, u32[]{:S(2)}, u32[]{:S(2)}) collective-permute-start(bf16[256,1024]{1,0:T(8,128)(2,1)} %bitcast.11.refs_0_.refs_6_), channel_id=1, source_target_pairs={{0,2},{1,3},{6,4},{7,5},{8,10},{9,11},{14,12},{15,13},{16,18},{17,... | collective-permute-start | bytes 1572872 | tf_op jit(solution)/shard_map/ppermute | solution.py:152
  29.4 2.2 %copy-done.1 = bf16[1,1024,2048]{2,1,0:T(8,128)(2,1)S(1)} copy-done((bf16[1,1024,2048]{2,1,0:T(8,128)(2,1)S(1)}, bf16[1,1024,2048]{2,1,0:T(8,128)(2,1)}, u32[]{:S(2)}) %copy-start.1) | copy-done | bytes 4194328
  31.6 3.4 %block_1.1 = (bf16[256,512]{1,0:T(8,128)(2,1)}, bf16[256,512]{1,0:T(8,128)(2,1)}, bf16[256,1024]{1,0:T(8,128)(2,1)}, bf16[256,1024]{1,0:T(8,128)(2,1)}, bf16[256,1024]{1,0:T(8,128)(2,1)}) custom-call(s32[4]{0:T(128)S(1)} %pad_add_fusion.starts_ref, bf16[320,1024]{1,0:T(8,128)(2,1)S(1)} %collective-permute-done.pack_ref.refs_1_, bf16[1024,2048]{1,0:T(8,128)(2,1)S(1)} %bitcast.37), custom_call_target="tpu_custom_call" | custom-call | flops 1 | bytes 1 | tf_op jit(solution)/shard_map/block_1/pallas_call | solution.py:417
  35.0 3.7 %block_3.1 = (bf16[256,512]{1,0:T(8,128)(2,1)}, bf16[256,512]{1,0:T(8,128)(2,1)}, bf16[256,1024]{1,0:T(8,128)(2,1)}, bf16[256,1024]{1,0:T(8,128)(2,1)}) custom-call(s32[4]{0:T(128)S(1)} %pad_add_fusion.starts_ref, bf16[320,1024]{1,0:T(8,128)(2,1)} %collective-permute-done.1.pack_ref, bf16[1024,2048]{1,0:T(8,128)(2,1)S(1)} %bitcast.38), custom_call_target="tpu_custom_call" | custom-call | flops 1 | bytes 1 | tf_op jit(solution)/shard_map/block_3/pallas_call | solution.py:417
  40.7 3.8 %block_2.1 = (bf16[256,512]{1,0:T(8,128)(2,1)}, bf16[256,512]{1,0:T(8,128)(2,1)}, bf16[256,1024]{1,0:T(8,128)(2,1)}, bf16[256,512]{1,0:T(8,128)(2,1)}, bf16[256,512]{1,0:T(8,128)(2,1)}) custom-call(s32[4]{0:T(128)S(1)} %pad_add_fusion.starts_ref, bf16[320,1024]{1,0:T(8,128)(2,1)} %collective-permute-done.2.pack_ref, bf16[1024,2048]{1,0:T(8,128)(2,1)S(1)} %bitcast.39), custom_call_target="tpu_custom_call" | custom-call | flops 1 | bytes 1 | tf_op jit(solution)/shard_map/block_2/pallas_call | solution.py:417
  46.9 5.7 %forward_segments.1 = (bf16[2,256,1024]{2,1,0:T(8,128)(2,1)}, bf16[4,256,1024]{2,1,0:T(8,128)(2,1)}, bf16[2,256,1024]{2,1,0:T(8,128)(2,1)}, bf16[4,256,512]{2,1,0:T(8,128)(2,1)}) custom-call(s32[4]{0:T(128)} %copy-done.31, bf16[16,1024]{1,0:T(8,128)(2,1)} %maximum_maximum_fusion.coef_ref, bf16[256,1024]{1,0:T(8,128)(2,1)} %get-tuple-element.71.refs_0_.refs_8_, ...), custom_call_target="tpu_custom_call" | custom-call | flops 1 | bytes 1 | tf_op jit(solution)/shard_map/forward_segments/pallas_call | solution.py:493
  56.6 2.6 %d_hidden.4 = (bf16[256,1024]{1,0:T(8,128)(2,1)S(1)}, bf16[256,1024]{1,0:T(8,128)(2,1)S(1)}) custom-call(bf16[1024,1024]{1,0:T(8,128)(2,1)S(1)} %bitcast.43, bf16[256,1024]{1,0:T(8,128)(2,1)} %collective-permute-done.3.refs_0_.refs_7_, bf16[256,1024]{1,0:T(8,128)(2,1)} %collective-permute-done.5.refs_1_.refs_9_), custom_call_target="tpu_custom_call" | custom-call | flops 1 | bytes 1 | tf_op jit(solution)/shard_map/d_hidden/pallas_call | solution.py:417
  59.3 1.9 %d_hidden.5.refs_2_ = bf16[256,1024]{1,0:T(8,128)(2,1)S(1)} custom-call(bf16[1024,1024]{1,0:T(8,128)(2,1)S(1)} %bitcast.44, bf16[256,1024]{1,0:T(8,128)(2,1)} %collective-permute-done.11.refs_0_.refs_8_), custom_call_target="tpu_custom_call" | custom-call | flops 1 | bytes 1 | tf_op jit(solution)/shard_map/d_hidden/pallas_call | solution.py:417
  61.4 2.2 %backward_segments.1 = (bf16[4,256,1024]{2,1,0:T(8,128)(2,1)S(1)}, bf16[256,1024]{1,0:T(8,128)(2,1)S(1)}, bf16[256,1024]{1,0:T(8,128)(2,1)S(1)}, bf16[256,1024]{...) custom-call(bf16[16,1024]{1,0:T(8,128)(2,1)S(1)} %copy-done.18, ...), custom_call_target="tpu_custom_call" | custom-call | flops 1 | bytes 1 | tf_op jit(solution)/shard_map/backward_segments/pallas_call | solution.py:530
  64.7 3.9 %early_grads.1 = (bf16[128,1024]{1,0:T(8,128)(2,1)S(1)}, bf16[128,1024]{1,0:T(8,128)(2,1)S(1)}, bf16[128,1024]{1,0:T(8,128)(2,1)S(1)}, bf16[128,1024]{1,0:T(8,128)(2,1)S(1)}, f32[512,1024]{1,0:T(8,128)S(1)}) custom-call(bf16[256,512]{1,0:T(8,128)(2,1)S(1)} %copy-done.27, bf16[256,512]{1,0:T(8,128)(2,1)S(1)} %copy-done.28, bf16[256,512]{1,0:T(8,128)(2,1)S(1)} %copy-done.30, ...), custom_call_target="tpu_custom_call" | custom-call | flops 1 | bytes 1 | tf_op jit(solution)/shard_map/early_grads/pallas_call | solution.py:417
  68.7 9.8 %collective-permute-done.10 = bf16[256,1024]{1,0:T(8,128)(2,1)S(1)} collective-permute-done((bf16[256,1024]{1,0:T(8,128)(2,1)S(1)}, bf16[256,1024]{1,0:T(8,128)(2,1)S(1)}, u32[]{:S(2)}, u32[]{:S(2)}) %collective-permute-start.10) | collective-permute-done | bytes 524320 | tf_op jit(solution)/shard_map/ppermute | solution.py:152
  83.6 2.0 %first_segment_grad.1 = (bf16[4,256,1024]{2,1,0:T(8,128)(2,1)S(1)}, f32[8,1024]{1,0:T(8,128)S(1)}) custom-call(bf16[16,1024]{1,0:T(8,128)(2,1)S(1)} %copy-done.18, bf16[256,1024]{1,0:T(8,128)(2,1)S(1)} %get-tuple-element.98.refs_0_, bf16[256,1024]{1,0:T(8,128)(2,1)S(1)} %get-tuple-element.99.refs_1_, bf16[256,1024]{1,0:T(8,128)(2,1)S(1)} %get-tuple-element.100.refs_2_, ...), custom_call_target="tpu_custom_call" | custom-call | flops 1 | bytes 1 | tf_op jit(solution)/shard_map/first_segment_grad/pallas_call | solution.py:555
  85.7 2.6 %own_grads.1 = (bf16[256,1024]{1,0:T(8,128)(2,1)S(1)}, bf16[256,1024]{1,0:T(8,128)(2,1)S(1)}) custom-call(bf16[4,256,1024]{2,1,0:T(8,128)(2,1)S(1)} %get-tuple-element.112.d_seg0_ref, bf16[4,256,1024]{2,1,0:T(8,128)(2,1)S(1)} %get-tuple-element.103.refs_4_.d_gate_ref, bf16[1024,2048]{1,0:T(8,128)(2,1)S(1)} %bitcast.40, bf16[320,1024]{1,0:T(8,128)(2,1)S(1)} %copy-done.5, ...), custom_call_target="tpu_custom_call" | custom-call | flops 1 | bytes 1 | tf_op jit(solution)/shard_map/own_grads/pallas_call | solution.py:417
  88.4 2.3 %value_grads.1 = (bf16[128,1024]{1,0:T(8,128)(2,1)S(1)}, bf16[128,1024]{1,0:T(8,128)(2,1)}, f32[128,1024]{1,0:T(8,128)}, f32[128,1024]{1,0:T(8,128)S(1)}, f32[256,256]{1,0:T(8,128)}, /*index=5*/f32[256,256]{1,0:T(8,128)S(1)}) custom-call(bf16[4,256,1024]{2,1,0:T(8,128)(2,1)S(1)} %get-tuple-element.112.d_seg0_ref, bf16[256,512]{1,0:T(8,128)(2,1)S(1)} %copy-done.23, ...), custom_call_target="tpu_custom_call" | custom-call | flops 1 | bytes 1 | tf_op jit(solution)/shard_map/value_grads/pallas_call | solution.py:417
  95.4 3.7 %collective-permute-done.20 = bf16[256,1024]{1,0:T(8,128)(2,1)} collective-permute-done((bf16[256,1024]{1,0:T(8,128)(2,1)}, bf16[256,1024]{1,0:T(8,128)(2,1)}, u32[]{:S(2)}, u32[]{:S(2)}) %collective-permute-start.20) | collective-permute-done | bytes 524320 | tf_op jit(solution)/shard_map/ppermute | solution.py:152
  102.4 2.1 %select_bitcast_fusion = (f32[1,128,1024]{2,1,0:T(8,128)}, f32[128,1024]{1,0:T(8,128)S(1)}) fusion(bf16[128,1024]{1,0:T(8,128)(2,1)S(1)} %collective-permute-done.18.refs_2_, f32[512,1024]{1,0:T(8,128)S(1)} %get-tuple-element.106.kept_ref, bf16[256,1024]{1,0:T(8,128)(2,1)} %collective-permute-done.20, pred[]{:T(512)S(6)} %or.3, ...), kind=kLoop, calls=%fused_computation.1 | loop fusion | flops 1048576 | bytes 3145729 | tf_op jit(solution)/shard_map/broadcast_in_dim | solution.py:633
  105.2 6.0 %collective-permute-done.24 = bf16[256,1024]{1,0:T(8,128)(2,1)} collective-permute-done((bf16[256,1024]{1,0:T(8,128)(2,1)}, bf16[256,1024]{1,0:T(8,128)(2,1)}, u32[]{:S(2)}, u32[]{:S(2)}) %collective-permute-start.24) | collective-permute-done | bytes 524320 | tf_op jit(solution)/shard_map/ppermute | solution.py:570
  111.3 1.9 %select_bitcast_fusion.1 = bf16[1,256,1024]{2,1,0:T(8,128)(2,1)} fusion(bf16[256,1024]{1,0:T(8,128)(2,1)} %collective-permute-done.23, bf16[256,1024]{1,0:T(8,128)(2,1)} %collective-permute-done.24, pred[]{:T(512)S(6)} %or.3), kind=kLoop, calls=%fused_computation.4 | loop fusion | flops 262144 | bytes 1572865 | tf_op jit(solution)/shard_map/broadcast_in_dim | solution.py:633
  113.2 4.8 %collective-permute-done.22 = bf16[192,1024]{1,0:T(8,128)(2,1)S(1)} collective-permute-done((bf16[192,1024]{1,0:T(8,128)(2,1)}, bf16[192,1024]{1,0:T(8,128)(2,1)S(1)}, u32[]{:S(2)}, u32[]{:S(2)}) %collective-permute-start.22) | collective-permute-done | bytes 393248 | tf_op jit(solution)/shard_map/ppermute | solution.py:152
  (167 shorter events, 38.3 us)
Async XLA Ops:
  2.6 17.8 %collective-permute-start = (bf16[320,1024]{1,0:T(8,128)(2,1)}, bf16[320,1024]{1,0:T(8,128)(2,1)S(1)}, u32[]{:S(2)}, u32[]{:S(2)}) collective-permute-start(bf16[320,1024]{1,0:T(8,128)(2,1)} %pack.1.pack_ref.refs_0_), channel_id=1, source_target_pairs={{0,2},{1,3},{6,4},{7,5},{8,10},{9,11},{14,12},{15,13},{16,18},{17,... | collective-permute-start | bytes 1966088 | tf_op jit(solution)/shard_map/ppermute | solution.py:152
  6.1 28.9 %collective-permute-start.1 = (bf16[320,1024]{1,0:T(8,128)(2,1)}, bf16[320,1024]{1,0:T(8,128)(2,1)}, u32[]{:S(2)}, u32[]{:S(2)}) collective-permute-start(bf16[320,1024]{1,0:T(8,128)(2,1)} %pack.1.pack_ref.refs_0_), channel_id=1, source_target_pairs={{2,4},{3,5},{4,2},{5,3},{10,12},{11,13},{12,10},{13,11},{18,20},{1... | collective-permute-start | bytes 1966088 | tf_op jit(solution)/shard_map/ppermute | solution.py:152
  14.3 30.2 %collective-permute-start.4 = (bf16[256,1024]{1,0:T(8,128)(2,1)}, bf16[256,1024]{1,0:T(8,128)(2,1)}, u32[]{:S(2)}, u32[]{:S(2)}) collective-permute-start(bf16[256,1024]{1,0:T(8,128)(2,1)} %get-tuple-element.71.refs_0_.refs_8_), channel_id=1, source_target_pairs={{0,1},{1,0},{2,3},{3,2},{4,5},{5,4},{6,7},{7,6},{8,9},{9,8},{10,11... | collective-permute-start | bytes 1572872 | tf_op jit(solution)/shard_map/ppermute | solution.py:152
  20.4 18.3 %collective-permute-start.3 = (bf16[256,1024]{1,0:T(8,128)(2,1)}, bf16[256,1024]{1,0:T(8,128)(2,1)}, u32[]{:S(2)}, u32[]{:S(2)}) collective-permute-start(bf16[256,1024]{1,0:T(8,128)(2,1)} %bitcast.11.refs_0_.refs_6_), channel_id=1, source_target_pairs={{0,2},{1,3},{6,4},{7,5},{8,10},{9,11},{14,12},{15,13},{16,18},{17,... | collective-permute-start | bytes 1572872 | tf_op jit(solution)/shard_map/ppermute | solution.py:152
  25.5 13.7 %collective-permute-start.2 = (bf16[320,1024]{1,0:T(8,128)(2,1)S(1)}, bf16[320,1024]{1,0:T(8,128)(2,1)}, u32[]{:S(2)}, u32[]{:S(2)}) collective-permute-start(bf16[320,1024]{1,0:T(8,128)(2,1)S(1)} %collective-permute-done.pack_ref.refs_1_), channel_id=1, source_target_pairs={{2,4},{3,5},{4,2},{5,3},{10,12},{11,13},{12,10},{13,11},{18,20},{1... | collective-permute-start | bytes 1966088 | tf_op jit(solution)/shard_map/ppermute | solution.py:152
  27.0 17.5 %collective-permute-start.5 = (bf16[256,1024]{1,0:T(8,128)(2,1)}, bf16[256,1024]{1,0:T(8,128)(2,1)}, u32[]{:S(2)}, u32[]{:S(2)}) collective-permute-start(bf16[256,1024]{1,0:T(8,128)(2,1)} %bitcast.11.refs_0_.refs_6_), channel_id=1, source_target_pairs={{2,4},{3,5},{4,2},{5,3},{10,12},{11,13},{12,10},{13,11},{18,20},{1... | collective-permute-start | bytes 1572872 | tf_op jit(solution)/shard_map/ppermute | solution.py:152
  35.0 10.0 %collective-permute-start.6 = (bf16[256,1024]{1,0:T(8,128)(2,1)}, bf16[256,1024]{1,0:T(8,128)(2,1)S(1)}, u32[]{:S(2)}, u32[]{:S(2)}) collective-permute-start(bf16[256,1024]{1,0:T(8,128)(2,1)} %get-tuple-element.73.refs_1_.refs_9_), channel_id=1, source_target_pairs={{0,1},{1,0},{2,3},{3,2},{4,5},{5,4},{6,7},{7,6},{8,9},{9,8},{10,11... | collective-permute-start | bytes 1572872 | tf_op jit(solution)/shard_map/ppermute | solution.py:152
  38.7 6.3 %collective-permute-start.7 = (bf16[256,1024]{1,0:T(8,128)(2,1)}, bf16[256,1024]{1,0:T(8,128)(2,1)}, u32[]{:S(2)}, u32[]{:S(2)}) collective-permute-start(bf16[256,1024]{1,0:T(8,128)(2,1)} %get-tuple-element.76.refs_2_), channel_id=1, source_target_pairs={{0,1},{1,0},{2,3},{3,2},{4,5},{5,4},{6,7},{7,6},{8,9},{9,8},{10,11... | collective-permute-start | bytes 1572872 | tf_op jit(solution)/shard_map/ppermute | solution.py:152
  39.2 20.1 %collective-permute-start.11 = (bf16[256,1024]{1,0:T(8,128)(2,1)}, bf16[256,1024]{1,0:T(8,128)(2,1)}, u32[]{:S(2)}, u32[]{:S(2)}) collective-permute-start(bf16[256,1024]{1,0:T(8,128)(2,1)} %collective-permute-done.3.refs_0_.refs_7_), channel_id=1, source_target_pairs={{2,4},{3,5},{4,2},{5,3},{10,12},{11,13},{12,10},{13,11},{18,20},{1... | collective-permute-start | bytes 1572872 | tf_op jit(solution)/shard_map/ppermute | solution.py:152
  44.5 2.2 %collective-permute-start.9 = (bf16[256,512]{1,0:T(8,128)(2,1)}, bf16[256,512]{1,0:T(8,128)(2,1)}, u32[]{:S(2)}, u32[]{:S(2)}) collective-permute-start(bf16[256,512]{1,0:T(8,128)(2,1)} %get-tuple-element.83.refs_4_), channel_id=1, source_target_pairs={{0,1},{1,0},{2,3},{3,2},{4,5},{5,4},{6,7},{7,6},{8,9},{9,8},{10,11... | collective-permute-start | bytes 786440 | tf_op jit(solution)/shard_map/ppermute | solution.py:152
  55.1 23.4 %collective-permute-start.10 = (bf16[256,1024]{1,0:T(8,128)(2,1)S(1)}, bf16[256,1024]{1,0:T(8,128)(2,1)S(1)}, u32[]{:S(2)}, u32[]{:S(2)}) collective-permute-start(bf16[256,1024]{1,0:T(8,128)(2,1)S(1)} %get-tuple-element.91), channel_id=1, source_target_pairs={{2,0},{3,1},{4,6},{5,7},{10,8},{11,9},{12,14},{13,15},{18,16},{19,... | collective-permute-start | bytes 1572872 | tf_op jit(solution)/shard_map/ppermute | solution.py:152
  63.6 14.9 %collective-permute-start.12 = (bf16[256,1024]{1,0:T(8,128)(2,1)S(1)}, bf16[256,1024]{1,0:T(8,128)(2,1)S(1)}, u32[]{:S(2)}, u32[]{:S(2)}) collective-permute-start(bf16[256,1024]{1,0:T(8,128)(2,1)S(1)} %get-tuple-element.98.refs_0_), channel_id=1, source_target_pairs={{0,1},{1,0},{2,3},{3,2},{4,5},{5,4},{6,7},{7,6},{8,9},{9,8},{10,11... | collective-permute-start | bytes 1572872 | tf_op jit(solution)/shard_map/ppermute | solution.py:152
  63.8 15.2 %collective-permute-start.13 = (bf16[256,1024]{1,0:T(8,128)(2,1)S(1)}, bf16[256,1024]{1,0:T(8,128)(2,1)S(1)}, u32[]{:S(2)}, u32[]{:S(2)}) collective-permute-start(bf16[256,1024]{1,0:T(8,128)(2,1)S(1)} %get-tuple-element.99.refs_1_), channel_id=1, source_target_pairs={{0,1},{1,0},{2,3},{3,2},{4,5},{5,4},{6,7},{7,6},{8,9},{9,8},{10,11... | collective-permute-start | bytes 1572872 | tf_op jit(solution)/shard_map/ppermute | solution.py:152
  64.2 14.9 %collective-permute-start.14 = (bf16[256,1024]{1,0:T(8,128)(2,1)S(1)}, bf16[256,1024]{1,0:T(8,128)(2,1)S(1)}, u32[]{:S(2)}, u32[]{:S(2)}) collective-permute-start(bf16[256,1024]{1,0:T(8,128)(2,1)S(1)} %get-tuple-element.100.refs_2_), channel_id=1, source_target_pairs={{0,1},{1,0},{2,3},{3,2},{4,5},{5,4},{6,7},{7,6},{8,9},{9,8},{10,11... | collective-permute-start | bytes 1572872 | tf_op jit(solution)/shard_map/ppermute | solution.py:152
  64.3 15.2 %collective-permute-start.15 = (bf16[256,1024]{1,0:T(8,128)(2,1)S(1)}, bf16[256,1024]{1,0:T(8,128)(2,1)S(1)}, u32[]{:S(2)}, u32[]{:S(2)}) collective-permute-start(bf16[256,1024]{1,0:T(8,128)(2,1)S(1)} %get-tuple-element.101.refs_3_), channel_id=1, source_target_pairs={{0,1},{1,0},{2,3},{3,2},{4,5},{5,4},{6,7},{7,6},{8,9},{9,8},{10,11... | collective-permute-start | bytes 1572872 | tf_op jit(solution)/shard_map/ppermute | solution.py:152
  82.0 17.1 %collective-permute-start.20 = (bf16[256,1024]{1,0:T(8,128)(2,1)}, bf16[256,1024]{1,0:T(8,128)(2,1)}, u32[]{:S(2)}, u32[]{:S(2)}) collective-permute-start(bf16[256,1024]{1,0:T(8,128)(2,1)} %early_sums.1), channel_id=1, source_target_pairs={{2,0},{3,1},{4,6},{5,7},{10,8},{11,9},{12,14},{13,15},{18,16},{19,... | collective-permute-start | bytes 1572872 | tf_op jit(solution)/shard_map/ppermute | solution.py:152
  91.4 7.7 %collective-permute-start.21 = (bf16[128,1024]{1,0:T(8,128)(2,1)}, bf16[128,1024]{1,0:T(8,128)(2,1)}, u32[]{:S(2)}, u32[]{:S(2)}) collective-permute-start(bf16[128,1024]{1,0:T(8,128)(2,1)} %get-tuple-element.123), channel_id=1, source_target_pairs={{0,1},{1,0},{2,3},{3,2},{4,5},{5,4},{6,7},{7,6},{8,9},{9,8},{10,11... | collective-permute-start | bytes 786440 | tf_op jit(solution)/shard_map/ppermute | solution.py:152
  91.5 19.7 %collective-permute-start.24 = (bf16[256,1024]{1,0:T(8,128)(2,1)}, bf16[256,1024]{1,0:T(8,128)(2,1)}, u32[]{:S(2)}, u32[]{:S(2)}) collective-permute-start(bf16[256,1024]{1,0:T(8,128)(2,1)} %copy-done.35), channel_id=1, source_target_pairs={{10,0},{11,1},{12,6},{13,7},{18,8},{19,9},{20,14},{21,15},{26,16},... | collective-permute-start | bytes 1572872 | tf_op jit(solution)/shard_map/ppermute | solution.py:570
  93.6 25.7 %collective-permute-start.25 = (bf16[128,1024]{1,0:T(8,128)(2,1)}, bf16[128,1024]{1,0:T(8,128)(2,1)}, u32[]{:S(2)}, u32[]{:S(2)}) collective-permute-start(bf16[128,1024]{1,0:T(8,128)(2,1)} %copy-done.37), channel_id=1, source_target_pairs={{0,1},{1,0},{2,3},{3,2},{4,5},{5,4},{6,7},{7,6},{8,9},{9,8},{10,11... | collective-permute-start | bytes 786440 | tf_op jit(solution)/shard_map/ppermute | solution.py:152
  94.0 11.3 %collective-permute-start.23 = (bf16[256,1024]{1,0:T(8,128)(2,1)}, bf16[256,1024]{1,0:T(8,128)(2,1)}, u32[]{:S(2)}, u32[]{:S(2)}) collective-permute-start(bf16[256,1024]{1,0:T(8,128)(2,1)} %copy-done.36), channel_id=1, source_target_pairs={{10,2},{11,3},{12,4},{13,5},{18,10},{19,11},{20,12},{21,13},{26,18... | collective-permute-start | bytes 1572872 | tf_op jit(solution)/shard_map/ppermute | solution.py:571
  100.9 17.1 %collective-permute-start.22 = (bf16[192,1024]{1,0:T(8,128)(2,1)}, bf16[192,1024]{1,0:T(8,128)(2,1)S(1)}, u32[]{:S(2)}, u32[]{:S(2)}) collective-permute-start(bf16[192,1024]{1,0:T(8,128)(2,1)} %late_sums.1), channel_id=1, source_target_pairs={{2,0},{3,1},{4,6},{5,7},{10,8},{11,9},{12,14},{13,15},{18,16},{19,... | collective-permute-start | bytes 1179656 | tf_op jit(solution)/shard_map/ppermute | solution.py:152
  102.3 2.2 %collective-permute-start.26 = (f32[3,2,2,1024]{3,2,1,0:T(2,128)S(1)}, f32[3,2,2,1024]{3,2,1,0:T(2,128)S(1)}, u32[]{:S(2)}, u32[]{:S(2)}) collective-permute-start(f32[3,2,2,1024]{3,2,1,0:T(2,128)S(1)} %pad_maximum_fusion), channel_id=1, source_target_pairs={{0,1},{1,0},{2,3},{3,2},{4,5},{5,4},{6,7},{7,6},{8,9},{9,8},{10,11... | collective-permute-start | bytes 147464 | tf_op jit(solution)/shard_map/ppermute | solution.py:152
  104.6 8.6 %collective-permute-start.27 = (f32[3,2,2,1024]{3,2,1,0:T(2,128)S(1)}, f32[3,2,2,1024]{3,2,1,0:T(2,128)S(1)}, u32[]{:S(2)}, u32[]{:S(2)}) collective-permute-start(f32[3,2,2,1024]{3,2,1,0:T(2,128)S(1)} %fusion.4), channel_id=1, source_target_pairs={{2,4},{3,5},{4,2},{5,3},{10,12},{11,13},{12,10},{13,11},{18,20},{1... | collective-permute-start | bytes 147464 | tf_op jit(solution)/shard_map/ppermute | solution.py:152
  118.0 6.0 %collective-permute-start.28 = (f32[3,2,2,1024]{3,2,1,0:T(2,128)S(1)}, f32[3,2,2,1024]{3,2,1,0:T(2,128)S(1)}, u32[]{:S(2)}, u32[]{:S(2)}) collective-permute-start(f32[3,2,2,1024]{3,2,1,0:T(2,128)S(1)} %fusion.6), channel_id=1, source_target_pairs={{2,0},{3,1},{4,6},{5,7},{10,8},{11,9},{12,14},{13,15},{18,16},{19,... | collective-permute-start | bytes 147464 | tf_op jit(solution)/shard_map/ppermute | solution.py:152
  (49 other events, 230.9 us)

commit v5 on v4

--- a/solution.py
+++ b/solution.py
@@ -473,7 +473,7 @@
             scalars=1,
         )
 
-    outer_pack, across_pack = hop(pack, INWARD), hop(pack, ACROSS)
+    outer_pack, across_pack = hop(pack, INWARD), hop(after(pack, coefs), ACROSS)
     own = block(0, pack, 4 * rows * width * width)
     (d_hidden_own,) = in_place(
         d_hidden_kernel, "d_hidden", [w_out, grad_out], full, work=2 * rows * width * width
@@ -481,10 +481,10 @@
     far_pack = hop(after(outer_pack, own[0], d_hidden_own), ACROSS)
     outer_cotan = hop(after(grad_out, outer_pack), INWARD)
     across_cotan = hop(after(grad_out, outer_pack), ACROSS)
-    far_cotan = hop(outer_cotan, ACROSS)
     outer = block(1, after(outer_pack, coefs))
     across = block(3, after(across_pack, outer[0]))
-    far = block(2, after(far_pack, outer_cotan, across[0]))
+    far = block(2, after(far_pack, across[0]))
+    far_cotan = hop(after(outer_cotan, far[0]), ACROSS)
 
     blocks = [own, outer, far, across]
     gates = [part[2] for part in blocks]
@@ -511,9 +511,9 @@
             shape_of(bf16, 4, rows, width // 2),
         ],
         scratch_shapes=[pltpu.VMEM((4, TILE, width), bf16)],
-    )(starts, coefs, *seg0, after(swapped[0], across_cotan), *swapped[1:], *gates)
+    )(starts, coefs, *seg0, *swapped, *gates)
     own_mixed, outer_mixed = in_place(
-        mixed_kernel, "mixed", [hidden, w_out], full, full
+        mixed_kernel, "mixed", [after(hidden, across_cotan), w_out], full, full
     )
     sent_mixed = hop(outer_mixed, OUTWARD)
 
@@ -605,8 +605,9 @@
         ]
     )
     terms = terms + hop(terms, CORE_SWAP)
+    terms = after(terms, outer_handed)
     terms = terms + hop(terms, ACROSS)
-    twiddle_grad = jnp.where(inner, terms, hop(after(terms, sent_late), OUTWARD))
+    twiddle_grad = jnp.where(inner, terms, hop(after(terms, late_sums), OUTWARD))
 
     mixed_out = jnp.where(inner, own_mixed, after(sent_mixed, sent_late))
     sent_early = after(sent_early, outer_d_acts)

time: 126 us -> 120 us (0.952)
  waiting for transfers between devices: 32.9 us -> 29.1 us
  Pallas kernels: 45.1 us -> 41.4 us
  starting transfers between devices: 27.3 us -> 28.6 us
    ppermute x27, waiting for transfers between devices: 26.8 us -> 21.9 us  [hop(): return lax.ppermute(value, 'seq', pairs)]
    pallas_call x14, Pallas kernels: 35.2 us -> 32.4 us  [in_place(): kernel_call(kernel, name, work, room, in_specs=[pl.BlockSpec(memory_space...]
    ppermute x27, starting transfers between devices: 24.6 us -> 25.9 us  [hop(): return lax.ppermute(value, 'seq', pairs)]
    unnamed x88 -> x92, local copies, waits for them, and re-layouts: 7.77 us -> 8.44 us
  transfers between devices with their start and end apart: 29 -> 29, of which waited for: 12 -> 11; matrix products, arithmetic and copies ran while one was open for 8% -> 5% of each run, Pallas kernels for 34% -> 33%
where the time goes in v5:
time: 120 us; the launch traced here: 118 us
  Pallas kernels  41.4 us (34%)
  waiting for transfers between devices  29.1 us (24%)
  starting transfers between devices  28.6 us (24%)
  local copies, waits for them, and re-layouts  9.38 us (8%)
  other arithmetic  8.24 us (7%)
  between operations  1.39 us (1%)
    pallas_call x14, Pallas kernels, in_place(): kernel_call(kernel, name, work, room, in_specs=[pl.BlockSpec(memory_space...  32.4 us
    ppermute x27, starting transfers between devices, hop(): return lax.ppermute(value, 'seq', pairs)  25.9 us
    ppermute x27, waiting for transfers between devices, hop(): return lax.ppermute(value, 'seq', pairs)  21.9 us
    unnamed x92, local copies, waits for them, and re-layouts  8.44 us
    broadcast_in_dim x6, other arithmetic, on_device(): result[None]  7.23 us
    ppermute x1, waiting for transfers between devices, relay_plan(): outer_handed = lax.ppermute(outer_d_acts, ('pipe', 'seq'), relay_back(True))  7.22 us
    pallas_call x1, Pallas kernels, relay_plan(): kernel_call(forward_kernel, 'forward_segments', room=60, grid=(rows // TI...  5.81 us
  transfers between devices with their start and end apart: 29, of which 11 were waited for; matrix products, arithmetic and copies ran while one was open for 5% of the time, Pallas kernels for 33%

profile of v5, /device:TPU:4, one launch (start us, length us, event | category | flops | bytes accessed | tf_op | source)
XLA Modules:
  0.0 118.2 jit_solution(1562011060378581519)
XLA Ops:
  0.6 1.9 %pack.1.pack_ref.refs_0_ = bf16[320,1024]{1,0:T(8,128)(2,1)} custom-call(bf16[256,1024]{1,0:T(8,128)(2,1)} %bitcast.45, bf16[256,256]{1,0:T(8,128)(2,1)} %bitcast.46), custom_call_target="tpu_custom_call" | custom-call | flops 1 | bytes 1 | tf_op jit(solution)/shard_map/pack/pallas_call | solution.py:417
  2.6 3.5 %collective-permute-start = (bf16[320,1024]{1,0:T(8,128)(2,1)}, bf16[320,1024]{1,0:T(8,128)(2,1)S(1)}, u32[]{:S(2)}, u32[]{:S(2)}) collective-permute-start(bf16[320,1024]{1,0:T(8,128)(2,1)} %pack.1.pack_ref.refs_0_), channel_id=1, source_target_pairs={{0,2},{1,3},{6,4},{7,5},{8,10},{9,11},{14,12},{15,13},{16,18},{17,... | collective-permute-start | bytes 1966088 | tf_op jit(solution)/shard_map/ppermute | solution.py:152
  8.6 2.2 %copy-done = bf16[1,1024,2048]{2,1,0:T(8,128)(2,1)S(1)} copy-done((bf16[1,1024,2048]{2,1,0:T(8,128)(2,1)S(1)}, bf16[1,1024,2048]{2,1,0:T(8,128)(2,1)}, u32[]{:S(2)}) %copy-start) | copy-done | bytes 4194328
  11.8 3.3 %block_0.1 = (bf16[256,512]{1,0:T(8,128)(2,1)}, bf16[256,512]{1,0:T(8,128)(2,1)}, bf16[256,1024]{1,0:T(8,128)(2,1)}, bf16[256,1024]{1,0:T(8,128)(2,1)}, bf16[256,1024]{1,0:T(8,128)(2,1)}) custom-call(s32[4]{0:T(128)S(1)} %pad_add_fusion.starts_ref, bf16[320,1024]{1,0:T(8,128)(2,1)S(1)} %copy-done.5, bf16[1024,2048]{1,0:T(8,128)(2,1)S(1)} %bitcast.36), custom_call_target="tpu_custom_call" | custom-call | flops 1073741824 | bytes 1 | tf_op jit(solution)/shard_map/block_0/pallas_call | solution.py:417
  15.2 1.6 %copy-done.3 = bf16[1,1024,1024]{2,1,0:T(8,128)(2,1)S(1)} copy-done((bf16[1,1024,1024]{2,1,0:T(8,128)(2,1)S(1)}, bf16[1,1024,1024]{2,1,0:T(8,128)(2,1)}, u32[]{:S(2)}) %copy-start.3) | copy-done | bytes 2097176
  16.8 1.8 %d_hidden.3.refs_0_ = bf16[256,1024]{1,0:T(8,128)(2,1)S(1)} custom-call(bf16[1024,1024]{1,0:T(8,128)(2,1)S(1)} %bitcast.41, bf16[256,1024]{1,0:T(8,128)(2,1)} %bitcast.11.refs_0_.refs_6_), custom_call_target="tpu_custom_call" | custom-call | flops 536870912 | bytes 1 | tf_op jit(solution)/shard_map/d_hidden/pallas_call | solution.py:417
  18.6 1.7 %collective-permute-done.pack_ref.refs_1_ = bf16[320,1024]{1,0:T(8,128)(2,1)S(1)} collective-permute-done((bf16[320,1024]{1,0:T(8,128)(2,1)}, bf16[320,1024]{1,0:T(8,128)(2,1)S(1)}, u32[]{:S(2)}, u32[]{:S(2)}) %collective-permute-start) | collective-permute-done | bytes 655392 | tf_op jit(solution)/shard_map/ppermute | solution.py:152
  21.0 7.9 %collective-permute-start.10 = (bf16[256,1024]{1,0:T(8,128)(2,1)}, bf16[256,1024]{1,0:T(8,128)(2,1)}, u32[]{:S(2)}, u32[]{:S(2)}) collective-permute-start(bf16[256,1024]{1,0:T(8,128)(2,1)} %bitcast.11.refs_0_.refs_6_), channel_id=1, source_target_pairs={{0,2},{1,3},{6,4},{7,5},{8,10},{9,11},{14,12},{15,13},{16,18},{17,... | collective-permute-start | bytes 1572872 | tf_op jit(solution)/shard_map/ppermute | solution.py:152
  28.9 3.4 %block_1.1 = (bf16[256,512]{1,0:T(8,128)(2,1)}, bf16[256,512]{1,0:T(8,128)(2,1)}, bf16[256,1024]{1,0:T(8,128)(2,1)}, bf16[256,1024]{1,0:T(8,128)(2,1)}, bf16[256,1024]{1,0:T(8,128)(2,1)}) custom-call(s32[4]{0:T(128)S(1)} %pad_add_fusion.starts_ref, bf16[320,1024]{1,0:T(8,128)(2,1)S(1)} %collective-permute-done.pack_ref.refs_1_, bf16[1024,2048]{1,0:T(8,128)(2,1)S(1)} %bitcast.37), custom_call_target="tpu_custom_call" | custom-call | flops 1 | bytes 1 | tf_op jit(solution)/shard_map/block_1/pallas_call | solution.py:417
  32.8 3.2 %block_3.1 = (bf16[256,512]{1,0:T(8,128)(2,1)}, bf16[256,512]{1,0:T(8,128)(2,1)}, bf16[256,1024]{1,0:T(8,128)(2,1)}, bf16[256,1024]{1,0:T(8,128)(2,1)}) custom-call(s32[4]{0:T(128)S(1)} %pad_add_fusion.starts_ref, bf16[320,1024]{1,0:T(8,128)(2,1)S(1)} %collective-permute-done.1.pack_ref, bf16[1024,2048]{1,0:T(8,128)(2,1)S(1)} %bitcast.38), custom_call_target="tpu_custom_call" | custom-call | flops 1 | bytes 1 | tf_op jit(solution)/shard_map/block_3/pallas_call | solution.py:417
  37.5 3.2 %block_2.1 = (bf16[256,512]{1,0:T(8,128)(2,1)}, bf16[256,512]{1,0:T(8,128)(2,1)}, bf16[256,1024]{1,0:T(8,128)(2,1)}, bf16[256,512]{1,0:T(8,128)(2,1)}, bf16[256,512]{1,0:T(8,128)(2,1)}) custom-call(s32[4]{0:T(128)S(1)} %pad_add_fusion.starts_ref, bf16[320,1024]{1,0:T(8,128)(2,1)S(1)} %collective-permute-done.2.pack_ref, bf16[1024,2048]{1,0:T(8,128)(2,1)S(1)} %bitcast.39), custom_call_target="tpu_custom_call" | custom-call | flops 1 | bytes 1 | tf_op jit(solution)/shard_map/block_2/pallas_call | solution.py:417
  45.2 5.8 %forward_segments.1 = (bf16[2,256,1024]{2,1,0:T(8,128)(2,1)}, bf16[4,256,1024]{2,1,0:T(8,128)(2,1)}, bf16[2,256,1024]{2,1,0:T(8,128)(2,1)}, bf16[4,256,512]{2,1,0:T(8,128)(2,1)}) custom-call(s32[4]{0:T(128)} %copy-done.36, bf16[16,1024]{1,0:T(8,128)(2,1)} %maximum_maximum_fusion.coef_ref, bf16[256,1024]{1,0:T(8,128)(2,1)} %get-tuple-element.74.refs_0_.refs_8_, ...), custom_call_target="tpu_custom_call" | custom-call | flops 1 | bytes 1 | tf_op jit(solution)/shard_map/forward_segments/pallas_call | solution.py:493
  55.0 2.6 %d_hidden.4 = (bf16[256,1024]{1,0:T(8,128)(2,1)S(1)}, bf16[256,1024]{1,0:T(8,128)(2,1)S(1)}) custom-call(bf16[1024,1024]{1,0:T(8,128)(2,1)S(1)} %bitcast.43, bf16[256,1024]{1,0:T(8,128)(2,1)} %collective-permute-done.10.refs_0_.refs_7_, bf16[256,1024]{1,0:T(8,128)(2,1)} %collective-permute-done.8.refs_1_.refs_9_), custom_call_target="tpu_custom_call" | custom-call | flops 1 | bytes 1 | tf_op jit(solution)/shard_map/d_hidden/pallas_call | solution.py:417
  57.7 1.9 %d_hidden.5.refs_2_ = bf16[256,1024]{1,0:T(8,128)(2,1)S(1)} custom-call(bf16[1024,1024]{1,0:T(8,128)(2,1)S(1)} %bitcast.44, bf16[256,1024]{1,0:T(8,128)(2,1)} %collective-permute-done.11.refs_0_.refs_8_), custom_call_target="tpu_custom_call" | custom-call | flops 1 | bytes 1 | tf_op jit(solution)/shard_map/d_hidden/pallas_call | solution.py:417
  59.8 2.2 %backward_segments.1 = (bf16[4,256,1024]{2,1,0:T(8,128)(2,1)S(1)}, bf16[256,1024]{1,0:T(8,128)(2,1)S(1)}, bf16[256,1024]{1,0:T(8,128)(2,1)S(1)}, bf16[256,1024]{...) custom-call(bf16[16,1024]{1,0:T(8,128)(2,1)S(1)} %copy-done.22, ...), custom_call_target="tpu_custom_call" | custom-call | flops 1 | bytes 1 | tf_op jit(solution)/shard_map/backward_segments/pallas_call | solution.py:530
  63.1 3.9 %early_grads.1 = (bf16[128,1024]{1,0:T(8,128)(2,1)S(1)}, bf16[128,1024]{1,0:T(8,128)(2,1)S(1)}, bf16[128,1024]{1,0:T(8,128)(2,1)S(1)}, bf16[128,1024]{1,0:T(8,128)(2,1)S(1)}, f32[512,1024]{1,0:T(8,128)S(1)}) custom-call(bf16[256,512]{1,0:T(8,128)(2,1)S(1)} %copy-done.32, bf16[256,512]{1,0:T(8,128)(2,1)S(1)} %copy-done.33, bf16[256,512]{1,0:T(8,128)(2,1)S(1)} %copy-done.35, ...), custom_call_target="tpu_custom_call" | custom-call | flops 1 | bytes 1 | tf_op jit(solution)/shard_map/early_grads/pallas_call | solution.py:417
  67.0 7.0 %collective-permute-done.9 = bf16[256,1024]{1,0:T(8,128)(2,1)S(1)} collective-permute-done((bf16[256,1024]{1,0:T(8,128)(2,1)S(1)}, bf16[256,1024]{1,0:T(8,128)(2,1)S(1)}, u32[]{:S(2)}, u32[]{:S(2)}) %collective-permute-start.9) | collective-permute-done | bytes 524320 | tf_op jit(solution)/shard_map/ppermute | solution.py:152
  79.6 3.4 %own_grads.1 = (bf16[256,1024]{1,0:T(8,128)(2,1)S(1)}, bf16[256,1024]{1,0:T(8,128)(2,1)}) custom-call(bf16[4,256,1024]{2,1,0:T(8,128)(2,1)S(1)} %get-tuple-element.117.d_seg0_ref, bf16[4,256,1024]{2,1,0:T(8,128)(2,1)S(1)} %get-tuple-element.108.refs_4_.d_gate_ref, bf16[1024,2048]{1,0:T(8,128)(2,1)S(1)} %bitcast.40, bf16[320,1024]{1,0:T(8,128)(2,1)S(1)} %copy-done.6, ...), custom_call_target="tpu_custom_call" | custom-call | flops 1 | bytes 1 | tf_op jit(solution)/shard_map/own_grads/pallas_call | solution.py:417
  83.0 2.2 %value_grads.1 = (bf16[128,1024]{1,0:T(8,128)(2,1)S(1)}, bf16[128,1024]{1,0:T(8,128)(2,1)S(1)}, f32[128,1024]{1,0:T(8,128)}, f32[128,1024]{1,0:T(8,128)S(1)}, f3...) custom-call(bf16[4,256,1024]{2,1,0:T(8,128)(2,1)S(1)} %get-tuple-element.117.d_seg0_ref, bf16[256,512]{1,0:T(8,128)(2,1)S(1)} %copy-done.28, ...), custom_call_target="tpu_custom_call" | custom-call | flops 1 | bytes 1 | tf_op jit(solution)/shard_map/value_grads/pallas_call | solution.py:417
  86.7 7.0 %collective-permute-done.20 = bf16[256,1024]{1,0:T(8,128)(2,1)S(1)} collective-permute-done((bf16[256,1024]{1,0:T(8,128)(2,1)S(1)}, bf16[256,1024]{1,0:T(8,128)(2,1)S(1)}, u32[]{:S(2)}, u32[]{:S(2)}) %collective-permute-start.20) | collective-permute-done | bytes 524320 | tf_op jit(solution)/shard_map/ppermute | solution.py:152
  98.8 7.2 %collective-permute-done.24 = bf16[256,1024]{1,0:T(8,128)(2,1)} collective-permute-done((bf16[256,1024]{1,0:T(8,128)(2,1)}, bf16[256,1024]{1,0:T(8,128)(2,1)}, u32[]{:S(2)}, u32[]{:S(2)}) %collective-permute-start.24) | collective-permute-done | bytes 524320 | tf_op jit(solution)/shard_map/ppermute | solution.py:570
  106.7 2.1 %select_bitcast_fusion = (f32[1,128,1024]{2,1,0:T(8,128)}, f32[128,1024]{1,0:T(8,128)S(1)}) fusion(bf16[128,1024]{1,0:T(8,128)(2,1)S(1)} %collective-permute-done.18.refs_2_, f32[512,1024]{1,0:T(8,128)S(1)} %get-tuple-element.111.kept_ref, bf16[256,1024]{1,0:T(8,128)(2,1)} %copy-done.42, pred[]{:T(512)S(6)} %or.3, ...), kind=kLoop, calls=%fused_computation.1 | loop fusion | flops 1048576 | bytes 3145729 | tf_op jit(solution)/shard_map/broadcast_in_dim | solution.py:634
  110.1 1.9 %select_bitcast_fusion.1 = bf16[1,256,1024]{2,1,0:T(8,128)(2,1)} fusion(bf16[256,1024]{1,0:T(8,128)(2,1)} %collective-permute-done.23, bf16[256,1024]{1,0:T(8,128)(2,1)} %collective-permute-done.24, pred[]{:T(512)S(6)} %or.3), kind=kLoop, calls=%fused_computation.4 | loop fusion | flops 262144 | bytes 1572865 | tf_op jit(solution)/shard_map/broadcast_in_dim | solution.py:634
  112.0 2.8 %collective-permute-done.28 = f32[3,2,2,1024]{3,2,1,0:T(2,128)S(1)} collective-permute-done((f32[3,2,2,1024]{3,2,1,0:T(2,128)S(1)}, f32[3,2,2,1024]{3,2,1,0:T(2,128)S(1)}, u32[]{:S(2)}, u32[]{:S(2)}) %collective-permute-start.28) | collective-permute-done | bytes 49184 | tf_op jit(solution)/shard_map/ppermute | solution.py:152
  (171 shorter events, 32.9 us)
Async XLA Ops:
  2.6 17.8 %collective-permute-start = (bf16[320,1024]{1,0:T(8,128)(2,1)}, bf16[320,1024]{1,0:T(8,128)(2,1)S(1)}, u32[]{:S(2)}, u32[]{:S(2)}) collective-permute-start(bf16[320,1024]{1,0:T(8,128)(2,1)} %pack.1.pack_ref.refs_0_), channel_id=1, source_target_pairs={{0,2},{1,3},{6,4},{7,5},{8,10},{9,11},{14,12},{15,13},{16,18},{17,... | collective-permute-start | bytes 1966088 | tf_op jit(solution)/shard_map/ppermute | solution.py:152
  7.8 25.0 %collective-permute-start.1 = (bf16[320,1024]{1,0:T(8,128)(2,1)}, bf16[320,1024]{1,0:T(8,128)(2,1)S(1)}, u32[]{:S(2)}, u32[]{:S(2)}) collective-permute-start(bf16[320,1024]{1,0:T(8,128)(2,1)} %pack.1.pack_ref.refs_0_), channel_id=1, source_target_pairs={{2,4},{3,5},{4,2},{5,3},{10,12},{11,13},{12,10},{13,11},{18,20},{1... | collective-permute-start | bytes 1966088 | tf_op jit(solution)/shard_map/ppermute | solution.py:152
  20.3 15.6 %collective-permute-start.2 = (bf16[320,1024]{1,0:T(8,128)(2,1)S(1)}, bf16[320,1024]{1,0:T(8,128)(2,1)S(1)}, u32[]{:S(2)}, u32[]{:S(2)}) collective-permute-start(bf16[320,1024]{1,0:T(8,128)(2,1)S(1)} %collective-permute-done.pack_ref.refs_1_), channel_id=1, source_target_pairs={{2,4},{3,5},{4,2},{5,3},{10,12},{11,13},{12,10},{13,11},{18,20},{1... | collective-permute-start | bytes 1966088 | tf_op jit(solution)/shard_map/ppermute | solution.py:152
  21.0 19.7 %collective-permute-start.10 = (bf16[256,1024]{1,0:T(8,128)(2,1)}, bf16[256,1024]{1,0:T(8,128)(2,1)}, u32[]{:S(2)}, u32[]{:S(2)}) collective-permute-start(bf16[256,1024]{1,0:T(8,128)(2,1)} %bitcast.11.refs_0_.refs_6_), channel_id=1, source_target_pairs={{0,2},{1,3},{6,4},{7,5},{8,10},{9,11},{14,12},{15,13},{16,18},{17,... | collective-permute-start | bytes 1572872 | tf_op jit(solution)/shard_map/ppermute | solution.py:152
  28.9 13.3 %collective-permute-start.3 = (bf16[256,1024]{1,0:T(8,128)(2,1)S(1)}, bf16[256,1024]{1,0:T(8,128)(2,1)S(1)}, u32[]{:S(2)}, u32[]{:S(2)}) collective-permute-start(bf16[256,1024]{1,0:T(8,128)(2,1)S(1)} %copy-done.12), channel_id=1, source_target_pairs={{0,1},{1,0},{2,3},{3,2},{4,5},{5,4},{6,7},{7,6},{8,9},{9,8},{10,11... | collective-permute-start | bytes 1572872 | tf_op jit(solution)/shard_map/ppermute | solution.py:152
  32.3 10.4 %collective-permute-start.4 = (bf16[256,1024]{1,0:T(8,128)(2,1)}, bf16[256,1024]{1,0:T(8,128)(2,1)S(1)}, u32[]{:S(2)}, u32[]{:S(2)}) collective-permute-start(bf16[256,1024]{1,0:T(8,128)(2,1)} %get-tuple-element.76.refs_1_.refs_9_), channel_id=1, source_target_pairs={{0,1},{1,0},{2,3},{3,2},{4,5},{5,4},{6,7},{7,6},{8,9},{9,8},{10,11... | collective-permute-start | bytes 1572872 | tf_op jit(solution)/shard_map/ppermute | solution.py:152
  36.0 6.8 %collective-permute-start.5 = (bf16[256,1024]{1,0:T(8,128)(2,1)}, bf16[256,1024]{1,0:T(8,128)(2,1)S(1)}, u32[]{:S(2)}, u32[]{:S(2)}) collective-permute-start(bf16[256,1024]{1,0:T(8,128)(2,1)} %get-tuple-element.80.refs_2_), channel_id=1, source_target_pairs={{0,1},{1,0},{2,3},{3,2},{4,5},{5,4},{6,7},{7,6},{8,9},{9,8},{10,11... | collective-permute-start | bytes 1572872 | tf_op jit(solution)/shard_map/ppermute | solution.py:152
  36.0 15.0 %collective-permute-start.8 = (bf16[256,1024]{1,0:T(8,128)(2,1)}, bf16[256,1024]{1,0:T(8,128)(2,1)}, u32[]{:S(2)}, u32[]{:S(2)}) collective-permute-start(bf16[256,1024]{1,0:T(8,128)(2,1)} %bitcast.11.refs_0_.refs_6_), channel_id=1, source_target_pairs={{2,4},{3,5},{4,2},{5,3},{10,12},{11,13},{12,10},{13,11},{18,20},{1... | collective-permute-start | bytes 1572872 | tf_op jit(solution)/shard_map/ppermute | solution.py:152
  40.7 17.0 %collective-permute-start.11 = (bf16[256,1024]{1,0:T(8,128)(2,1)}, bf16[256,1024]{1,0:T(8,128)(2,1)}, u32[]{:S(2)}, u32[]{:S(2)}) collective-permute-start(bf16[256,1024]{1,0:T(8,128)(2,1)} %collective-permute-done.10.refs_0_.refs_7_), channel_id=1, source_target_pairs={{2,4},{3,5},{4,2},{5,3},{10,12},{11,13},{12,10},{13,11},{18,20},{1... | collective-permute-start | bytes 1572872 | tf_op jit(solution)/shard_map/ppermute | solution.py:152
  53.5 20.6 %collective-permute-start.9 = (bf16[256,1024]{1,0:T(8,128)(2,1)S(1)}, bf16[256,1024]{1,0:T(8,128)(2,1)S(1)}, u32[]{:S(2)}, u32[]{:S(2)}) collective-permute-start(bf16[256,1024]{1,0:T(8,128)(2,1)S(1)} %get-tuple-element.95), channel_id=1, source_target_pairs={{2,0},{3,1},{4,6},{5,7},{10,8},{11,9},{12,14},{13,15},{18,16},{19,... | collective-permute-start | bytes 1572872 | tf_op jit(solution)/shard_map/ppermute | solution.py:152
  62.0 12.1 %collective-permute-start.12 = (bf16[256,1024]{1,0:T(8,128)(2,1)S(1)}, bf16[256,1024]{1,0:T(8,128)(2,1)S(1)}, u32[]{:S(2)}, u32[]{:S(2)}) collective-permute-start(bf16[256,1024]{1,0:T(8,128)(2,1)S(1)} %get-tuple-element.104.refs_0_), channel_id=1, source_target_pairs={{0,1},{1,0},{2,3},{3,2},{4,5},{5,4},{6,7},{7,6},{8,9},{9,8},{10,11... | collective-permute-start | bytes 1572872 | tf_op jit(solution)/shard_map/ppermute | solution.py:152
  62.4 12.1 %collective-permute-start.13 = (bf16[256,1024]{1,0:T(8,128)(2,1)S(1)}, bf16[256,1024]{1,0:T(8,128)(2,1)S(1)}, u32[]{:S(2)}, u32[]{:S(2)}) collective-permute-start(bf16[256,1024]{1,0:T(8,128)(2,1)S(1)} %get-tuple-element.105.refs_1_), channel_id=1, source_target_pairs={{0,1},{1,0},{2,3},{3,2},{4,5},{5,4},{6,7},{7,6},{8,9},{9,8},{10,11... | collective-permute-start | bytes 1572872 | tf_op jit(solution)/shard_map/ppermute | solution.py:152
  62.6 12.1 %collective-permute-start.14 = (bf16[256,1024]{1,0:T(8,128)(2,1)S(1)}, bf16[256,1024]{1,0:T(8,128)(2,1)S(1)}, u32[]{:S(2)}, u32[]{:S(2)}) collective-permute-start(bf16[256,1024]{1,0:T(8,128)(2,1)S(1)} %get-tuple-element.106.refs_2_), channel_id=1, source_target_pairs={{0,1},{1,0},{2,3},{3,2},{4,5},{5,4},{6,7},{7,6},{8,9},{9,8},{10,11... | collective-permute-start | bytes 1572872 | tf_op jit(solution)/shard_map/ppermute | solution.py:152
  62.9 12.2 %collective-permute-start.15 = (bf16[256,1024]{1,0:T(8,128)(2,1)S(1)}, bf16[256,1024]{1,0:T(8,128)(2,1)S(1)}, u32[]{:S(2)}, u32[]{:S(2)}) collective-permute-start(bf16[256,1024]{1,0:T(8,128)(2,1)S(1)} %get-tuple-element.107.refs_3_), channel_id=1, source_target_pairs={{0,1},{1,0},{2,3},{3,2},{4,5},{5,4},{6,7},{7,6},{8,9},{9,8},{10,11... | collective-permute-start | bytes 1572872 | tf_op jit(solution)/shard_map/ppermute | solution.py:152
  74.7 2.1 %collective-permute-start.19 = (bf16[128,1024]{1,0:T(8,128)(2,1)S(1)}, bf16[128,1024]{1,0:T(8,128)(2,1)S(1)}, u32[]{:S(2)}, u32[]{:S(2)}) collective-permute-start(bf16[128,1024]{1,0:T(8,128)(2,1)S(1)} %get-tuple-element.115), channel_id=1, source_target_pairs={{0,1},{1,0},{2,3},{3,2},{4,5},{5,4},{6,7},{7,6},{8,9},{9,8},{10,11... | collective-permute-start | bytes 786440 | tf_op jit(solution)/shard_map/ppermute | solution.py:152
  76.8 16.9 %collective-permute-start.20 = (bf16[256,1024]{1,0:T(8,128)(2,1)S(1)}, bf16[256,1024]{1,0:T(8,128)(2,1)S(1)}, u32[]{:S(2)}, u32[]{:S(2)}) collective-permute-start(bf16[256,1024]{1,0:T(8,128)(2,1)S(1)} %early_sums.1), channel_id=1, source_target_pairs={{2,0},{3,1},{4,6},{5,7},{10,8},{11,9},{12,14},{13,15},{18,16},{19,... | collective-permute-start | bytes 1572872 | tf_op jit(solution)/shard_map/ppermute | solution.py:152
  85.3 8.5 %collective-permute-start.21 = (bf16[128,1024]{1,0:T(8,128)(2,1)S(1)}, bf16[128,1024]{1,0:T(8,128)(2,1)S(1)}, u32[]{:S(2)}, u32[]{:S(2)}) collective-permute-start(bf16[128,1024]{1,0:T(8,128)(2,1)S(1)} %get-tuple-element.128), channel_id=1, source_target_pairs={{0,1},{1,0},{2,3},{3,2},{4,5},{5,4},{6,7},{7,6},{8,9},{9,8},{10,11... | collective-permute-start | bytes 786440 | tf_op jit(solution)/shard_map/ppermute | solution.py:152
  85.4 20.6 %collective-permute-start.24 = (bf16[256,1024]{1,0:T(8,128)(2,1)}, bf16[256,1024]{1,0:T(8,128)(2,1)}, u32[]{:S(2)}, u32[]{:S(2)}) collective-permute-start(bf16[256,1024]{1,0:T(8,128)(2,1)} %get-tuple-element.119), channel_id=1, source_target_pairs={{10,0},{11,1},{12,6},{13,7},{18,8},{19,9},{20,14},{21,15},{26,16},... | collective-permute-start | bytes 1572872 | tf_op jit(solution)/shard_map/ppermute | solution.py:570
  95.4 3.3 %collective-permute-start.26 = (f32[3,2,2,1024]{3,2,1,0:T(2,128)S(1)}, f32[3,2,2,1024]{3,2,1,0:T(2,128)S(1)}, u32[]{:S(2)}, u32[]{:S(2)}) collective-permute-start(f32[3,2,2,1024]{3,2,1,0:T(2,128)S(1)} %pad_maximum_fusion), channel_id=1, source_target_pairs={{0,1},{1,0},{2,3},{3,2},{4,5},{5,4},{6,7},{7,6},{8,9},{9,8},{10,11... | collective-permute-start | bytes 147464 | tf_op jit(solution)/shard_map/ppermute | solution.py:152
  95.5 14.6 %collective-permute-start.23 = (bf16[256,1024]{1,0:T(8,128)(2,1)}, bf16[256,1024]{1,0:T(8,128)(2,1)}, u32[]{:S(2)}, u32[]{:S(2)}) collective-permute-start(bf16[256,1024]{1,0:T(8,128)(2,1)} %copy-done.37), channel_id=1, source_target_pairs={{10,2},{11,3},{12,4},{13,5},{18,10},{19,11},{20,12},{21,13},{26,18... | collective-permute-start | bytes 1572872 | tf_op jit(solution)/shard_map/ppermute | solution.py:571
  97.0 18.4 %collective-permute-start.25 = (bf16[128,1024]{1,0:T(8,128)(2,1)S(1)}, bf16[128,1024]{1,0:T(8,128)(2,1)S(1)}, u32[]{:S(2)}, u32[]{:S(2)}) collective-permute-start(bf16[128,1024]{1,0:T(8,128)(2,1)S(1)} %get-tuple-element.133), channel_id=1, source_target_pairs={{0,1},{1,0},{2,3},{3,2},{4,5},{5,4},{6,7},{7,6},{8,9},{9,8},{10,11... | collective-permute-start | bytes 786440 | tf_op jit(solution)/shard_map/ppermute | solution.py:152
  97.5 18.0 %collective-permute-start.22 = (bf16[192,1024]{1,0:T(8,128)(2,1)}, bf16[192,1024]{1,0:T(8,128)(2,1)S(1)}, u32[]{:S(2)}, u32[]{:S(2)}) collective-permute-start(bf16[192,1024]{1,0:T(8,128)(2,1)} %copy-done.27), channel_id=1, source_target_pairs={{2,0},{3,1},{4,6},{5,7},{10,8},{11,9},{12,14},{13,15},{18,16},{19,... | collective-permute-start | bytes 1179656 | tf_op jit(solution)/shard_map/ppermute | solution.py:152
  106.0 2.7 %collective-permute-start.27 = (f32[3,2,2,1024]{3,2,1,0:T(2,128)S(1)}, f32[3,2,2,1024]{3,2,1,0:T(2,128)S(1)}, u32[]{:S(2)}, u32[]{:S(2)}) collective-permute-start(f32[3,2,2,1024]{3,2,1,0:T(2,128)S(1)} %fusion.4), channel_id=1, source_target_pairs={{2,4},{3,5},{4,2},{5,3},{10,12},{11,13},{12,10},{13,11},{18,20},{1... | collective-permute-start | bytes 147464 | tf_op jit(solution)/shard_map/ppermute | solution.py:152
  108.8 6.0 %collective-permute-start.28 = (f32[3,2,2,1024]{3,2,1,0:T(2,128)S(1)}, f32[3,2,2,1024]{3,2,1,0:T(2,128)S(1)}, u32[]{:S(2)}, u32[]{:S(2)}) collective-permute-start(f32[3,2,2,1024]{3,2,1,0:T(2,128)S(1)} %add.49), channel_id=1, source_target_pairs={{2,0},{3,1},{4,6},{5,7},{10,8},{11,9},{12,14},{13,15},{18,16},{19,... | collective-permute-start | bytes 147464 | tf_op jit(solution)/shard_map/ppermute | solution.py:152
  (51 other events, 235.5 us)

commit v6 on v5

--- a/solution.py
+++ b/solution.py
@@ -605,9 +605,8 @@
         ]
     )
     terms = terms + hop(terms, CORE_SWAP)
-    terms = after(terms, outer_handed)
     terms = terms + hop(terms, ACROSS)
-    twiddle_grad = jnp.where(inner, terms, hop(after(terms, late_sums), OUTWARD))
+    sent_terms = hop(after(terms, late_sums), OUTWARD)
 
     mixed_out = jnp.where(inner, own_mixed, after(sent_mixed, sent_late))
     sent_early = after(sent_early, outer_d_acts)
@@ -626,6 +625,8 @@
     )
     grad_square = jnp.where(inner, own_square, wide(sent_square))
     handed = jnp.where(inner, own_handed, outer_handed)
+    sent_terms = after(sent_terms, win_share, wout_share, grad_square, mixed_out, handed)
+    twiddle_grad = jnp.where(inner, terms, sent_terms)
     return mixed_out, handed, win_share, wout_share, grad_square, twiddle_grad
 
 

time: 120 us -> 120 us (level); the launches traced: 118 us -> 119 us
  waiting for transfers between devices: 29.1 us -> 26.2 us
  Pallas kernels: 41.4 us -> 43.1 us
  local copies, waits for them, and re-layouts: 9.38 us -> 10.8 us
    broadcast_in_dim x6 -> x2, other arithmetic: 7.23 us -> 1.7 us  [on_device(): result[None]]
    select_n x0 -> x3, other arithmetic: none -> 3.47 us  [the longest x1 1.89 us: relay_plan(): handed = jnp.where(inner, own_handed, outer_handed)]
    select_n x1 -> x2, other arithmetic: 0.09 us -> 3.24 us  [share_of(): return jnp.where(inner, mine, wide(sent[at * share:(at + 1) * share]))]
    pallas_call x14, Pallas kernels: 32.4 us -> 34 us  [in_place(): kernel_call(kernel, name, work, room, in_specs=[pl.BlockSpec(memory_space...]
    ppermute x27, waiting for transfers between devices: 21.9 us -> 20.4 us  [hop(): return lax.ppermute(value, 'seq', pairs)]
    ppermute x1, waiting for transfers between devices: 7.22 us -> 5.87 us  [relay_plan(): outer_handed = lax.ppermute(outer_d_acts, ('pipe', 'seq'), relay_back(True))]
    unnamed x92 -> x98, local copies, waits for them, and re-layouts: 8.44 us -> 8.28 us
  transfers between devices with their start and end apart: 29 -> 29, of which waited for: 11 -> 11; matrix products, arithmetic and copies ran while one was open for 5% -> 8% of each run, Pallas kernels for 33% -> 34%
where the time goes in v6:
time: 120 us; the launch traced here: 119 us
  Pallas kernels  43.1 us (36%)
  starting transfers between devices  28.6 us (24%)
  waiting for transfers between devices  26.2 us (22%)
  local copies, waits for them, and re-layouts  10.8 us (9%)
  other arithmetic  9.35 us (8%)
  between operations  1.44 us (1%)
    pallas_call x14, Pallas kernels, in_place(): kernel_call(kernel, name, work, room, in_specs=[pl.BlockSpec(memory_space...  34 us
    ppermute x27, starting transfers between devices, hop(): return lax.ppermute(value, 'seq', pairs)  25.8 us
    ppermute x27, waiting for transfers between devices, hop(): return lax.ppermute(value, 'seq', pairs)  20.4 us
    unnamed x98, local copies, waits for them, and re-layouts  8.28 us
    ppermute x1, waiting for transfers between devices, relay_plan(): outer_handed = lax.ppermute(outer_d_acts, ('pipe', 'seq'), relay_back(True))  5.87 us
    pallas_call x1, Pallas kernels, relay_plan(): kernel_call(forward_kernel, 'forward_segments', room=60, grid=(rows // TI...  5.84 us
    select_n x2, other arithmetic, share_of(): return jnp.where(inner, mine, wide(sent[at * share:(at + 1) * share]))  3.24 us
  transfers between devices with their start and end apart: 29, of which 11 were waited for; matrix products, arithmetic and copies ran while one was open for 8% of the time, Pallas kernels for 34%

profile of v6, /device:TPU:4, one launch (start us, length us, event | category | flops | bytes accessed | tf_op | source)
XLA Modules:
  0.0 119.5 jit_solution(9850979107143962942)
XLA Ops:
  0.6 1.9 %pack.1.pack_ref.refs_0_ = bf16[320,1024]{1,0:T(8,128)(2,1)} custom-call(bf16[256,1024]{1,0:T(8,128)(2,1)} %bitcast.41, bf16[256,256]{1,0:T(8,128)(2,1)} %bitcast.46), custom_call_target="tpu_custom_call" | custom-call | flops 1 | bytes 1 | tf_op jit(solution)/shard_map/pack/pallas_call | solution.py:417
  2.6 3.5 %collective-permute-start = (bf16[320,1024]{1,0:T(8,128)(2,1)}, bf16[320,1024]{1,0:T(8,128)(2,1)S(1)}, u32[]{:S(2)}, u32[]{:S(2)}) collective-permute-start(bf16[320,1024]{1,0:T(8,128)(2,1)} %pack.1.pack_ref.refs_0_), channel_id=1, source_target_pairs={{0,2},{1,3},{6,4},{7,5},{8,10},{9,11},{14,12},{15,13},{16,18},{17,... | collective-permute-start | bytes 1966088 | tf_op jit(solution)/shard_map/ppermute | solution.py:152
  8.6 2.2 %copy-done = bf16[1,1024,2048]{2,1,0:T(8,128)(2,1)S(1)} copy-done((bf16[1,1024,2048]{2,1,0:T(8,128)(2,1)S(1)}, bf16[1,1024,2048]{2,1,0:T(8,128)(2,1)}, u32[]{:S(2)}) %copy-start) | copy-done | bytes 4194328
  11.8 3.3 %block_0.1 = (bf16[256,512]{1,0:T(8,128)(2,1)}, bf16[256,512]{1,0:T(8,128)(2,1)}, bf16[256,1024]{1,0:T(8,128)(2,1)}, bf16[256,1024]{1,0:T(8,128)(2,1)}, bf16[256,1024]{1,0:T(8,128)(2,1)}) custom-call(s32[4]{0:T(128)S(1)} %pad_add_fusion.starts_ref, bf16[320,1024]{1,0:T(8,128)(2,1)S(1)} %copy-done.5, bf16[1024,2048]{1,0:T(8,128)(2,1)S(1)} %bitcast.32), custom_call_target="tpu_custom_call" | custom-call | flops 1073741824 | bytes 1 | tf_op jit(solution)/shard_map/block_0/pallas_call | solution.py:417
  16.8 1.8 %d_hidden.3.refs_0_ = bf16[256,1024]{1,0:T(8,128)(2,1)S(1)} custom-call(bf16[1024,1024]{1,0:T(8,128)(2,1)S(1)} %bitcast.37, bf16[256,1024]{1,0:T(8,128)(2,1)} %bitcast.11.refs_0_.refs_6_), custom_call_target="tpu_custom_call" | custom-call | flops 536870912 | bytes 1 | tf_op jit(solution)/shard_map/d_hidden/pallas_call | solution.py:417
  18.6 1.7 %collective-permute-done.pack_ref.refs_1_ = bf16[320,1024]{1,0:T(8,128)(2,1)S(1)} collective-permute-done((bf16[320,1024]{1,0:T(8,128)(2,1)}, bf16[320,1024]{1,0:T(8,128)(2,1)S(1)}, u32[]{:S(2)}, u32[]{:S(2)}) %collective-permute-start) | collective-permute-done | bytes 655392 | tf_op jit(solution)/shard_map/ppermute | solution.py:152
  21.0 7.8 %collective-permute-start.10 = (bf16[256,1024]{1,0:T(8,128)(2,1)}, bf16[256,1024]{1,0:T(8,128)(2,1)}, u32[]{:S(2)}, u32[]{:S(2)}) collective-permute-start(bf16[256,1024]{1,0:T(8,128)(2,1)} %bitcast.11.refs_0_.refs_6_), channel_id=1, source_target_pairs={{0,2},{1,3},{6,4},{7,5},{8,10},{9,11},{14,12},{15,13},{16,18},{17,... | collective-permute-start | bytes 1572872 | tf_op jit(solution)/shard_map/ppermute | solution.py:152
  28.9 3.4 %block_1.1 = (bf16[256,512]{1,0:T(8,128)(2,1)}, bf16[256,512]{1,0:T(8,128)(2,1)}, bf16[256,1024]{1,0:T(8,128)(2,1)}, bf16[256,1024]{1,0:T(8,128)(2,1)}, bf16[256,1024]{1,0:T(8,128)(2,1)}) custom-call(s32[4]{0:T(128)S(1)} %pad_add_fusion.starts_ref, bf16[320,1024]{1,0:T(8,128)(2,1)S(1)} %collective-permute-done.pack_ref.refs_1_, bf16[1024,2048]{1,0:T(8,128)(2,1)S(1)} %bitcast.33), custom_call_target="tpu_custom_call" | custom-call | flops 1 | bytes 1 | tf_op jit(solution)/shard_map/block_1/pallas_call | solution.py:417
  32.8 3.1 %block_3.1 = (bf16[256,512]{1,0:T(8,128)(2,1)}, bf16[256,512]{1,0:T(8,128)(2,1)}, bf16[256,1024]{1,0:T(8,128)(2,1)}, bf16[256,1024]{1,0:T(8,128)(2,1)}) custom-call(s32[4]{0:T(128)S(1)} %pad_add_fusion.starts_ref, bf16[320,1024]{1,0:T(8,128)(2,1)S(1)} %collective-permute-done.1.pack_ref, bf16[1024,2048]{1,0:T(8,128)(2,1)S(1)} %bitcast.34), custom_call_target="tpu_custom_call" | custom-call | flops 1 | bytes 1 | tf_op jit(solution)/shard_map/block_3/pallas_call | solution.py:417
  37.4 3.2 %block_2.1 = (bf16[256,512]{1,0:T(8,128)(2,1)}, bf16[256,512]{1,0:T(8,128)(2,1)}, bf16[256,1024]{1,0:T(8,128)(2,1)}, bf16[256,512]{1,0:T(8,128)(2,1)}, bf16[256,512]{1,0:T(8,128)(2,1)}) custom-call(s32[4]{0:T(128)S(1)} %pad_add_fusion.starts_ref, bf16[320,1024]{1,0:T(8,128)(2,1)S(1)} %collective-permute-done.2.pack_ref, bf16[1024,2048]{1,0:T(8,128)(2,1)S(1)} %bitcast.35), custom_call_target="tpu_custom_call" | custom-call | flops 1 | bytes 1 | tf_op jit(solution)/shard_map/block_2/pallas_call | solution.py:417
  45.1 5.8 %forward_segments.1 = (bf16[2,256,1024]{2,1,0:T(8,128)(2,1)}, bf16[4,256,1024]{2,1,0:T(8,128)(2,1)}, bf16[2,256,1024]{2,1,0:T(8,128)(2,1)}, bf16[4,256,512]{2,1,0:T(8,128)(2,1)}) custom-call(s32[4]{0:T(128)} %copy-done.35, bf16[16,1024]{1,0:T(8,128)(2,1)} %maximum_maximum_fusion.coef_ref, bf16[256,1024]{1,0:T(8,128)(2,1)} %get-tuple-element.74.refs_0_.refs_8_, ...), custom_call_target="tpu_custom_call" | custom-call | flops 1 | bytes 1 | tf_op jit(solution)/shard_map/forward_segments/pallas_call | solution.py:493
  54.9 2.6 %d_hidden.4 = (bf16[256,1024]{1,0:T(8,128)(2,1)S(1)}, bf16[256,1024]{1,0:T(8,128)(2,1)S(1)}) custom-call(bf16[1024,1024]{1,0:T(8,128)(2,1)S(1)} %bitcast.39, bf16[256,1024]{1,0:T(8,128)(2,1)} %collective-permute-done.10.refs_0_.refs_7_, bf16[256,1024]{1,0:T(8,128)(2,1)} %collective-permute-done.8.refs_1_.refs_9_), custom_call_target="tpu_custom_call" | custom-call | flops 1 | bytes 1 | tf_op jit(solution)/shard_map/d_hidden/pallas_call | solution.py:417
  57.6 1.9 %d_hidden.5.refs_2_ = bf16[256,1024]{1,0:T(8,128)(2,1)S(1)} custom-call(bf16[1024,1024]{1,0:T(8,128)(2,1)S(1)} %bitcast.40, bf16[256,1024]{1,0:T(8,128)(2,1)} %collective-permute-done.11.refs_0_.refs_8_), custom_call_target="tpu_custom_call" | custom-call | flops 1 | bytes 1 | tf_op jit(solution)/shard_map/d_hidden/pallas_call | solution.py:417
  59.7 2.2 %backward_segments.1 = (bf16[4,256,1024]{2,1,0:T(8,128)(2,1)S(1)}, bf16[256,1024]{1,0:T(8,128)(2,1)S(1)}, bf16[256,1024]{1,0:T(8,128)(2,1)S(1)}, bf16[256,1024]{...) custom-call(bf16[16,1024]{1,0:T(8,128)(2,1)S(1)} %copy-done.22, ...), custom_call_target="tpu_custom_call" | custom-call | flops 1 | bytes 1 | tf_op jit(solution)/shard_map/backward_segments/pallas_call | solution.py:530
  63.6 3.9 %early_grads.1 = (bf16[128,1024]{1,0:T(8,128)(2,1)S(1)}, bf16[128,1024]{1,0:T(8,128)(2,1)S(1)}, bf16[128,1024]{1,0:T(8,128)(2,1)S(1)}, bf16[128,1024]{1,0:T(8,128)(2,1)S(1)}, f32[512,1024]{1,0:T(8,128)S(1)}) custom-call(bf16[256,512]{1,0:T(8,128)(2,1)S(1)} %copy-done.31, bf16[256,512]{1,0:T(8,128)(2,1)S(1)} %copy-done.32, bf16[256,512]{1,0:T(8,128)(2,1)S(1)} %copy-done.34, ...), custom_call_target="tpu_custom_call" | custom-call | flops 1 | bytes 1 | tf_op jit(solution)/shard_map/early_grads/pallas_call | solution.py:417
  67.5 6.5 %collective-permute-done.9 = bf16[256,1024]{1,0:T(8,128)(2,1)S(1)} collective-permute-done((bf16[256,1024]{1,0:T(8,128)(2,1)S(1)}, bf16[256,1024]{1,0:T(8,128)(2,1)S(1)}, u32[]{:S(2)}, u32[]{:S(2)}) %collective-permute-start.9) | collective-permute-done | bytes 524320 | tf_op jit(solution)/shard_map/ppermute | solution.py:152
  80.3 2.6 %own_grads.1 = (bf16[256,1024]{1,0:T(8,128)(2,1)S(1)}, bf16[256,1024]{1,0:T(8,128)(2,1)S(1)}) custom-call(bf16[4,256,1024]{2,1,0:T(8,128)(2,1)S(1)} %get-tuple-element.117.d_seg0_ref, bf16[4,256,1024]{2,1,0:T(8,128)(2,1)S(1)} %get-tuple-element.108.refs_4_.d_gate_ref, bf16[1024,2048]{1,0:T(8,128)(2,1)S(1)} %bitcast.36, bf16[320,1024]{1,0:T(8,128)(2,1)S(1)} %copy-done.6, ...), custom_call_target="tpu_custom_call" | custom-call | flops 1 | bytes 1 | tf_op jit(solution)/shard_map/own_grads/pallas_call | solution.py:417
  83.1 2.2 %value_grads.1 = (bf16[128,1024]{1,0:T(8,128)(2,1)S(1)}, bf16[128,1024]{1,0:T(8,128)(2,1)}, f32[128,1024]{1,0:T(8,128)}, f32[128,1024]{1,0:T(8,128)S(1)}, f32[256,256]{1,0:T(8,128)}, /*index=5*/f32[256,256]{1,0:T(8,128)S(1)}) custom-call(bf16[4,256,1024]{2,1,0:T(8,128)(2,1)S(1)} %get-tuple-element.117.d_seg0_ref, bf16[256,512]{1,0:T(8,128)(2,1)S(1)} %copy-done.27, ...), custom_call_target="tpu_custom_call" | custom-call | flops 1 | bytes 1 | tf_op jit(solution)/shard_map/value_grads/pallas_call | solution.py:417
  90.0 4.8 %collective-permute-done.20 = bf16[256,1024]{1,0:T(8,128)(2,1)} collective-permute-done((bf16[256,1024]{1,0:T(8,128)(2,1)}, bf16[256,1024]{1,0:T(8,128)(2,1)}, u32[]{:S(2)}, u32[]{:S(2)}) %collective-permute-start.20) | collective-permute-done | bytes 524320 | tf_op jit(solution)/shard_map/ppermute | solution.py:152
  94.8 1.8 %late_sums.1 = bf16[192,1024]{1,0:T(8,128)(2,1)} custom-call(f32[128,1024]{1,0:T(8,128)S(1)} %get-tuple-element.127.there_ref, bf16[128,1024]{1,0:T(8,128)(2,1)} %collective-permute-done.21.got_ref, f32[256,256]{1,0:T(8,128)S(1)} %get-tuple-element.129.square_ref), custom_call_target="tpu_custom_call" | custom-call | flops 1 | bytes 1 | tf_op jit(solution)/shard_map/late_sums/pallas_call | solution.py:417
  98.1 2.1 %convert_select_fusion = (f32[128,1024]{1,0:T(8,128)}, f32[128,1024]{1,0:T(8,128)S(1)}) fusion(bf16[128,1024]{1,0:T(8,128)(2,1)S(1)} %collective-permute-done.18.refs_2_, f32[512,1024]{1,0:T(8,128)S(1)} %get-tuple-element.111.kept_ref, bf16[256,1024]{1,0:T(8,128)(2,1)} %collective-permute-done.20, pred[]{:T(512)S(6)} %or.3, ...), kind=kLoop, calls=%fused_computation.1 | loop fusion | flops 1048576 | bytes 3145729 | tf_op jit(solution)/shard_map/jit(_where)/select_n | solution.py:616
  101.1 5.9 %collective-permute-done.24 = bf16[256,1024]{1,0:T(8,128)(2,1)} collective-permute-done((bf16[256,1024]{1,0:T(8,128)(2,1)}, bf16[256,1024]{1,0:T(8,128)(2,1)}, u32[]{:S(2)}, u32[]{:S(2)}) %collective-permute-start.24) | collective-permute-done | bytes 524320 | tf_op jit(solution)/shard_map/ppermute | solution.py:570
  107.0 1.9 %broadcast_select_fusion = bf16[256,1024]{1,0:T(8,128)(2,1)} fusion(bf16[256,1024]{1,0:T(8,128)(2,1)} %collective-permute-done.23, bf16[256,1024]{1,0:T(8,128)(2,1)} %collective-permute-done.24, pred[]{:T(512)S(6)} %or.3), kind=kLoop, calls=%fused_computation.4 | loop fusion | flops 262144 | bytes 1572865 | tf_op jit(solution)/shard_map/jit(_where)/select_n | solution.py:627
  110.2 4.0 %collective-permute-done.22 = bf16[192,1024]{1,0:T(8,128)(2,1)} collective-permute-done((bf16[192,1024]{1,0:T(8,128)(2,1)}, bf16[192,1024]{1,0:T(8,128)(2,1)}, u32[]{:S(2)}, u32[]{:S(2)}) %collective-permute-start.22) | collective-permute-done | bytes 393248 | tf_op jit(solution)/shard_map/ppermute | solution.py:152
  (177 shorter events, 37.6 us)
Async XLA Ops:
  2.6 17.8 %collective-permute-start = (bf16[320,1024]{1,0:T(8,128)(2,1)}, bf16[320,1024]{1,0:T(8,128)(2,1)S(1)}, u32[]{:S(2)}, u32[]{:S(2)}) collective-permute-start(bf16[320,1024]{1,0:T(8,128)(2,1)} %pack.1.pack_ref.refs_0_), channel_id=1, source_target_pairs={{0,2},{1,3},{6,4},{7,5},{8,10},{9,11},{14,12},{15,13},{16,18},{17,... | collective-permute-start | bytes 1966088 | tf_op jit(solution)/shard_map/ppermute | solution.py:152
  7.8 25.0 %collective-permute-start.1 = (bf16[320,1024]{1,0:T(8,128)(2,1)}, bf16[320,1024]{1,0:T(8,128)(2,1)S(1)}, u32[]{:S(2)}, u32[]{:S(2)}) collective-permute-start(bf16[320,1024]{1,0:T(8,128)(2,1)} %pack.1.pack_ref.refs_0_), channel_id=1, source_target_pairs={{2,4},{3,5},{4,2},{5,3},{10,12},{11,13},{12,10},{13,11},{18,20},{1... | collective-permute-start | bytes 1966088 | tf_op jit(solution)/shard_map/ppermute | solution.py:152
  20.3 15.6 %collective-permute-start.2 = (bf16[320,1024]{1,0:T(8,128)(2,1)S(1)}, bf16[320,1024]{1,0:T(8,128)(2,1)S(1)}, u32[]{:S(2)}, u32[]{:S(2)}) collective-permute-start(bf16[320,1024]{1,0:T(8,128)(2,1)S(1)} %collective-permute-done.pack_ref.refs_1_), channel_id=1, source_target_pairs={{2,4},{3,5},{4,2},{5,3},{10,12},{11,13},{12,10},{13,11},{18,20},{1... | collective-permute-start | bytes 1966088 | tf_op jit(solution)/shard_map/ppermute | solution.py:152
  21.0 19.6 %collective-permute-start.10 = (bf16[256,1024]{1,0:T(8,128)(2,1)}, bf16[256,1024]{1,0:T(8,128)(2,1)}, u32[]{:S(2)}, u32[]{:S(2)}) collective-permute-start(bf16[256,1024]{1,0:T(8,128)(2,1)} %bitcast.11.refs_0_.refs_6_), channel_id=1, source_target_pairs={{0,2},{1,3},{6,4},{7,5},{8,10},{9,11},{14,12},{15,13},{16,18},{17,... | collective-permute-start | bytes 1572872 | tf_op jit(solution)/shard_map/ppermute | solution.py:152
  28.9 13.2 %collective-permute-start.3 = (bf16[256,1024]{1,0:T(8,128)(2,1)S(1)}, bf16[256,1024]{1,0:T(8,128)(2,1)S(1)}, u32[]{:S(2)}, u32[]{:S(2)}) collective-permute-start(bf16[256,1024]{1,0:T(8,128)(2,1)S(1)} %copy-done.12), channel_id=1, source_target_pairs={{0,1},{1,0},{2,3},{3,2},{4,5},{5,4},{6,7},{7,6},{8,9},{9,8},{10,11... | collective-permute-start | bytes 1572872 | tf_op jit(solution)/shard_map/ppermute | solution.py:152
  32.3 10.4 %collective-permute-start.4 = (bf16[256,1024]{1,0:T(8,128)(2,1)}, bf16[256,1024]{1,0:T(8,128)(2,1)S(1)}, u32[]{:S(2)}, u32[]{:S(2)}) collective-permute-start(bf16[256,1024]{1,0:T(8,128)(2,1)} %get-tuple-element.76.refs_1_.refs_9_), channel_id=1, source_target_pairs={{0,1},{1,0},{2,3},{3,2},{4,5},{5,4},{6,7},{7,6},{8,9},{9,8},{10,11... | collective-permute-start | bytes 1572872 | tf_op jit(solution)/shard_map/ppermute | solution.py:152
  35.9 6.8 %collective-permute-start.5 = (bf16[256,1024]{1,0:T(8,128)(2,1)}, bf16[256,1024]{1,0:T(8,128)(2,1)S(1)}, u32[]{:S(2)}, u32[]{:S(2)}) collective-permute-start(bf16[256,1024]{1,0:T(8,128)(2,1)} %get-tuple-element.80.refs_2_), channel_id=1, source_target_pairs={{0,1},{1,0},{2,3},{3,2},{4,5},{5,4},{6,7},{7,6},{8,9},{9,8},{10,11... | collective-permute-start | bytes 1572872 | tf_op jit(solution)/shard_map/ppermute | solution.py:152
  35.9 15.0 %collective-permute-start.8 = (bf16[256,1024]{1,0:T(8,128)(2,1)}, bf16[256,1024]{1,0:T(8,128)(2,1)}, u32[]{:S(2)}, u32[]{:S(2)}) collective-permute-start(bf16[256,1024]{1,0:T(8,128)(2,1)} %bitcast.11.refs_0_.refs_6_), channel_id=1, source_target_pairs={{2,4},{3,5},{4,2},{5,3},{10,12},{11,13},{12,10},{13,11},{18,20},{1... | collective-permute-start | bytes 1572872 | tf_op jit(solution)/shard_map/ppermute | solution.py:152
  40.6 17.0 %collective-permute-start.11 = (bf16[256,1024]{1,0:T(8,128)(2,1)}, bf16[256,1024]{1,0:T(8,128)(2,1)}, u32[]{:S(2)}, u32[]{:S(2)}) collective-permute-start(bf16[256,1024]{1,0:T(8,128)(2,1)} %collective-permute-done.10.refs_0_.refs_7_), channel_id=1, source_target_pairs={{2,4},{3,5},{4,2},{5,3},{10,12},{11,13},{12,10},{13,11},{18,20},{1... | collective-permute-start | bytes 1572872 | tf_op jit(solution)/shard_map/ppermute | solution.py:152
  53.4 20.6 %collective-permute-start.9 = (bf16[256,1024]{1,0:T(8,128)(2,1)S(1)}, bf16[256,1024]{1,0:T(8,128)(2,1)S(1)}, u32[]{:S(2)}, u32[]{:S(2)}) collective-permute-start(bf16[256,1024]{1,0:T(8,128)(2,1)S(1)} %get-tuple-element.95), channel_id=1, source_target_pairs={{2,0},{3,1},{4,6},{5,7},{10,8},{11,9},{12,14},{13,15},{18,16},{19,... | collective-permute-start | bytes 1572872 | tf_op jit(solution)/shard_map/ppermute | solution.py:152
  62.6 11.5 %collective-permute-start.12 = (bf16[256,1024]{1,0:T(8,128)(2,1)S(1)}, bf16[256,1024]{1,0:T(8,128)(2,1)S(1)}, u32[]{:S(2)}, u32[]{:S(2)}) collective-permute-start(bf16[256,1024]{1,0:T(8,128)(2,1)S(1)} %get-tuple-element.104.refs_0_), channel_id=1, source_target_pairs={{0,1},{1,0},{2,3},{3,2},{4,5},{5,4},{6,7},{7,6},{8,9},{9,8},{10,11... | collective-permute-start | bytes 1572872 | tf_op jit(solution)/shard_map/ppermute | solution.py:152
  62.9 11.6 %collective-permute-start.13 = (bf16[256,1024]{1,0:T(8,128)(2,1)S(1)}, bf16[256,1024]{1,0:T(8,128)(2,1)S(1)}, u32[]{:S(2)}, u32[]{:S(2)}) collective-permute-start(bf16[256,1024]{1,0:T(8,128)(2,1)S(1)} %get-tuple-element.105.refs_1_), channel_id=1, source_target_pairs={{0,1},{1,0},{2,3},{3,2},{4,5},{5,4},{6,7},{7,6},{8,9},{9,8},{10,11... | collective-permute-start | bytes 1572872 | tf_op jit(solution)/shard_map/ppermute | solution.py:152
  63.1 11.6 %collective-permute-start.14 = (bf16[256,1024]{1,0:T(8,128)(2,1)S(1)}, bf16[256,1024]{1,0:T(8,128)(2,1)S(1)}, u32[]{:S(2)}, u32[]{:S(2)}) collective-permute-start(bf16[256,1024]{1,0:T(8,128)(2,1)S(1)} %get-tuple-element.106.refs_2_), channel_id=1, source_target_pairs={{0,1},{1,0},{2,3},{3,2},{4,5},{5,4},{6,7},{7,6},{8,9},{9,8},{10,11... | collective-permute-start | bytes 1572872 | tf_op jit(solution)/shard_map/ppermute | solution.py:152
  63.4 11.6 %collective-permute-start.15 = (bf16[256,1024]{1,0:T(8,128)(2,1)S(1)}, bf16[256,1024]{1,0:T(8,128)(2,1)S(1)}, u32[]{:S(2)}, u32[]{:S(2)}) collective-permute-start(bf16[256,1024]{1,0:T(8,128)(2,1)S(1)} %get-tuple-element.107.refs_3_), channel_id=1, source_target_pairs={{0,1},{1,0},{2,3},{3,2},{4,5},{5,4},{6,7},{7,6},{8,9},{9,8},{10,11... | collective-permute-start | bytes 1572872 | tf_op jit(solution)/shard_map/ppermute | solution.py:152
  74.6 2.1 %collective-permute-start.19 = (bf16[128,1024]{1,0:T(8,128)(2,1)S(1)}, bf16[128,1024]{1,0:T(8,128)(2,1)S(1)}, u32[]{:S(2)}, u32[]{:S(2)}) collective-permute-start(bf16[128,1024]{1,0:T(8,128)(2,1)S(1)} %get-tuple-element.115), channel_id=1, source_target_pairs={{0,1},{1,0},{2,3},{3,2},{4,5},{5,4},{6,7},{7,6},{8,9},{9,8},{10,11... | collective-permute-start | bytes 786440 | tf_op jit(solution)/shard_map/ppermute | solution.py:152
  77.6 17.2 %collective-permute-start.20 = (bf16[256,1024]{1,0:T(8,128)(2,1)}, bf16[256,1024]{1,0:T(8,128)(2,1)}, u32[]{:S(2)}, u32[]{:S(2)}) collective-permute-start(bf16[256,1024]{1,0:T(8,128)(2,1)} %early_sums.1), channel_id=1, source_target_pairs={{2,0},{3,1},{4,6},{5,7},{10,8},{11,9},{12,14},{13,15},{18,16},{19,... | collective-permute-start | bytes 1572872 | tf_op jit(solution)/shard_map/ppermute | solution.py:152
  86.0 8.8 %collective-permute-start.21 = (bf16[128,1024]{1,0:T(8,128)(2,1)}, bf16[128,1024]{1,0:T(8,128)(2,1)}, u32[]{:S(2)}, u32[]{:S(2)}) collective-permute-start(bf16[128,1024]{1,0:T(8,128)(2,1)} %get-tuple-element.128), channel_id=1, source_target_pairs={{0,1},{1,0},{2,3},{3,2},{4,5},{5,4},{6,7},{7,6},{8,9},{9,8},{10,11... | collective-permute-start | bytes 786440 | tf_op jit(solution)/shard_map/ppermute | solution.py:152
  86.1 20.8 %collective-permute-start.24 = (bf16[256,1024]{1,0:T(8,128)(2,1)}, bf16[256,1024]{1,0:T(8,128)(2,1)}, u32[]{:S(2)}, u32[]{:S(2)}) collective-permute-start(bf16[256,1024]{1,0:T(8,128)(2,1)} %copy-done.39), channel_id=1, source_target_pairs={{10,0},{11,1},{12,6},{13,7},{18,8},{19,9},{20,14},{21,15},{26,16},... | collective-permute-start | bytes 1572872 | tf_op jit(solution)/shard_map/ppermute | solution.py:570
  88.2 29.1 %collective-permute-start.25 = (bf16[128,1024]{1,0:T(8,128)(2,1)}, bf16[128,1024]{1,0:T(8,128)(2,1)}, u32[]{:S(2)}, u32[]{:S(2)}) collective-permute-start(bf16[128,1024]{1,0:T(8,128)(2,1)} %copy-done.41), channel_id=1, source_target_pairs={{0,1},{1,0},{2,3},{3,2},{4,5},{5,4},{6,7},{7,6},{8,9},{9,8},{10,11... | collective-permute-start | bytes 786440 | tf_op jit(solution)/shard_map/ppermute | solution.py:152
  88.6 12.5 %collective-permute-start.23 = (bf16[256,1024]{1,0:T(8,128)(2,1)}, bf16[256,1024]{1,0:T(8,128)(2,1)}, u32[]{:S(2)}, u32[]{:S(2)}) collective-permute-start(bf16[256,1024]{1,0:T(8,128)(2,1)} %copy-done.40), channel_id=1, source_target_pairs={{10,2},{11,3},{12,4},{13,5},{18,10},{19,11},{20,12},{21,13},{26,18... | collective-permute-start | bytes 1572872 | tf_op jit(solution)/shard_map/ppermute | solution.py:571
  96.6 17.6 %collective-permute-start.22 = (bf16[192,1024]{1,0:T(8,128)(2,1)}, bf16[192,1024]{1,0:T(8,128)(2,1)}, u32[]{:S(2)}, u32[]{:S(2)}) collective-permute-start(bf16[192,1024]{1,0:T(8,128)(2,1)} %late_sums.1), channel_id=1, source_target_pairs={{2,0},{3,1},{4,6},{5,7},{10,8},{11,9},{12,14},{13,15},{18,16},{19,... | collective-permute-start | bytes 1179656 | tf_op jit(solution)/shard_map/ppermute | solution.py:152
  98.0 2.2 %collective-permute-start.26 = (f32[3,2,2,1024]{3,2,1,0:T(2,128)S(1)}, f32[3,2,2,1024]{3,2,1,0:T(2,128)S(1)}, u32[]{:S(2)}, u32[]{:S(2)}) collective-permute-start(f32[3,2,2,1024]{3,2,1,0:T(2,128)S(1)} %pad_maximum_fusion.1), channel_id=1, source_target_pairs={{0,1},{1,0},{2,3},{3,2},{4,5},{5,4},{6,7},{7,6},{8,9},{9,8},{10,11... | collective-permute-start | bytes 147464 | tf_op jit(solution)/shard_map/ppermute | solution.py:152
  100.3 8.6 %collective-permute-start.27 = (f32[3,2,2,1024]{3,2,1,0:T(2,128)S(1)}, f32[3,2,2,1024]{3,2,1,0:T(2,128)S(1)}, u32[]{:S(2)}, u32[]{:S(2)}) collective-permute-start(f32[3,2,2,1024]{3,2,1,0:T(2,128)S(1)} %fusion.4), channel_id=1, source_target_pairs={{2,4},{3,5},{4,2},{5,3},{10,12},{11,13},{12,10},{13,11},{18,20},{1... | collective-permute-start | bytes 147464 | tf_op jit(solution)/shard_map/ppermute | solution.py:152
  108.9 7.7 %collective-permute-start.28 = (f32[3,2,2,1024]{3,2,1,0:T(2,128)S(1)}, f32[3,2,2,1024]{3,2,1,0:T(2,128)S(1)}, u32[]{:S(2)}, u32[]{:S(2)}) collective-permute-start(f32[3,2,2,1024]{3,2,1,0:T(2,128)S(1)} %fusion.7), channel_id=1, source_target_pairs={{2,0},{3,1},{4,6},{5,7},{10,8},{11,9},{12,14},{13,15},{18,16},{19,... | collective-permute-start | bytes 147464 | tf_op jit(solution)/shard_map/ppermute | solution.py:152
  (54 other events, 290.5 us)
